TPU v7x, 32 devices: a whole 2x2x4 slice. The times are simulated.
32 devices in a mesh: fsdp: 16 (over z, y, core), tp: 2 (over x).
Axes of the slice: x: 2, y: 2, z: 4, core: 2. Of those that a mesh axis runs over, the one named last changes fastest.
Arguments:
- layer_in: bfloat16 [2, 8192, 2048], P(None, 'fsdp'), may hold values from -6 to 6
- out_grad: bfloat16 [2, 8192, 2048], P(None, 'fsdp'), may hold values from -6 to 6
- parents: int32 [2, 13], replicated, may hold values from 0 to 4, as said below
- seg_len: int32 [2, 13], replicated, may hold values from 1 to 1024, as said below
- attn_gain: bfloat16 [2048], P('fsdp'), may hold values from 0.5 to 1.5
- w_query: bfloat16 [2048, 2048], P('fsdp', 'tp'), may hold values from -0.25 to 0.25
- key_weight: bfloat16 [2048, 512], P('fsdp', 'tp'), may hold values from -0.125 to 0.125
- value_weight: bfloat16 [2048, 512], P('fsdp', 'tp'), may hold values from -0.125 to 0.125
- w_out: bfloat16 [2048, 2048], P('tp', 'fsdp'), may hold values from -0.75 to 0.75
- ffn_gain: bfloat16 [2048], P('fsdp'), may hold values from 0.5 to 1.5
- w_gate: bfloat16 [2048, 8192], P('fsdp', 'tp'), may hold values from -0.125 to 0.125
- w_up: bfloat16 [2048, 8192], P('fsdp', 'tp'), may hold values from -0.125 to 0.125
- w_down: bfloat16 [8192, 2048], P('tp', 'fsdp'), may hold values from -0.0625 to 0.0625
Outputs:
- output: bfloat16 [2, 8192, 2048], P(None, 'fsdp')
- input_grad: float32 [2, 8192, 2048], P(None, 'fsdp')
- attn_gain_grad: float32 [2048], P('fsdp')
- query_grad: float32 [2048, 2048], P('fsdp', 'tp')
- key_grad: float32 [2048, 512], P('fsdp', 'tp')
- value_grad: float32 [2048, 512], P('fsdp', 'tp')
- out_proj_grad: float32 [2048, 2048], P('tp', 'fsdp')
- ffn_gain_grad: float32 [2048], P('fsdp')
- gate_grad: float32 [2048, 8192], P('fsdp', 'tp')
- up_grad: float32 [2048, 8192], P('fsdp', 'tp')
- down_grad: float32 [8192, 2048], P('tp', 'fsdp')
Inputs may be any that keep to these rules, and one draw needn't show every extreme that they name: Segment 0 is the trunk, its own parent; segments 1 to 4 are branches whose parent is 0; the 8 segments after them are leaves whose parents are branches, each branch the parent of one leaf or more. `seg_len`: the lengths of a tree's segments are positive and sum to 8192; the trunk's is the largest.
All inputs are finite; a program needn't handle non-finite values.
Results may differ from a plain program's by a relative error of at most 0.02.
Values may be sent and summed in bfloat16 or wider, within the bound.
A program may use at most 320 MiB of HBM per device.

v0:
```python
import math

import jax
import jax.numpy as jnp
from jax import lax
from jax.sharding import PartitionSpec as P

QUERY_HEADS = 32
KEY_VALUE_HEADS = 8
HEAD_SIZE = 64
LEVELS = 3


EPS = 1e-05
THETA = 500000.0
NEG = -1e30


def normalize(rows_in):
    return rows_in * lax.rsqrt(jnp.mean(rows_in * rows_in, axis=-1, keepdims=True) + EPS)


def norm_back(grad_normed, normed, rows_in):
    row_scale = lax.rsqrt(jnp.mean(rows_in * rows_in, axis=-1, keepdims=True) + EPS)
    return row_scale * (
        grad_normed - normed * jnp.mean(grad_normed * normed, axis=-1, keepdims=True)
    )


def rope_tables(position, head_dim):
    half_dim = head_dim // 2
    index_row = jnp.arange(half_dim, dtype=jnp.float32)
    inverse = THETA ** (-2.0 * index_row / head_dim)
    wavelen = 2.0 * math.pi / inverse
    smooth = jnp.clip((8192.0 / wavelen - 1.0) / 3.0, 0.0, 1.0)
    inverse = (1.0 - smooth) * inverse / 32.0 + smooth * inverse
    angles = position.astype(jnp.float32)[:, None] * inverse[None, :]
    return (jnp.cos(angles), jnp.sin(angles))


def rotary_apply(values_in, cosine_table, sine_table):
    half_dim = values_in.shape[-1] // 2
    first_half = values_in[..., :half_dim]
    second_half = values_in[..., half_dim:]
    cos_rows = cosine_table[:, None, :]
    sin_rows = sine_table[:, None, :]
    return jnp.concatenate(
        [
            first_half * cos_rows - second_half * sin_rows,
            second_half * cos_rows + first_half * sin_rows,
        ],
        axis=-1,
    )


def rotate_back(grad_in, cosine_table, sine_table):
    half_dim = grad_in.shape[-1] // 2
    first_half = grad_in[..., :half_dim]
    second_half = grad_in[..., half_dim:]
    cos_rows = cosine_table[:, None, :]
    sin_rows = sine_table[:, None, :]
    return jnp.concatenate(
        [
            first_half * cos_rows + second_half * sin_rows,
            second_half * cos_rows - first_half * sin_rows,
        ],
        axis=-1,
    )


def tree_tables(parents_row, lengths):
    seg_count = parents_row.shape[0]
    labels = jnp.arange(seg_count, dtype=jnp.int32)
    ends_at = jnp.cumsum(lengths)
    starts_at = ends_at - lengths
    reaches = labels[:, None] == labels[None, :]
    climber = labels
    for level_index in range(LEVELS - 1):
        climber = jnp.sum(
            jnp.where(climber[:, None] == labels[None, :], parents_row[None, :], 0), axis=1
        )
        reaches = reaches | (climber[:, None] == labels[None, :])
    before = jnp.sum(
        jnp.where(reaches & (labels[:, None] != labels[None, :]), lengths[None, :], 0), axis=1
    )
    return (reaches, starts_at, ends_at, before)


def place_tokens(tokens, starts_at, ends_at, before):
    labels = jnp.arange(starts_at.shape[0], dtype=jnp.int32)
    segment = jnp.sum((tokens[:, None] >= ends_at[None, :]).astype(jnp.int32), axis=1)
    member = segment[:, None] == labels[None, :]
    position = (
        tokens
        - jnp.sum(jnp.where(member, starts_at[None, :], 0), axis=1)
        + jnp.sum(jnp.where(member, before[None, :], 0), axis=1)
    )
    return (segment, position)


def key_mask(allowed, own_tokens, ends_at, key_tokens):
    labels = jnp.arange(ends_at.shape[0], dtype=jnp.int32)
    key_seg = jnp.sum((key_tokens[:, None] >= ends_at[None, :]).astype(jnp.int32), axis=1)
    key_hot = (key_seg[:, None] == labels[None, :]).astype(jnp.float32)
    linked = jnp.dot(allowed, key_hot.T) > 0.5
    return linked & (key_tokens[None, :] <= own_tokens[:, None])


def shards(
    layer_in,
    out_grad,
    parents,
    seg_len,
    attn_gain,
    w_query,
    key_weight,
    value_weight,
    w_out,
    ffn_gain,
    w_gate,
    w_up,
    w_down,
):
    micro_count, row_count, model_width = layer_in.shape
    fsdp_count = lax.axis_size("fsdp")
    tensor_parallel_count = lax.axis_size("tp")
    tree_row_block = row_count * fsdp_count
    head_count = QUERY_HEADS // tensor_parallel_count
    query_groups = KEY_VALUE_HEADS // tensor_parallel_count
    head_repeat_count = head_count // query_groups
    head_dim = HEAD_SIZE
    score_scale = head_dim ** (-0.5)
    own_tokens = lax.axis_index("fsdp") * row_count + jnp.arange(row_count, dtype=jnp.int32)
    grad_totals = None
    outputs = []
    in_grads = []
    for micro_index in range(micro_count):
        gain_a, full_q, full_k, full_v, full_o = (
            lax.all_gather(attn_gain, "fsdp", axis=0, tiled=True),
            lax.all_gather(w_query, "fsdp", axis=0, tiled=True),
            lax.all_gather(key_weight, "fsdp", axis=0, tiled=True),
            lax.all_gather(value_weight, "fsdp", axis=0, tiled=True),
            lax.all_gather(w_out, "fsdp", axis=1, tiled=True),
        )
        gain_f, full_gate, full_up, full_down = (
            lax.all_gather(ffn_gain, "fsdp", axis=0, tiled=True),
            lax.all_gather(w_gate, "fsdp", axis=0, tiled=True),
            lax.all_gather(w_up, "fsdp", axis=0, tiled=True),
            lax.all_gather(w_down, "fsdp", axis=1, tiled=True),
        )
        reaches, starts_at, ends_at, before = tree_tables(
            parents[micro_index], seg_len[micro_index]
        )
        own_seg, own_pos = place_tokens(own_tokens, starts_at, ends_at, before)
        labels = jnp.arange(ends_at.shape[0], dtype=jnp.int32)
        own_hot = (own_seg[:, None] == labels[None, :]).astype(jnp.float32)
        allowed = jnp.dot(own_hot, reaches.astype(jnp.float32))
        cosine_table, sine_table = rope_tables(own_pos, head_dim)
        rows_in = layer_in[micro_index].astype(jnp.float32)
        normed_a = normalize(rows_in)
        attention_inner = (normed_a * gain_a.astype(jnp.float32)).astype(jnp.bfloat16)
        query_pre = jnp.dot(attention_inner, full_q, preferred_element_type=jnp.float32).reshape(
            row_count, head_count, head_dim
        )
        query_rows = rotary_apply(query_pre, cosine_table, sine_table).astype(jnp.bfloat16)
        key_pre = jnp.dot(attention_inner, full_k, preferred_element_type=jnp.float32).reshape(
            row_count, query_groups, head_dim
        )
        key_row_block = (
            rotary_apply(key_pre, cosine_table, sine_table)
            .astype(jnp.bfloat16)
            .reshape(row_count, query_groups * head_dim)
        )
        value_row_block = jnp.dot(
            attention_inner, full_v, preferred_element_type=jnp.float32
        ).astype(jnp.bfloat16)
        query_grp = query_rows.reshape(row_count, query_groups, head_repeat_count, head_dim)
        start_state = (
            jnp.full((query_groups, head_repeat_count, row_count), NEG, jnp.float32),
            jnp.zeros((query_groups, head_repeat_count, row_count), jnp.float32),
            jnp.zeros((query_groups, head_repeat_count, row_count, head_dim), jnp.float32),
        )
        fold_state = start_state
        key_piece = lax.all_gather(key_row_block, "fsdp", axis=0, tiled=True)
        value_piece = lax.all_gather(value_row_block, "fsdp", axis=0, tiled=True)
        count_rows = key_piece.shape[0]
        attend_block_rows = math.gcd(count_rows, 512)
        block_count = count_rows // attend_block_rows
        key_blocks = key_piece.reshape(block_count, attend_block_rows, query_groups, head_dim)
        value_blocks = value_piece.reshape(block_count, attend_block_rows, query_groups, head_dim)
        offsets = attend_block_rows * jnp.arange(block_count, dtype=jnp.int32)

        def advance(carry, block_items):
            key_blk, value_blk, offset = block_items
            visible = key_mask(
                allowed,
                own_tokens,
                ends_at,
                offset + jnp.arange(attend_block_rows, dtype=jnp.int32),
            )

            def attend_block(carry):
                top_run, total_run, accumulated = carry
                scores = (
                    jnp.einsum(
                        "qgrd,kgd->grqk", query_grp, key_blk, preferred_element_type=jnp.float32
                    )
                    * score_scale
                )
                scores = jnp.where(visible[None, None], scores, NEG)
                top_new = jnp.maximum(top_run, jnp.max(scores, axis=-1))
                exp_terms = jnp.where(
                    visible[None, None], jnp.exp(scores - top_new[..., None]), 0.0
                )
                factor = jnp.exp(top_run - top_new)
                total_new = total_run * factor + jnp.sum(exp_terms, axis=-1)
                accum_new = accumulated * factor[..., None] + jnp.einsum(
                    "grqk,kgd->grqd",
                    exp_terms.astype(jnp.bfloat16),
                    value_blk,
                    preferred_element_type=jnp.float32,
                )
                return (top_new, total_new, accum_new)

            return (lax.cond(jnp.any(visible), attend_block, lambda carry: carry, carry), None)

        fold_state, unused = lax.scan(advance, fold_state, (key_blocks, value_blocks, offsets))
        top_run, total_run, accumulated = fold_state
        attn_f32 = jnp.transpose(accumulated / total_run[..., None], (2, 0, 1, 3)).reshape(
            row_count, head_count * head_dim
        )
        log_total = top_run + jnp.log(total_run)
        attn_low = attn_f32.astype(jnp.bfloat16)
        middle = rows_in + lax.psum(
            jnp.dot(attn_low, full_o, preferred_element_type=jnp.float32).astype(jnp.bfloat16), "tp"
        ).astype(jnp.float32)
        normed_f = normalize(middle)
        inner_f = (normed_f * gain_f.astype(jnp.float32)).astype(jnp.bfloat16)
        gate_rows = jnp.dot(inner_f, full_gate, preferred_element_type=jnp.float32)
        up_rows = jnp.dot(inner_f, full_up, preferred_element_type=jnp.float32)
        sigmoid_gate = jax.nn.sigmoid(gate_rows)
        activated = gate_rows * sigmoid_gate
        hidden = (activated * up_rows).astype(jnp.bfloat16)
        result = middle + lax.psum(
            jnp.dot(hidden, full_down, preferred_element_type=jnp.float32).astype(jnp.bfloat16),
            "tp",
        ).astype(jnp.float32)
        outputs.append(result.astype(jnp.bfloat16))
        gain_a, full_q, full_k, full_v, full_o = (
            lax.all_gather(attn_gain, "fsdp", axis=0, tiled=True),
            lax.all_gather(w_query, "fsdp", axis=0, tiled=True),
            lax.all_gather(key_weight, "fsdp", axis=0, tiled=True),
            lax.all_gather(value_weight, "fsdp", axis=0, tiled=True),
            lax.all_gather(w_out, "fsdp", axis=1, tiled=True),
        )
        gain_f, full_gate, full_up, full_down = (
            lax.all_gather(ffn_gain, "fsdp", axis=0, tiled=True),
            lax.all_gather(w_gate, "fsdp", axis=0, tiled=True),
            lax.all_gather(w_up, "fsdp", axis=0, tiled=True),
            lax.all_gather(w_down, "fsdp", axis=1, tiled=True),
        )
        grad_rows = out_grad[micro_index].astype(jnp.float32)
        grad_low = out_grad[micro_index]
        term_down = jnp.dot(hidden.T, grad_low, preferred_element_type=jnp.float32)
        grad_hidden = jnp.dot(grad_low, full_down.T, preferred_element_type=jnp.float32)
        grad_gate = (
            grad_hidden * up_rows * sigmoid_gate * (1.0 + gate_rows * (1.0 - sigmoid_gate))
        ).astype(jnp.bfloat16)
        grad_up = (grad_hidden * activated).astype(jnp.bfloat16)
        term_gate = jnp.dot(inner_f.T, grad_gate, preferred_element_type=jnp.float32)
        term_up = jnp.dot(inner_f.T, grad_up, preferred_element_type=jnp.float32)
        unit_terms = jnp.dot(grad_gate, full_gate.T, preferred_element_type=jnp.float32) + jnp.dot(
            grad_up, full_up.T, preferred_element_type=jnp.float32
        )
        grad_inner_f = lax.psum(unit_terms.astype(jnp.bfloat16), "tp").astype(jnp.float32)
        term_gain_f = jnp.sum(grad_inner_f * normed_f, axis=0)
        grad_middle = grad_rows + norm_back(
            grad_inner_f * gain_f.astype(jnp.float32), normed_f, middle
        )
        grad_mid_low = grad_middle.astype(jnp.bfloat16)
        term_out = jnp.dot(attn_low.T, grad_mid_low, preferred_element_type=jnp.float32)
        grad_attn = jnp.dot(grad_mid_low, full_o.T, preferred_element_type=jnp.float32).astype(
            jnp.bfloat16
        )
        grad_grp = grad_attn.reshape(row_count, query_groups, head_repeat_count, head_dim)
        row_delta = jnp.sum(
            grad_grp.astype(jnp.float32)
            * attn_f32.reshape(row_count, query_groups, head_repeat_count, head_dim),
            axis=-1,
        )
        row_delta = jnp.transpose(row_delta, (1, 2, 0))
        key_all, value_all = (
            lax.all_gather(key_row_block, "fsdp", axis=0, tiled=True),
            lax.all_gather(value_row_block, "fsdp", axis=0, tiled=True),
        )
        block_rows = math.gcd(tree_row_block, 512)
        block_count = tree_row_block // block_rows
        offsets = block_rows * jnp.arange(block_count, dtype=jnp.int32)

        def retrace(grad_query, block_items):
            key_blk, value_blk, offset = block_items
            visible = key_mask(
                allowed, own_tokens, ends_at, offset + jnp.arange(block_rows, dtype=jnp.int32)
            )

            def back_block(grad_query):
                scores = (
                    jnp.einsum(
                        "qgrd,kgd->grqk", query_grp, key_blk, preferred_element_type=jnp.float32
                    )
                    * score_scale
                )
                probs = jnp.where(visible[None, None], jnp.exp(scores - log_total[..., None]), 0.0)
                grad_probs = jnp.einsum(
                    "qgrd,kgd->grqk", grad_grp, value_blk, preferred_element_type=jnp.float32
                )
                grad_scores = (probs * (grad_probs - row_delta[..., None]) * score_scale).astype(
                    jnp.bfloat16
                )
                grad_query = grad_query + jnp.einsum(
                    "grqk,kgd->qgrd", grad_scores, key_blk, preferred_element_type=jnp.float32
                )
                grad_keys = jnp.einsum(
                    "grqk,qgrd->kgd", grad_scores, query_grp, preferred_element_type=jnp.float32
                )
                grad_values = jnp.einsum(
                    "grqk,qgrd->kgd",
                    probs.astype(jnp.bfloat16),
                    grad_grp,
                    preferred_element_type=jnp.float32,
                )
                return (
                    grad_query,
                    (
                        grad_keys.reshape(block_rows, query_groups * head_dim),
                        grad_values.reshape(block_rows, query_groups * head_dim),
                    ),
                )

            def skipped(grad_query):
                empty_rows = jnp.zeros((block_rows, query_groups * head_dim), jnp.float32)
                return (grad_query, (empty_rows, empty_rows))

            return lax.cond(jnp.any(visible), back_block, skipped, grad_query)

        grad_query, (key_terms, value_terms) = lax.scan(
            retrace,
            jnp.zeros((row_count, query_groups, head_repeat_count, head_dim), jnp.float32),
            (
                key_all.reshape(block_count, block_rows, query_groups, head_dim),
                value_all.reshape(block_count, block_rows, query_groups, head_dim),
                offsets,
            ),
        )
        key_sum, value_sum = (
            lax.psum_scatter(
                key_terms.reshape(tree_row_block, query_groups * head_dim),
                "fsdp",
                scatter_dimension=0,
                tiled=True,
            ),
            lax.psum_scatter(
                value_terms.reshape(tree_row_block, query_groups * head_dim),
                "fsdp",
                scatter_dimension=0,
                tiled=True,
            ),
        )
        grad_key_pre = (
            rotate_back(
                key_sum.reshape(row_count, query_groups, head_dim), cosine_table, sine_table
            )
            .astype(jnp.bfloat16)
            .reshape(row_count, query_groups * head_dim)
        )
        grad_value_low = value_sum.astype(jnp.bfloat16)
        grad_query_pre = (
            rotate_back(
                grad_query.reshape(row_count, head_count, head_dim), cosine_table, sine_table
            )
            .astype(jnp.bfloat16)
            .reshape(row_count, head_count * head_dim)
        )
        term_q = jnp.dot(attention_inner.T, grad_query_pre, preferred_element_type=jnp.float32)
        term_k = jnp.dot(attention_inner.T, grad_key_pre, preferred_element_type=jnp.float32)
        term_v = jnp.dot(attention_inner.T, grad_value_low, preferred_element_type=jnp.float32)
        head_terms = (
            jnp.dot(grad_query_pre, full_q.T, preferred_element_type=jnp.float32)
            + jnp.dot(grad_key_pre, full_k.T, preferred_element_type=jnp.float32)
            + jnp.dot(grad_value_low, full_v.T, preferred_element_type=jnp.float32)
        )
        grad_inner_a = lax.psum(head_terms.astype(jnp.bfloat16), "tp").astype(jnp.float32)
        term_gain_a = jnp.sum(grad_inner_a * normed_a, axis=0)
        in_grads.append(
            grad_middle + norm_back(grad_inner_a * gain_a.astype(jnp.float32), normed_a, rows_in)
        )
        shares = (
            term_gain_a,
            term_q,
            term_k,
            term_v,
            term_out,
            term_gain_f,
            term_gate,
            term_up,
            term_down,
        )
        grad_totals = (
            shares if grad_totals is None else tuple((a + b for a, b in zip(grad_totals, shares)))
        )
    grad_totals = (
        lax.psum_scatter(grad_totals[0], "fsdp", scatter_dimension=0, tiled=True),
        lax.psum_scatter(grad_totals[1], "fsdp", scatter_dimension=0, tiled=True),
        lax.psum_scatter(grad_totals[2], "fsdp", scatter_dimension=0, tiled=True),
        lax.psum_scatter(grad_totals[3], "fsdp", scatter_dimension=0, tiled=True),
        lax.psum_scatter(grad_totals[4], "fsdp", scatter_dimension=1, tiled=True),
        lax.psum_scatter(grad_totals[5], "fsdp", scatter_dimension=0, tiled=True),
        lax.psum_scatter(grad_totals[6], "fsdp", scatter_dimension=0, tiled=True),
        lax.psum_scatter(grad_totals[7], "fsdp", scatter_dimension=0, tiled=True),
        lax.psum_scatter(grad_totals[8], "fsdp", scatter_dimension=1, tiled=True),
    )
    return (
        jnp.stack(outputs),
        jnp.stack(in_grads),
        grad_totals[0],
        grad_totals[1],
        grad_totals[2],
        grad_totals[3],
        grad_totals[4],
        grad_totals[5],
        grad_totals[6],
        grad_totals[7],
        grad_totals[8],
    )


def solution(mesh):
    in_specs = (
        P(None, "fsdp", None),
        P(None, "fsdp", None),
        P(),
        P(),
        P("fsdp"),
        P("fsdp", "tp"),
        P("fsdp", "tp"),
        P("fsdp", "tp"),
        P("tp", "fsdp"),
        P("fsdp"),
        P("fsdp", "tp"),
        P("fsdp", "tp"),
        P("tp", "fsdp"),
    )
    out_specs = (
        P(None, "fsdp", None),
        P(None, "fsdp", None),
        P("fsdp"),
        P("fsdp", "tp"),
        P("fsdp", "tp"),
        P("fsdp", "tp"),
        P("tp", "fsdp"),
        P("fsdp"),
        P("fsdp", "tp"),
        P("fsdp", "tp"),
        P("tp", "fsdp"),
    )
    return jax.shard_map(shards, mesh=mesh, in_specs=in_specs, out_specs=out_specs, check_vma=False)
```

profile of v0, /device:TPU:0, one launch (start us, length us, event | category | flops | bytes accessed | tf_op | source)
XLA Modules:
  0.0 4177.3 jit_solution(43257257959838387)
XLA Ops:
  102.2 39.6 all-gather.18.cloned.1.call-done
  157.2 38.9 all-gather.32.cloned.1.call-done
  204.5 42.9 %all-gather.34.cloned.1.call-done = bf16[8192,256]{1,0:T(8,128)(2,1)} async-done(((bf16[512,256]{1,0:T(8,128)(2,1)}), bf16[8192,256]{1,0:T(8,128)(2,1)}) %all-gather.34.cloned.1.call-update) | async-done | bytes 4194320 | tf_op jit(solution)/shard_map/all_gather | solution.py:185
  274.7 65.1 %while.67 = (s32[]{:T(128)}, f32[4,4,512]{2,1,0:T(4,128)S(1)}, f32[4,4,512]{2,1,0:T(4,128)S(1)}, f32[4,4,512,64]{2,3,1,0:T(8,128)}, s32[16]{0:T(128)S(1)}, /*ind...) while((s32[]{:T(128)}, f32[4,4,512]{2,1,0:T(4,128)S(1)}, ...), condition=%wide.region_34.35_spmd.clone, body=%wide.region_27.34_spmd.clone.sunk | while | flops 1137224192 | bytes 74477944 | solution.py:227
  381.0 63.5 %while.66 = (s32[]{:T(128)}, f32[4,4,512]{2,1,0:T(4,128)S(1)}, f32[4,4,512]{2,1,0:T(4,128)S(1)}, f32[4,4,512,64]{2,3,1,0:T(8,128)S(1)}, s32[16]{0:T(128)S(1)}, /...) while((s32[]{:T(128)}, f32[4,4,512]{2,1,0:T(4,128)S(1)}, ...), condition=%wide.region_15.16_spmd.clone, body=%wide.region_8.15_spmd.clone.sunk | while | flops 1137224192 | bytes 57700672 | solution.py:227
  458.2 214.5 %all-gather.1 = bf16[16,1,128]{2,1,0:T(2,128)(2,1)S(1)} all-gather(bf16[1,1,128]{2,1,0:T(2,128)(2,1)S(1)} %bitcast.574), channel_id=1, replica_groups=mesh['fsdp'=16,'tp'=2] {'fsdp'}, dimensions={0}, use_global_device_ids=true | all-gather | bytes 4352 | tf_op jit(solution)/shard_map/all_gather | solution.py:146
  672.7 87.9 %all-reduce.14.cloned.1.call-done = (bf16[512,2048]{1,0:T(8,128)(2,1)}, bf16[512,2048]{1,0:T(8,128)(2,1)}) async-done(((bf16[512,2048]{1,0:T(8,128)(2,1)}, bf16[512,2048]{1,0:T(8,128)(2,1)}), (bf16[512,2048]{1,0:T(8,128)(2,1)}, bf16[512,2048]{1,0:T(8,128)(2,1)})) %all-reduce.14.cloned.1.call-update) | async-done | bytes 4194320 | tf_op jit(solution)/shard_map/psum | solution.py:234
  770.6 119.2 %all-gather.26.cloned.1.call-done = bf16[2048,4096]{1,0:T(8,128)(2,1)} async-done(((bf16[128,4096]{1,0:T(8,128)(2,1)}), bf16[2048,4096]{1,0:T(8,128)(2,1)}) %all-gather.26.cloned.1.call-update) | async-done | bytes 16777232 | tf_op jit(solution)/shard_map/all_gather | solution.py:147
  904.2 113.0 %all-gather.28.cloned.1.call-done = bf16[2048,4096]{1,0:T(8,128)(2,1)} async-done(((bf16[128,4096]{1,0:T(8,128)(2,1)}), bf16[2048,4096]{1,0:T(8,128)(2,1)}) %all-gather.28.cloned.1.call-update) | async-done | bytes 16777232 | tf_op jit(solution)/shard_map/all_gather | solution.py:148
  1057.4 90.6 %all-gather.30.cloned.1.call-done = bf16[4096,2048]{1,0:T(8,128)(2,1)} async-done(((bf16[4096,128]{1,0:T(8,128)(2,1)}), bf16[4096,2048]{1,0:T(8,128)(2,1)}) %all-gather.30.cloned.1.call-update) | async-done | bytes 16777232 | tf_op jit(solution)/shard_map/all_gather | solution.py:149
  1252.4 105.8 %all-reduce.12.cloned.1.call-done = (bf16[512,2048]{1,0:T(8,128)(2,1)}, bf16[512,2048]{1,0:T(8,128)(2,1)}) async-done(((bf16[512,2048]{1,0:T(8,128)(2,1)}, bf16[512,2048]{1,0:T(8,128)(2,1)}), (bf16[512,2048]{1,0:T(8,128)(2,1)}, bf16[512,2048]{1,0:T(8,128)(2,1)})) %all-reduce.12.cloned.1.call-update) | async-done | bytes 4194320 | tf_op jit(solution)/shard_map/psum | solution.py:275
  1389.7 209.9 %while.69 = (s32[]{:T(128)}, f32[512,4,4,64]{0,3,2,1:T(8,128)S(1)}, f32[16,512,256]{2,1,0:T(8,128)}, f32[16,512,256]{2,1,0:T(8,128)}, s32[16]{0:T(128)S(1)}, /*i...) while((s32[]{:T(128)}, f32[512,4,4,64]{0,3,2,1:T(8,128)S(1)}, ...), condition=%wide.region_59.60_spmd.clone, body=%wide.region_54.59_spmd.clone.sunk | while | flops 2738907648 | bytes 95024480 | solution.py:346
  1618.7 210.0 %while.68 = (s32[]{:T(128)}, f32[512,4,4,64]{0,3,2,1:T(8,128)S(1)}, f32[16,512,256]{2,1,0:T(8,128)}, f32[16,512,256]{2,1,0:T(8,128)}, s32[16]{0:T(128)S(1)}, /*i...) while((s32[]{:T(128)}, f32[512,4,4,64]{0,3,2,1:T(8,128)S(1)}, ...), condition=%wide.region_46.47_spmd.clone, body=%wide.region_41.46_spmd.clone.sunk | while | flops 2738907648 | bytes 95024480 | solution.py:346
  1871.0 92.4 %reduce-scatter.16.cloned.1.call-done = f32[512,256]{1,0:T(8,128)} async-done(((f32[8192,256]{1,0:T(8,128)}), f32[512,256]{1,0:T(8,128)}) %reduce-scatter.16.cloned.1.call-update) | async-done | bytes 524304 | tf_op jit(solution)/shard_map/reduce_scatter | solution.py:356
  1964.6 424.7 %reduce-scatter.12.cloned.1.call-done = f32[512,256]{1,0:T(8,128)} async-done(((f32[8192,256]{1,0:T(8,128)}), f32[512,256]{1,0:T(8,128)}) %reduce-scatter.12.cloned.1.call-update) | async-done | bytes 524304 | tf_op jit(solution)/shard_map/reduce_scatter | solution.py:356
  2396.4 101.2 %reduce-scatter.18.cloned.1.call-done = f32[512,256]{1,0:T(8,128)} async-done(((f32[8192,256]{1,0:T(8,128)}), f32[512,256]{1,0:T(8,128)}) %reduce-scatter.18.cloned.1.call-update) | async-done | bytes 524304 | tf_op jit(solution)/shard_map/reduce_scatter | solution.py:362
  2503.4 102.5 %reduce-scatter.14.cloned.1.call-done = f32[512,256]{1,0:T(8,128)} async-done(((f32[8192,256]{1,0:T(8,128)}), f32[512,256]{1,0:T(8,128)}) %reduce-scatter.14.cloned.1.call-update) | async-done | bytes 524304 | tf_op jit(solution)/shard_map/reduce_scatter | solution.py:362
  2816.0 63.5 %all-reduce.2 = (f32[2048]{0:T(1024)S(1)}, f32[2048]{0:T(1024)S(1)}) all-reduce(f32[2048]{0:T(1024)S(1)} %add.369, f32[2048]{0:T(1024)S(1)} %add.374), channel_id=6, replica_groups=mesh['fsdp'=16,'tp'=2] {'fsdp'}, use_global_device_ids=true, to_apply=%region_66.67.clone | all-reduce | flops 4096 | bytes 32768
  2921.0 109.1 %reduce-scatter.26.cloned.1.call-done = f32[1024,128]{1,0:T(8,128)} async-done(((f32[1024,2048]{1,0:T(8,128)}), f32[1024,128]{1,0:T(8,128)}) %reduce-scatter.26.cloned.1.call-update) | async-done | bytes 524304 | tf_op jit(solution)/shard_map/reduce_scatter | solution.py:416
  3030.1 65.7 %reduce-scatter.22.cloned.1.call-done = f32[128,256]{1,0:T(8,128)} async-done(((f32[2048,256]{1,0:T(8,128)}), f32[128,256]{1,0:T(8,128)}) %reduce-scatter.22.cloned.1.call-update) | async-done | bytes 131088 | tf_op jit(solution)/shard_map/reduce_scatter | solution.py:414
  3095.8 65.4 %reduce-scatter.24.cloned.1.call-done = f32[128,256]{1,0:T(8,128)} async-done(((f32[2048,256]{1,0:T(8,128)}), f32[128,256]{1,0:T(8,128)}) %reduce-scatter.24.cloned.1.call-update) | async-done | bytes 131088 | tf_op jit(solution)/shard_map/reduce_scatter | solution.py:415
  3161.1 336.5 %reduce-scatter.28.cloned.1.call-done = f32[128,4096]{1,0:T(8,128)} async-done(((f32[2048,4096]{1,0:T(8,128)}), f32[128,4096]{1,0:T(8,128)}) %reduce-scatter.28.cloned.1.call-update) | async-done | bytes 2097168 | tf_op jit(solution)/shard_map/reduce_scatter | solution.py:418
  3497.6 336.4 %reduce-scatter.30.cloned.1.call-done = f32[128,4096]{1,0:T(8,128)} async-done(((f32[2048,4096]{1,0:T(8,128)}), f32[128,4096]{1,0:T(8,128)}) %reduce-scatter.30.cloned.1.call-update) | async-done | bytes 2097168 | tf_op jit(solution)/shard_map/reduce_scatter | solution.py:419
  3834.0 336.5 %reduce-scatter.32.cloned.1.call-done = f32[4096,128]{1,0:T(8,128)} async-done(((f32[4096,2048]{1,0:T(8,128)}), f32[4096,128]{1,0:T(8,128)}) %reduce-scatter.32.cloned.1.call-update) | async-done | bytes 2097168 | tf_op jit(solution)/shard_map/reduce_scatter | solution.py:420
  (919 shorter events, 1378.4 us)
Async XLA Ops:
  7.9 82.1 %all-gather.20.cloned.1.call-start = ((), (), s32[]{:S(2)}) async-start(), calls=%async_computation.14 | async-start | bytes 1114112 | tf_op jit(solution)/shard_map/all_gather | solution.py:142
  8.7 133.1 %all-gather.18.cloned.1.call-start = ((), (), s32[]{:S(2)}) async-start(), calls=%async_computation.13 | async-start | bytes 4456448 | tf_op jit(solution)/shard_map/all_gather | solution.py:140
  9.4 186.7 %all-gather.32.cloned.1.call-start = ((), (), s32[]{:S(2)}) async-start(), calls=%async_computation.20 | async-start | bytes 4456448 | tf_op jit(solution)/shard_map/all_gather | solution.py:184
  55.7 191.7 %all-gather.34.cloned.1.call-start = ((), (), s32[]{:S(2)}) async-start(), calls=%async_computation.21 | async-start | bytes 4456448 | tf_op jit(solution)/shard_map/all_gather | solution.py:185
  93.3 246.5 %all-gather.16.cloned.1.call-start = ((), (), s32[]{:S(2)}) async-start(), calls=%async_computation.12 | async-start | bytes 4456448 | tf_op jit(solution)/shard_map/all_gather | solution.py:184
  96.8 256.8 %all-gather.22.cloned.1.call-start = ((), (), s32[]{:S(2)}) async-start(), calls=%async_computation.15 | async-start | bytes 4456448 | tf_op jit(solution)/shard_map/all_gather | solution.py:185
  99.9 346.1 %all-gather.24.cloned.1.call-start = ((), (), s32[]{:S(2)}) async-start(), calls=%async_computation.16 | async-start | bytes 4456448 | tf_op jit(solution)/shard_map/all_gather | solution.py:143
  100.7 659.9 %all-reduce.14.cloned.1.call-start = ((), (), s32[]{:S(2)}) async-start(), calls=%async_computation.35 | async-start | bytes 8388608 | tf_op jit(solution)/shard_map/psum | solution.py:234
  456.2 433.6 %all-gather.26.cloned.1.call-start = ((), (), s32[]{:S(2)}) async-start(), calls=%async_computation.17 | async-start | bytes 17825792 | tf_op jit(solution)/shard_map/all_gather | solution.py:147
  456.8 560.4 %all-gather.28.cloned.1.call-start = ((), (), s32[]{:S(2)}) async-start(), calls=%async_computation.18 | async-start | bytes 17825792 | tf_op jit(solution)/shard_map/all_gather | solution.py:148
  457.6 690.5 %all-gather.30.cloned.1.call-start = ((), (), s32[]{:S(2)}) async-start(), calls=%async_computation.19 | async-start | bytes 17825792 | tf_op jit(solution)/shard_map/all_gather | solution.py:149
  458.1 900.0 %all-reduce.12.cloned.1.call-start = ((), (), s32[]{:S(2)}) async-start(), calls=%async_computation.34 | async-start | bytes 8388608 | tf_op jit(solution)/shard_map/psum | solution.py:275
  1251.6 711.7 %reduce-scatter.16.cloned.1.call-start = ((), (), s32[]{:S(2)}) async-start(), calls=%async_computation.24 | async-start | bytes 8912896 | tf_op jit(solution)/shard_map/reduce_scatter | solution.py:356
  1600.9 788.4 %reduce-scatter.12.cloned.1.call-start = ((), (), s32[]{:S(2)}) async-start(), calls=%async_computation.22 | async-start | bytes 8912896 | tf_op jit(solution)/shard_map/reduce_scatter | solution.py:356
  1828.7 668.9 %reduce-scatter.18.cloned.1.call-start = ((), (), s32[]{:S(2)}) async-start(), calls=%async_computation.25 | async-start | bytes 8912896 | tf_op jit(solution)/shard_map/reduce_scatter | solution.py:362
  1829.3 776.6 %reduce-scatter.14.cloned.1.call-start = ((), (), s32[]{:S(2)}) async-start(), calls=%async_computation.23 | async-start | bytes 8912896 | tf_op jit(solution)/shard_map/reduce_scatter | solution.py:362
  1829.9 981.2 %all-reduce.10.cloned.1.call-start = ((), (), s32[]{:S(2)}) async-start(), calls=%async_computation.33 | async-start | bytes 16777216 | tf_op jit(solution)/shard_map/psum | solution.py:244
  2611.6 309.3 %reduce-scatter.20.cloned.1.call-start = ((), (), s32[]{:S(2)}) async-start(), calls=%async_computation.26 | async-start | bytes 8912896 | tf_op jit(solution)/shard_map/reduce_scatter | solution.py:413
  2623.3 406.8 %reduce-scatter.26.cloned.1.call-start = ((), (), s32[]{:S(2)}) async-start(), calls=%async_computation.29 | async-start | bytes 8912896 | tf_op jit(solution)/shard_map/reduce_scatter | solution.py:416
  2634.9 460.9 %reduce-scatter.22.cloned.1.call-start = ((), (), s32[]{:S(2)}) async-start(), calls=%async_computation.27 | async-start | bytes 2228224 | tf_op jit(solution)/shard_map/reduce_scatter | solution.py:414
  2641.2 519.9 %reduce-scatter.24.cloned.1.call-start = ((), (), s32[]{:S(2)}) async-start(), calls=%async_computation.28 | async-start | bytes 2228224 | tf_op jit(solution)/shard_map/reduce_scatter | solution.py:415
  2647.2 850.3 %reduce-scatter.28.cloned.1.call-start = ((), (), s32[]{:S(2)}) async-start(), calls=%async_computation.30 | async-start | bytes 35651584 | tf_op jit(solution)/shard_map/reduce_scatter | solution.py:418
  2690.5 1143.5 %reduce-scatter.30.cloned.1.call-start = ((), (), s32[]{:S(2)}) async-start(), calls=%async_computation.31 | async-start | bytes 35651584 | tf_op jit(solution)/shard_map/reduce_scatter | solution.py:419
  2734.0 1436.6 %reduce-scatter.32.cloned.1.call-start = ((), (), s32[]{:S(2)}) async-start(), calls=%async_computation.32 | async-start | bytes 35651584 | tf_op jit(solution)/shard_map/reduce_scatter | solution.py:420
  (99 other events, 2780.9 us)
Sparse Core Ops, SparseCore 0:
  10.2 40.7 all-gather.13
  92.1 49.5 all-gather.17
  144.3 51.6 all-gather.31
  198.7 48.7 all-gather.33
  250.0 51.6 all-gather.15
  304.5 49.0 all-gather.21
  355.7 51.7 all-gather.23
  456.4 304.2 all-reduce.13
  762.9 126.8 all-gather.25
  892.2 124.9 all-gather.27
  1019.5 128.5 all-gather.29
  1251.8 106.3 all-reduce.11
  1599.7 363.5 reduce-scatter.15
  1967.3 421.9 reduce-scatter.11
  2393.3 104.3 reduce-scatter.17
  2501.5 104.3 reduce-scatter.13
  2611.7 199.3 all-reduce.9
  2815.8 105.1 reduce-scatter.19
  2925.4 104.6 reduce-scatter.25
  3034.4 61.2 reduce-scatter.21
  3100.5 60.5 reduce-scatter.23
  3166.0 331.5 reduce-scatter.27
  3502.3 331.7 reduce-scatter.29
  3838.8 331.6 reduce-scatter.31
  (1 shorter events, 36.8 us)
where the time goes:
time: 4190 us; the launch traced here: 4180 us
  waiting for transfers between devices  2720 us (65%)
  matrix products  574 us (14%)
  local copies, waits for them, and re-layouts  409 us (10%)
  blocking collectives  301 us (7%)
  other arithmetic  114 us (3%)
  loops' own time  45.7 us (1%)
    reduce_scatter x2, waiting for transfers between devices, shards(): lax.psum_scatter(key_terms.reshape(tree_row_block, query_groups * head_di...  517 us
    reduce_scatter x1, waiting for transfers between devices, shards(): lax.psum_scatter(grad_totals[8], 'fsdp', scatter_dimension=1, tiled=True)  337 us
    reduce_scatter x1, waiting for transfers between devices, shards(): lax.psum_scatter(grad_totals[6], 'fsdp', scatter_dimension=0, tiled=True)  336 us
    reduce_scatter x1, waiting for transfers between devices, shards(): lax.psum_scatter(grad_totals[7], 'fsdp', scatter_dimension=0, tiled=True)  336 us
    all_gather x1, blocking collectives, shards(): lax.all_gather(ffn_gain, 'fsdp', axis=0, tiled=True)  215 us
    reduce_scatter x2, waiting for transfers between devices, shards(): lax.psum_scatter(value_terms.reshape(tree_row_block, query_groups * head_...  204 us
    dynamic_update_slice x96, local copies, waits for them, and re-layouts, shards(): lax.scan(retrace, jnp.zeros((row_count, query_groups, head_repeat_count,...  202 us
    all_gather x1, waiting for transfers between devices, shards(): lax.all_gather(w_gate, 'fsdp', axis=0, tiled=True)  119 us
  transfers between devices with their start and end apart: 25, of which 23 were waited for; matrix products, arithmetic and copies ran while one was open for 18% of the time, Pallas kernels for 0%

commit v1 on v0

v1 whole, which is shorter than its diff:
```python
import functools
import math

import jax
import jax.numpy as jnp
from jax import lax
from jax.experimental import pallas as pl
from jax.experimental.pallas import tpu as pltpu
from jax.sharding import Mesh
from jax.sharding import PartitionSpec as P

QUERY_HEADS = 32
KEY_VALUE_HEADS = 8
HEAD_SIZE = 64
LEVELS = 3

EPS = 1e-05
THETA = 500000.0
NEG = -1e30
LN2 = math.log(2.0)
SWAP = [(0, 1), (1, 0)]
F32 = jnp.float32
BF16 = jnp.bfloat16


def dot(left, right, left_dim=1, right_dim=0):
    return lax.dot_general(
        left, right, (((left_dim,), (right_dim,)), ((), ())), preferred_element_type=F32
    )


def row_scale_of(rows_in):
    return lax.rsqrt(jnp.mean(rows_in * rows_in, axis=-1, keepdims=True) + EPS)


def norm_back(grad_normed, normed, row_scale):
    return row_scale * (
        grad_normed - normed * jnp.mean(grad_normed * normed, axis=-1, keepdims=True)
    )


def rope_angles(position, head_dim):
    half_dim = head_dim // 2
    index_row = jnp.arange(half_dim, dtype=F32)
    inverse = THETA ** (-2.0 * index_row / head_dim)
    wavelen = 2.0 * math.pi / inverse
    smooth = jnp.clip((8192.0 / wavelen - 1.0) / 3.0, 0.0, 1.0)
    inverse = (1.0 - smooth) * inverse / 32.0 + smooth * inverse
    return inverse[:, None] * position.astype(F32)[None, :]


def turn(first_half, second_half, cosine, sine):
    return first_half * cosine - second_half * sine, second_half * cosine + first_half * sine


def tree_tables(parents_row, lengths):
    seg_count = parents_row.shape[0]
    labels = jnp.arange(seg_count, dtype=jnp.int32)
    ends_at = jnp.cumsum(lengths)
    starts_at = ends_at - lengths
    reaches = labels[:, None] == labels[None, :]
    climber = labels
    for _ in range(LEVELS - 1):
        climber = jnp.sum(
            jnp.where(climber[:, None] == labels[None, :], parents_row[None, :], 0), axis=1
        )
        reaches = reaches | (climber[:, None] == labels[None, :])
    before = jnp.sum(
        jnp.where(reaches & (labels[:, None] != labels[None, :]), lengths[None, :], 0), axis=1
    )
    return reaches, starts_at, ends_at, before


def after(value, *others):
    return lax.optimization_barrier((value,) + others)[0]


class Ring:
    def __init__(self):
        self.count = lax.axis_size("zy")
        count = self.count
        place = [2 * i if i < count // 2 else 2 * (count - 1 - i) + 1 for i in range(count)]
        self.right = [(place[i], place[(i + 1) % count]) for i in range(count)]
        self.left = [(b, a) for a, b in self.right]
        me = lax.axis_index("zy")
        self.spot = jnp.where(me % 2 == 0, me // 2, count - 1 - me // 2)

    def chip(self, offset):
        spot = lax.rem(self.spot + offset + self.count, self.count)
        return jnp.where(spot < self.count // 2, 2 * spot, 2 * (self.count - 1 - spot) + 1)

    def go_right(self, value):
        return lax.ppermute(value, "zy", self.right)

    def go_left(self, value):
        return lax.ppermute(value, "zy", self.left)

    def gather(self, piece, line=None):
        count, half = self.count, self.count // 2
        cut = piece.shape[0] // 2
        if line is not None:
            piece = after(piece, *line)
        zeros = (0,) * (piece.ndim - 1)
        whole = jnp.zeros((count,) + piece.shape, piece.dtype)

        def put(whole, part, offset, row=0):
            return lax.dynamic_update_slice(whole, part[None], (self.chip(offset), row) + zeros)

        whole = put(whole, piece, 0)
        rightward = leftward = piece
        for step in range(1, half):
            rightward = self.go_right(rightward)
            leftward = self.go_left(leftward)
            whole = put(whole, rightward, -step)
            whole = put(whole, leftward, step)
        mark = (rightward, leftward)
        whole = put(whole, self.go_right(rightward[:cut]), half)
        whole = put(whole, self.go_left(leftward[cut:]), half, cut)
        return whole, mark

    def reduce(self, terms, line=None):
        half = self.count // 2
        cut = terms.shape[1] // 2
        if line is not None:
            terms = after(terms, *line)

        def term(offset):
            return lax.dynamic_index_in_dim(terms, self.chip(offset), 0, keepdims=False)

        far = term(half)
        rightward = self.go_right(far[:cut])
        leftward = self.go_left(far[cut:])
        for step in range(half - 1, 0, -1):
            mine, other = term(step), term(-step)
            if step == half - 1:
                rightward = jnp.concatenate([add_low(mine[:cut], rightward), mine[cut:]], axis=0)
                leftward = jnp.concatenate([other[:cut], add_low(other[cut:], leftward)], axis=0)
            else:
                rightward, leftward = add_low(mine, rightward), add_low(other, leftward)
            rightward, leftward = self.go_right(rightward), self.go_left(leftward)
        total = term(0).astype(F32) + rightward.astype(F32) + leftward.astype(F32)
        return total, (rightward, leftward)


def add_low(left, right):
    return (left.astype(F32) + right.astype(F32)).astype(BF16)


def other_core(value):
    return lax.ppermute(value, "core", SWAP)


def other_half(value):
    return lax.ppermute(value, "tp", SWAP)


def by_core(own, other, axis):
    first = lax.axis_index("core") == 0
    return jnp.concatenate(
        [jnp.where(first, own, other), jnp.where(first, other, own)], axis=axis
    )


def split_by_core(value, axis):
    core = lax.axis_index("core")
    size = value.shape[axis] // 2
    return (
        lax.dynamic_slice_in_dim(value, core * size, size, axis),
        lax.dynamic_slice_in_dim(value, (1 - core) * size, size, axis),
    )


def split3(value):
    high = value.astype(BF16)
    rest = value - high.astype(F32)
    middle = rest.astype(BF16)
    low = (rest - middle.astype(F32)).astype(BF16)
    return high, middle, low


def causal(scores, block):
    key_at = lax.broadcasted_iota(jnp.int32, scores.shape, 0)
    query_at = lax.rem(lax.broadcasted_iota(jnp.int32, scores.shape, 1), block)
    return jnp.where(key_at <= query_at, scores, NEG)


def block_of(ref, index, block, per_piece, lanes):
    piece = lax.div(index, per_piece)
    start = pl.multiple_of(lax.rem(index, per_piece) * block, block)
    return ref[piece, 0, pl.ds(start, block), lanes]


KEYS = slice(0, 128)
VALUES = slice(128, 256)


def attend_kernel(
    block, rep, per_piece, count_ref, list_ref, diag_ref, query_ref, mask_ref, kv_ref, hot_ref,
    out_ref, lse_ref, query_aug, value_turned,
):
    group, at = pl.program_id(0), pl.program_id(1)
    key_blocks = hot_ref.shape[0] // block - 1

    @pl.when((group == 0) & (at == 0))
    def _():
        rows = per_piece * block
        for piece in range(kv_ref.shape[0]):
            value_turned[:, piece * rows : (piece + 1) * rows] = kv_ref[piece, 0, :, VALUES].T

    query_aug[...] = jnp.zeros_like(query_aug)
    own = pl.ds(pl.multiple_of(group * HEAD_SIZE, HEAD_SIZE), HEAD_SIZE)
    for r in range(rep):
        columns = slice(r * block, (r + 1) * block)
        query_aug[own, columns] = query_ref[r * HEAD_SIZE : (r + 1) * HEAD_SIZE, :]
        query_aug[128:144, columns] = mask_ref[...]

    def scores_of(index):
        keys = block_of(kv_ref, jnp.minimum(index, key_blocks - 1), block, per_piece, KEYS)
        hot = hot_ref[pl.ds(pl.multiple_of(index * block, block), block), :]
        return jnp.dot(
            jnp.concatenate([keys, hot], axis=1), query_aug[...], preferred_element_type=F32
        )

    def values_of(index):
        index = jnp.minimum(index, key_blocks - 1)
        return value_turned[own, pl.ds(pl.multiple_of(index * block, block), block)]

    diagonal = diag_ref[at]
    scores = causal(scores_of(diagonal), block)
    top = jnp.max(scores, axis=0, keepdims=True)
    probs = jnp.exp2(scores - top)
    total = jnp.sum(probs, axis=0, keepdims=True)
    mixed = jnp.dot(values_of(diagonal), probs.astype(BF16), preferred_element_type=F32)

    def step(j, carry):
        top, total, mixed = carry
        one, two = list_ref[at, 2 * j], list_ref[at, 2 * j + 1]
        first, second = scores_of(one), scores_of(two)
        new = jnp.maximum(top, jnp.max(first, axis=0, keepdims=True))
        new = jnp.maximum(new, jnp.max(second, axis=0, keepdims=True))
        factor = jnp.exp2(top - new)
        first, second = jnp.exp2(first - new), jnp.exp2(second - new)
        total = (
            total * factor
            + jnp.sum(first, axis=0, keepdims=True)
            + jnp.sum(second, axis=0, keepdims=True)
        )
        values = jnp.concatenate([values_of(one), values_of(two)], axis=1)
        probs = jnp.concatenate([first.astype(BF16), second.astype(BF16)], axis=0)
        mixed = mixed * factor + jnp.dot(values, probs, preferred_element_type=F32)
        return new, total, mixed

    pairs = lax.div(count_ref[at] + 1, 2)
    top, total, mixed = lax.fori_loop(0, pairs, step, (top, total, mixed))
    mixed = mixed * (1.0 / total)
    lse = top + jnp.log2(total)
    for r in range(rep):
        columns = slice(r * block, (r + 1) * block)
        out_ref[r * HEAD_SIZE : (r + 1) * HEAD_SIZE, :] = mixed[:, columns].astype(BF16)
        lse_ref[0, r : r + 1, :] = lse[:, columns]


def attend(tree, tables, query, mask, kv, rep, block):
    counts, lists, diagonals, hot = tables
    heads = query.shape[0]
    pieces, _, rows, _ = kv.shape
    groups, query_blocks = heads // (rep * HEAD_SIZE), rows // block
    keys = pieces * rows
    grid_spec = pltpu.PrefetchScalarGridSpec(
        num_scalar_prefetch=3,
        grid=(groups, query_blocks),
        in_specs=[
            pl.BlockSpec(
                (rep * HEAD_SIZE, block), lambda g, q, *_: (g, tree * query_blocks + q)
            ),
            pl.BlockSpec((16, block), lambda g, q, *_: (0, q)),
            pl.BlockSpec((pieces, 1, rows, 256), lambda g, q, *_: (0, 0, 0, 0)),
            pl.BlockSpec((keys + block, 128), lambda g, q, *_: (0, 0)),
        ],
        out_specs=[
            pl.BlockSpec((rep * HEAD_SIZE, block), lambda g, q, *_: (g, q)),
            pl.BlockSpec((1, rep, block), lambda g, q, *_: (g, 0, q)),
        ],
        scratch_shapes=[
            pltpu.VMEM((256, rep * block), BF16),
            pltpu.VMEM((128, keys), BF16),
        ],
    )
    return pl.pallas_call(
        functools.partial(attend_kernel, block, rep, rows // block),
        grid_spec=grid_spec,
        out_shape=[
            jax.ShapeDtypeStruct((heads, rows), BF16),
            jax.ShapeDtypeStruct((groups, rep, rows), F32),
        ],
        compiler_params=pltpu.CompilerParams(vmem_limit_bytes=48 * 2**20),
        cost_estimate=pl.CostEstimate(
            flops=28 * 10**9, bytes_accessed=12 * 2**20, transcendentals=0
        ),
        name="tree_attention",
    )(counts, lists, diagonals, query, mask, kv, hot)


def attend_back_kernel(
    block, rep, per_piece, seen_ref, query_ref, mask_ref, mixed_ref, grad_ref, lse_ref, kv_ref,
    hot_ref, grad_query_ref, grad_kv_ref, query_aug, grad_aug, query_rows, grad_rows, key_turned,
    grad_query, grad_keys, grad_values,
):
    group = pl.program_id(0)
    rows = per_piece * block
    query_blocks = rows // block
    key_blocks = kv_ref.shape[0] * per_piece
    width = rep * block

    @pl.when(group == 0)
    def _():
        for piece in range(kv_ref.shape[0]):
            key_turned[:, piece * rows : (piece + 1) * rows] = kv_ref[piece, 0, :, KEYS].T
        grad_keys[...] = jnp.zeros_like(grad_keys)
        grad_values[...] = jnp.zeros_like(grad_values)

    query_aug[...] = jnp.zeros_like(query_aug)
    grad_aug[...] = jnp.zeros_like(grad_aug)
    grad_query[...] = jnp.zeros_like(grad_query)
    own = pl.ds(pl.multiple_of(group * HEAD_SIZE, HEAD_SIZE), HEAD_SIZE)
    none = jnp.zeros((HEAD_SIZE, block), BF16)
    for at in range(query_blocks):
        columns = slice(at * block, (at + 1) * block)
        for r in range(rep):
            here = slice(at * width + r * block, at * width + (r + 1) * block)
            head = slice(r * HEAD_SIZE, (r + 1) * HEAD_SIZE)
            query, grad = query_ref[head, columns], grad_ref[head, columns]
            query_aug[own, here] = query
            grad_aug[own, here] = grad
            delta = jnp.sum(
                grad.astype(F32) * mixed_ref[head, columns].astype(F32), axis=0, keepdims=True
            )
            empty = jnp.zeros((13, block), BF16)
            query_aug[128:160, here] = jnp.concatenate(
                [mask_ref[:, columns], *split3(-lse_ref[0, r : r + 1, columns]), empty], axis=0
            )
            grad_aug[128:160, here] = jnp.concatenate(
                [jnp.zeros((16, block), BF16), *split3(-delta), empty], axis=0
            )

            @pl.when(group == 0)
            def _():
                query_rows[here, :] = jnp.concatenate([query, none], axis=0).T
                grad_rows[here, :] = jnp.concatenate([grad, none], axis=0).T

            @pl.when(group == 1)
            def _():
                query_rows[here, :] = jnp.concatenate([none, query], axis=0).T
                grad_rows[here, :] = jnp.concatenate([none, grad], axis=0).T

    def over_keys(index, _):
        rows_at = pl.ds(pl.multiple_of(index * block, block), block)
        for at in range(query_blocks):
            columns = slice(at * width, (at + 1) * width)

            def work(on_diagonal):
                hot = hot_ref[rows_at, :]
                keys = block_of(kv_ref, index, block, per_piece, KEYS)
                values = block_of(kv_ref, index, block, per_piece, VALUES)
                scores = jnp.dot(
                    jnp.concatenate([keys, hot], axis=1),
                    query_aug[:, columns],
                    preferred_element_type=F32,
                )
                if on_diagonal:
                    scores = causal(scores, block)
                probs = jnp.exp2(scores)
                grad_probs = jnp.dot(
                    jnp.concatenate([values, hot], axis=1),
                    grad_aug[:, columns],
                    preferred_element_type=F32,
                )
                grad_scores = (probs * grad_probs).astype(BF16)
                grad_values[rows_at, :] += jnp.dot(
                    probs.astype(BF16), grad_rows[columns, :], preferred_element_type=F32
                )
                grad_keys[rows_at, :] += jnp.dot(
                    grad_scores, query_rows[columns, :], preferred_element_type=F32
                )
                grad_query[:, columns] += jnp.dot(
                    key_turned[own, rows_at], grad_scores, preferred_element_type=F32
                )

            seen = seen_ref[at, index]
            pl.when(seen == 1)(functools.partial(work, False))
            pl.when(seen == 2)(functools.partial(work, True))
        return 0

    lax.fori_loop(0, key_blocks, over_keys, 0)
    for at in range(query_blocks):
        for r in range(rep):
            here = slice(at * width + r * block, at * width + (r + 1) * block)
            grad_query_ref[
                r * HEAD_SIZE : (r + 1) * HEAD_SIZE, at * block : (at + 1) * block
            ] = grad_query[:, here]

    @pl.when(group == pl.num_programs(0) - 1)
    def _():
        for piece in range(kv_ref.shape[0]):
            at = slice(piece * rows, (piece + 1) * rows)
            grad_kv_ref[piece, :, KEYS] = (grad_keys[at, :] * LN2).astype(BF16)
            grad_kv_ref[piece, :, VALUES] = grad_values[at, :].astype(BF16)


def attend_back(tree, seen, hot, query, mask, mixed, grad, lse, kv, rep, block):
    heads = query.shape[0]
    pieces, _, rows, _ = kv.shape
    groups = heads // (rep * HEAD_SIZE)
    keys = pieces * rows
    head = pl.BlockSpec((rep * HEAD_SIZE, rows), lambda g, *_: (g, 0))
    grid_spec = pltpu.PrefetchScalarGridSpec(
        num_scalar_prefetch=1,
        grid=(groups,),
        in_specs=[
            pl.BlockSpec((rep * HEAD_SIZE, rows), lambda g, *_: (g, tree)),
            pl.BlockSpec((16, rows), lambda g, *_: (0, 0)),
            head,
            head,
            pl.BlockSpec((1, rep, rows), lambda g, *_: (g, 0, 0)),
            pl.BlockSpec((pieces, 1, rows, 256), lambda g, *_: (0, 0, 0, 0)),
            pl.BlockSpec((keys + block, 128), lambda g, *_: (0, 0)),
        ],
        out_specs=[
            head,
            pl.BlockSpec((pieces, rows, 256), lambda g, *_: (0, 0, 0)),
        ],
        scratch_shapes=[
            pltpu.VMEM((256, rep * rows), BF16),
            pltpu.VMEM((256, rep * rows), BF16),
            pltpu.VMEM((rep * rows, 128), BF16),
            pltpu.VMEM((rep * rows, 128), BF16),
            pltpu.VMEM((128, keys), BF16),
            pltpu.VMEM((HEAD_SIZE, rep * rows), F32),
            pltpu.VMEM((keys, 128), F32),
            pltpu.VMEM((keys, 128), F32),
        ],
    )
    return pl.pallas_call(
        functools.partial(attend_back_kernel, block, rep, rows // block),
        grid_spec=grid_spec,
        out_shape=[
            jax.ShapeDtypeStruct((heads, rows), F32),
            jax.ShapeDtypeStruct((pieces, rows, 256), BF16),
        ],
        compiler_params=pltpu.CompilerParams(vmem_limit_bytes=56 * 2**20),
        cost_estimate=pl.CostEstimate(
            flops=60 * 10**9, bytes_accessed=20 * 2**20, transcendentals=0
        ),
        name="tree_attention_back",
    )(seen, query, mask, mixed, grad, lse, kv, hot)


def shards(
    layer_in,
    out_grad,
    parents,
    seg_len,
    attn_gain,
    w_query,
    key_weight,
    value_weight,
    w_out,
    ffn_gain,
    w_gate,
    w_up,
    w_down,
):
    trees, rows, width = layer_in.shape
    ring = Ring()
    chips = ring.count
    here, core = lax.axis_index("zy"), lax.axis_index("core")
    chip_rows = 2 * rows
    keys = chips * chip_rows
    groups = KEY_VALUE_HEADS // (2 * lax.axis_size("tp"))
    rep = QUERY_HEADS // KEY_VALUE_HEADS
    heads = groups * rep
    head_cols, kv_cols = heads * HEAD_SIZE, groups * HEAD_SIZE
    block = math.gcd(rows, 256)
    per_half = rows // block
    query_blocks, key_blocks = chip_rows // block, keys // block

    def column_piece(weight):
        keep, give = split_by_core(weight, 1)
        return by_core(keep, other_core(give), 0)

    def row_piece(weight):
        keep, give = split_by_core(weight, 0)
        return by_core(keep.T, other_core(give).T, 0)

    qkv_piece = jnp.concatenate(
        [column_piece(w_query), column_piece(key_weight), column_piece(value_weight)], axis=1
    )
    gains = jnp.stack([attn_gain, ffn_gain])
    gain_piece = by_core(gains, other_core(gains), 1)
    gain_all, _ = ring.gather(gain_piece)
    gain_all = jnp.transpose(gain_all, (1, 0, 2)).reshape(2, width).astype(F32)
    gain_a, gain_f = gain_all[0], gain_all[1]
    w_qkv, line = ring.gather(qkv_piece)
    w_qkv = w_qkv.reshape(width, head_cols + 2 * kv_cols)
    w_q, w_kv = w_qkv[:, :head_cols], w_qkv[:, head_cols:]
    out_piece = row_piece(w_out)
    gate_piece, up_piece, down_piece = column_piece(w_gate), column_piece(w_up), row_piece(w_down)
    w_o, line = ring.gather(out_piece, line)
    w_o = w_o.reshape(width, head_cols)

    def token_order(chip):
        first = (chip * 2 + core) * rows
        second = (chip * 2 + 1 - core) * rows
        steps = jnp.arange(rows, dtype=jnp.int32)
        return jnp.concatenate(
            [first[..., None] + steps, second[..., None] + steps], axis=-1
        ).reshape(-1)

    own_tokens = token_order(here)
    key_tokens = token_order(jnp.arange(chips, dtype=jnp.int32))
    own_block = own_tokens[::block] // block
    key_block = key_tokens[::block] // block
    diagonals = here * query_blocks + jnp.arange(query_blocks, dtype=jnp.int32)
    labels = jnp.arange(16, dtype=jnp.int32)
    tables, positions, masks, seens = [], [], [], []
    for tree in range(trees):
        reaches, starts_at, ends_at, before = tree_tables(parents[tree], seg_len[tree])
        seg_count = ends_at.shape[0]
        extra = 16 - seg_count
        reach16 = jnp.pad(reaches, ((0, extra), (0, extra)))
        starts16 = jnp.pad(starts_at, (0, extra))
        before16 = jnp.pad(before, (0, extra))
        ends16 = jnp.pad(ends_at, (0, extra), constant_values=2**30)
        own_seg = jnp.sum((own_tokens[:, None] >= ends_at[None, :]).astype(jnp.int32), axis=1)
        key_seg = jnp.sum((key_tokens[:, None] >= ends_at[None, :]).astype(jnp.int32), axis=1)
        member = own_seg[None, :] == labels[:, None]
        positions.append(
            own_tokens + jnp.sum(jnp.where(member, (before16 - starts16)[:, None], 0), axis=0)
        )
        seen_by = jnp.sum(
            jnp.where(member[:, None, :], reach16.astype(jnp.int32)[:, :, None], 0), axis=0
        )
        masks.append(jnp.where(seen_by > 0, 0.0, NEG).astype(BF16))
        lanes = jnp.arange(128, dtype=jnp.int32)
        key_seg_all = jnp.concatenate([key_seg, jnp.full((block,), seg_count, jnp.int32)])
        hot = (lanes[None, :] == key_seg_all[:, None]) | ((lanes >= 16) & (lanes < 19))[None, :]
        hot = hot.astype(BF16)

        def holds(blocks):
            low = blocks[:, None] * block
            return ((starts_at[None, :] < low + block) & (ends_at[None, :] > low)).astype(F32)

        linked = dot(dot(holds(own_block), reaches.astype(F32)), holds(key_block), 1, 1) > 0.5
        seen = linked & (key_block[None, :] < own_block[:, None])
        rank = jnp.cumsum(seen.astype(jnp.int32), axis=1) - 1
        slots = jnp.arange(key_blocks + 2, dtype=jnp.int32)
        index = jnp.arange(key_blocks, dtype=jnp.int32)
        chosen = seen[:, :, None] & (rank[:, :, None] == slots[None, None, :])
        lists = key_blocks + jnp.sum(
            jnp.where(chosen, index[None, :, None] - key_blocks, 0), axis=1
        )
        counts = jnp.sum(seen.astype(jnp.int32), axis=1)
        tables.append((counts, lists, diagonals, hot))
        on_diagonal = index[None, :] == diagonals[:, None]
        seens.append(jnp.where(on_diagonal, 2, seen.astype(jnp.int32)))
    position = jnp.concatenate(positions)
    angles = rope_angles(position, HEAD_SIZE)
    cosine, sine = jnp.cos(angles), jnp.sin(angles)

    rows_in = layer_in.astype(F32)
    scale_a = row_scale_of(rows_in)
    normed_a = rows_in * scale_a

    def both_cores(own):
        return jnp.concatenate([own, other_core(own)], axis=1)

    inner_a = both_cores((normed_a * gain_a).astype(BF16)).reshape(trees * chip_rows, width)
    grad_low = both_cores(out_grad).reshape(trees * chip_rows, width)

    def by_head(value):
        return value.reshape(-1, 2, HEAD_SIZE // 2, value.shape[-1])

    def query_turn(value, cosine, sine):
        value = by_head(value)
        first, second = turn(value[:, 0], value[:, 1], cosine[None], sine[None])
        return jnp.stack([first, second], axis=1).reshape(-1, value.shape[-1])

    query = dot(w_q, inner_a, 0, 1)
    query = (query_turn(query, cosine, sine) * (HEAD_SIZE**-0.5 / LN2)).astype(BF16)
    key_value = dot(inner_a, w_kv)
    key_pre = key_value[:, :kv_cols].reshape(-1, groups, 2, HEAD_SIZE // 2)
    cosine_rows, sine_rows = cosine.T[:, None, :], sine.T[:, None, :]
    first, second = turn(key_pre[:, :, 0], key_pre[:, :, 1], cosine_rows, sine_rows)
    key_low = jnp.stack([first, second], axis=2).reshape(-1, kv_cols)
    key_value = jnp.concatenate([key_low, key_value[:, kv_cols:]], axis=1).astype(BF16)
    key_value = key_value.reshape(trees, 1, chip_rows, 2 * kv_cols)

    kvs = []
    for tree in range(trees):
        kv, line = ring.gather(key_value[tree].reshape(chip_rows, 2 * kv_cols), line)
        kvs.append(kv.reshape(chips, 1, chip_rows, 2 * kv_cols))

    w_g, line = ring.gather(gate_piece, line)
    w_u, line = ring.gather(up_piece, line)
    w_d, line = ring.gather(down_piece, line)
    w_g, w_u, w_d = (w.reshape(width, -1) for w in (w_g, w_u, w_d))

    def sum_parts(part):
        own = part[:rows] + other_core(part[rows:].astype(BF16)).astype(F32)
        low = own.astype(BF16)
        return low.astype(F32) + other_half(low).astype(F32), own

    mixes, lses, middles, inners, normeds_f, scales_f = [], [], [], [], [], []
    for tree in range(trees):
        mixed, lse = attend(tree, tables[tree], query, masks[tree], kvs[tree], rep, block)
        mixes.append(mixed)
        lses.append(lse)
        middle = rows_in[tree] + sum_parts(dot(mixed, w_o, 0, 1))[0]
        scale_f = row_scale_of(middle)
        normed_f = middle * scale_f
        inner = (normed_f * gain_f).astype(BF16)
        inners += [inner, other_core(inner)]
        middles.append(middle)
        scales_f.append(scale_f)
        normeds_f.append(normed_f)
    inner_f = jnp.concatenate(inners, axis=0)

    gate = dot(inner_f, w_g)
    up = dot(inner_f, w_u)
    sigmoid = jax.nn.sigmoid(gate)
    activated = gate * sigmoid
    hidden = (activated * up).astype(BF16)
    outputs = []
    for tree in range(trees):
        span = slice(tree * chip_rows, (tree + 1) * chip_rows)
        outputs.append((middles[tree] + sum_parts(dot(hidden[span], w_d, 1, 1))[0]).astype(BF16))

    def pieces(term):
        return term.astype(BF16).reshape(chips, width // chips, -1)

    grad_hidden = dot(grad_low, w_d)
    down_sum, line = ring.reduce(pieces(dot(grad_low, hidden, 0, 0)), line)
    grad_gate = (grad_hidden * up * sigmoid * (1.0 + gate * (1.0 - sigmoid))).astype(BF16)
    grad_up = (grad_hidden * activated).astype(BF16)
    grads_middle, grads_low, gain_f_terms = [], [], []
    for tree in range(trees):
        span = slice(tree * chip_rows, (tree + 1) * chip_rows)
        part = dot(grad_gate[span], w_g, 1, 1) + dot(grad_up[span], w_u, 1, 1)
        grad_inner, _ = sum_parts(part)
        gain_f_terms.append(jnp.sum(grad_inner * normeds_f[tree], axis=0))
        grad_middle = out_grad[tree].astype(F32) + norm_back(
            grad_inner * gain_f, normeds_f[tree], scales_f[tree]
        )
        low = grad_middle.astype(BF16)
        grads_middle.append(grad_middle)
        grads_low += [low, other_core(low)]
    gate_sum, line = ring.reduce(pieces(dot(inner_f, grad_gate, 0, 0)), line)
    up_sum, line = ring.reduce(pieces(dot(inner_f, grad_up, 0, 0)), line)

    grad_queries, kv_sums, line_kv = [], [], line
    for tree in range(trees):
        low = jnp.concatenate(grads_low[2 * tree : 2 * tree + 2], axis=0)
        grad_mixed = dot(w_o, low, 0, 1).astype(BF16)
        grad_query, grad_kv = attend_back(
            tree,
            seens[tree],
            tables[tree][3],
            query,
            masks[tree],
            mixes[tree],
            grad_mixed,
            lses[tree],
            kvs[tree],
            rep,
            block,
        )
        grad_queries.append(grad_query)
        kv_sum, line_kv = ring.reduce(grad_kv, line_kv)
        kv_sums.append(kv_sum)
    grad_mid_low = jnp.concatenate(grads_low, axis=0)
    mixed_all = jnp.concatenate(mixes, axis=1)
    out_sum, _ = ring.reduce(pieces(dot(grad_mid_low, mixed_all, 0, 1)), line)

    grads_q, grads_kv, in_grads, gain_a_terms = [], [], [], []
    for tree in range(trees):
        span = slice(tree * chip_rows, (tree + 1) * chip_rows)
        grad_q = query_turn(grad_queries[tree], cosine[:, span], -sine[:, span])
        grad_q = (grad_q * HEAD_SIZE**-0.5).astype(BF16)
        grad_k = kv_sums[tree][:, :kv_cols].reshape(-1, groups, 2, HEAD_SIZE // 2)
        first, second = turn(
            grad_k[:, :, 0], grad_k[:, :, 1], cosine_rows[span], -sine_rows[span]
        )
        grad_k = jnp.stack([first, second], axis=2).reshape(-1, kv_cols)
        grad_kv = jnp.concatenate([grad_k, kv_sums[tree][:, kv_cols:]], axis=1).astype(BF16)
        grads_q.append(grad_q)
        grads_kv.append(grad_kv)
        part = dot(grad_q, w_q, 0, 1) + dot(grad_kv, w_kv, 1, 1)
        grad_inner, core_sum = sum_parts(part)
        gain_a_terms.append(jnp.sum(core_sum * normed_a[tree], axis=0))
        in_grads.append(
            grads_middle[tree] + norm_back(grad_inner * gain_a, normed_a[tree], scale_a[tree])
        )
    term_q = dot(inner_a, jnp.concatenate(grads_q, axis=1), 0, 1)
    term_kv = dot(inner_a, jnp.concatenate(grads_kv, axis=0), 0, 0)
    qkv_sum, _ = ring.reduce(pieces(jnp.concatenate([term_q, term_kv], axis=1)), line_kv)

    def gain_sum(terms):
        keep, give = split_by_core(sum(terms).reshape(chips, 2, width // chips // 2), 1)
        both = (keep + other_core(give)).reshape(chips, 2, -1)
        total = both_ways(ring, both)
        return total.reshape(-1)

    gain_f_grad = gain_sum(gain_f_terms)
    gain_a_grad = gain_sum(gain_a_terms)
    gain_a_grad = gain_a_grad + other_half(gain_a_grad)

    def column_grad(total):
        keep, give = split_by_core(total, 0)
        return by_core(keep, other_core(give), 1)

    def row_grad(total):
        keep, give = split_by_core(total, 0)
        return by_core(keep, other_core(give), 1).T

    return (
        jnp.stack(outputs),
        jnp.stack(in_grads),
        gain_a_grad,
        column_grad(qkv_sum[:, :head_cols]),
        column_grad(qkv_sum[:, head_cols : head_cols + kv_cols]),
        column_grad(qkv_sum[:, head_cols + kv_cols :]),
        row_grad(out_sum),
        gain_f_grad,
        column_grad(gate_sum),
        column_grad(up_sum),
        row_grad(down_sum),
    )


def both_ways(ring, terms):
    half = ring.count // 2

    def term(offset):
        return lax.dynamic_index_in_dim(terms, ring.chip(offset), 0, keepdims=False)

    rightward, leftward = ring.go_right(term(half)), None
    for step in range(half - 1, 0, -1):
        rightward = ring.go_right(rightward + term(step))
        leftward = ring.go_left(term(-step) if leftward is None else leftward + term(-step))
    total = term(0) + rightward
    return total if leftward is None else total + leftward


def solution(mesh):
    devices = mesh.devices
    mesh = Mesh(devices.reshape(-1, 2, devices.shape[1]), ("zy", "core", "tp"))
    fsdp = ("zy", "core")
    specs = (
        P(fsdp),
        P(fsdp, "tp"),
        P(fsdp, "tp"),
        P(fsdp, "tp"),
        P("tp", fsdp),
        P(fsdp),
        P(fsdp, "tp"),
        P(fsdp, "tp"),
        P("tp", fsdp),
    )
    tokens = P(None, fsdp, None)
    return jax.shard_map(
        shards,
        mesh=mesh,
        in_specs=(tokens, tokens, P(), P()) + specs,
        out_specs=(tokens, tokens) + specs,
        check_vma=False,
    )
```

time: 4190 us -> 1750 us (0.42)
  waiting for transfers between devices: 2720 us -> 602 us
  starting transfers between devices: 2.36 us -> 324 us
  blocking collectives: 301 us -> 0 us
  matrix products: 574 us -> 324 us
  local copies, waits for them, and re-layouts: 409 us -> 200 us
  Pallas kernels: 0 us -> 98.4 us
  other arithmetic: 114 us -> 192 us
  loops' own time: 45.7 us -> 0 us
    reduce_scatter x11 -> x0, waiting for transfers between devices: 1990 us -> none  [the longest x2 517 us: shards(): lax.psum_scatter(key_terms.reshape(tree_row_block, query_groups * head_di...]
    ppermute x0 -> x174, waiting for transfers between devices: none -> 602 us  [the longest x68 319 us: go_right(): return lax.ppermute(value, 'zy', self.right)]
    all_gather x11 -> x0, waiting for transfers between devices: 494 us -> none  [the longest x1 119 us: shards(): lax.all_gather(w_gate, 'fsdp', axis=0, tiled=True)]
    ppermute x0 -> x174, starting transfers between devices: none -> 324 us  [the longest x68 237 us: go_right(): return lax.ppermute(value, 'zy', self.right)]
    dot_general x122 -> x27, matrix products: 574 us -> 324 us  [dot(): lax.dot_general(left, right, (((left_dim,), (right_dim,)), ((), ())), pre...]
    all_gather x2 -> x0, blocking collectives: 238 us -> none  [the longest x1 215 us: shards(): lax.all_gather(ffn_gain, 'fsdp', axis=0, tiled=True)]
    psum x3 -> x0, waiting for transfers between devices: 222 us -> none  [the longest x1 106 us: shards(): lax.psum(unit_terms.astype(jnp.bfloat16), 'tp').astype(jnp.float32)]
    dynamic_update_slice x96 -> x71, local copies, waits for them, and re-layouts: 202 us -> 103 us  [put(): lax.dynamic_update_slice(whole, part[None], (self.chip(offset), row) + ze...]
  transfers between devices with their start and end apart: 25 -> 174, of which waited for: 23 -> 82; matrix products, arithmetic and copies ran while one was open for 18% -> 32% of each run, Pallas kernels for 0% -> 6%
where the time goes in v1:
time: 1750 us; the launch traced here: 1740 us
  waiting for transfers between devices  602 us (34%)
  starting transfers between devices  324 us (19%)
  matrix products  324 us (19%)
  local copies, waits for them, and re-layouts  200 us (11%)
  other arithmetic  192 us (11%)
  Pallas kernels  98.4 us (6%)
    dot_general x27, matrix products, dot(): lax.dot_general(left, right, (((left_dim,), (right_dim,)), ((), ())), pre...  324 us
    ppermute x68, waiting for transfers between devices, go_right(): return lax.ppermute(value, 'zy', self.right)  319 us
    ppermute x68, starting transfers between devices, go_right(): return lax.ppermute(value, 'zy', self.right)  237 us
    ppermute x9, waiting for transfers between devices, other_half(): return lax.ppermute(value, 'tp', SWAP)  145 us
    ppermute x66, waiting for transfers between devices, go_left(): return lax.ppermute(value, 'zy', self.left)  135 us
    dynamic_update_slice x71, local copies, waits for them, and re-layouts, put(): lax.dynamic_update_slice(whole, part[None], (self.chip(offset), row) + ze...  103 us
    ppermute x66, starting transfers between devices, go_left(): return lax.ppermute(value, 'zy', self.left)  69.5 us
    pallas_call x2, Pallas kernels, attend_back(): pl.pallas_call(functools.partial(attend_back_kernel, block, rep, rows //...  64.9 us
  transfers between devices with their start and end apart: 174, of which 82 were waited for; matrix products, arithmetic and copies ran while one was open for 32% of the time, Pallas kernels for 6%

profile of v1, /device:TPU:0, one launch (start us, length us, event | category | flops | bytes accessed | tf_op | source)
XLA Modules:
  0.0 1743.7 jit_solution(18405252807880685163)
XLA Ops:
  131.7 27.2 %dynamic_update_slice.242 = bf16[8,256,768]{1,0,2:T(8,128)(2,1)} dynamic-update-slice(bf16[8,256,768]{1,0,2:T(8,128)(2,1)} %copy.82, bf16[1,128,768]{1,0,2:T(2,128)(2,1)} %copy.83, s32[]{:T(128)S(6)} %select_n.645, s32[]{:T(128)} %constant.339.clone.1, s32[]{:T(128)} %constant.322.clone.1) | dynamic-update-slice | bytes 393220 | tf_op jit(solution)/shard_map/dynamic_update_slice | solution.py:107
  306.3 17.6 %collective-permute-start.43 = (bf16[1024,256]{1,0:T(8,128)(2,1)S(1)}, bf16[1024,256]{1,0:T(8,128)(2,1)S(1)}, u32[]{:S(2)}, u32[]{:S(2)}) collective-permute-start(bf16[1024,256]{1,0:T(8,128)(2,1)S(1)} %collective-permute-done.41), channel_id=1, source_target_pairs={{0,8},{8,16},{16,24},{24,28},{28,20},{20,12},{12,4},{4,0},{1,9},{9... | collective-permute-start | bytes 1572872 | tf_op jit(solution)/shard_map/ppermute | solution.py:93
  330.7 17.0 collective-permute-start.45
  369.4 22.4 %collective-permute-done.47 = bf16[512,256]{1,0:T(8,128)(2,1)S(1)} collective-permute-done((bf16[512,256]{1,0:T(8,128)(2,1)S(1)}, bf16[512,256]{1,0:T(8,128)(2,1)S(1)}, u32[]{:S(2)}, u32[]{:S(2)}) %collective-permute-start.47) | collective-permute-done | bytes 262176 | tf_op jit(solution)/shard_map/ppermute | solution.py:93
  415.0 17.2 collective-permute-start.55
  477.0 17.5 %collective-permute-done.57 = bf16[256,2048]{1,0:T(8,128)(2,1)S(1)} collective-permute-done((bf16[256,2048]{1,0:T(8,128)(2,1)S(1)}, bf16[256,2048]{1,0:T(8,128)(2,1)S(1)}, u32[]{:S(2)}, u32[]{:S(2)}) %collective-permute-start.57) | collective-permute-done | bytes 1048608 | tf_op jit(solution)/shard_map/ppermute | solution.py:93
  511.9 24.3 %collective-permute-done.59 = bf16[128,2048]{1,0:T(8,128)(2,1)} collective-permute-done((bf16[128,2048]{1,0:T(8,128)(2,1)}, bf16[128,2048]{1,0:T(8,128)(2,1)}, u32[]{:S(2)}, u32[]{:S(2)}) %collective-permute-start.59) | collective-permute-done | bytes 524320 | tf_op jit(solution)/shard_map/ppermute | solution.py:93
  606.1 21.6 %collective-permute-done.68 = bf16[128,2048]{1,0:T(8,128)(2,1)S(1)} collective-permute-done((bf16[128,2048]{1,0:T(8,128)(2,1)S(1)}, bf16[128,2048]{1,0:T(8,128)(2,1)S(1)}, u32[]{:S(2)}, u32[]{:S(2)}) %collective-permute-start.68) | collective-permute-done | bytes 524320 | tf_op jit(solution)/shard_map/ppermute | solution.py:93
  645.1 27.5 %fusion.263 = f32[2048,2048]{1,0:T(8,128)} fusion(bf16[2048,2048]{1,0:T(8,128)(2,1)} %bitcast.94, bf16[512,2048]{1,0:T(8,128)(2,1)} %copy-done.120, bf16[512,2048]{1,0:T(8,128)(2,1)} %copy-done.62, bf16[512,2048]{1,0:T(8,128)(2,1)} %copy-done.118, bf16[512,2048]{1,0:T(8,128)(2,1)S(1)} %get-tuple-element.254), kind=kOutput, calls=%fused_computation.661 | convolution fusion | flops 17213423616 | bytes 33554432 | tf_op jit(solution)/shard_map/dot_general | solution.py:27
  706.7 24.4 %fusion.284 = f32[2048,2048]{1,0:T(8,128)} fusion(bf16[2048,2048]{1,0:T(8,128)(2,1)} %bitcast.636, bf16[2048,2048]{1,0:T(8,128)(2,1)} %bitcast.106), kind=kOutput, calls=%fused_computation.672 | convolution fusion | flops 17179869184 | bytes 33554432 | tf_op jit(solution)/shard_map/dot_general | solution.py:27
  731.1 37.4 %multiply_convert_fusion.1 = (bf16[2048,2048]{1,0:T(8,128)(2,1)}, bf16[2048,2048]{1,0:T(8,128)(2,1)}, bf16[2048,2048]{1,0:T(8,128)(2,1)}) fusion(f32[2048,2048]{1,0:T(8,128)} %fusion.284, f32[2048,2048]{1,0:T(8,128)} %fusion.263, bf16[2048,2048]{1,0:T(8,128)(2,1)} %bitcast.654, bf16[512,2048]{1,0:T(8,128)(2,1)} %copy-done.120, ...), kind=kOutput, calls=%fused_computation.1 | convolution fusion | flops 17276338176 | bytes 75497472 | tf_op jit(solution)/shard_map/dot_general | solution.py:27
  797.0 20.9 %convolution_convert_fusion = bf16[2048,2048]{1,0:T(8,128)(2,1)S(1)} fusion(bf16[2048,2048]{1,0:T(8,128)(2,1)S(1)} %bitcast.639, bf16[2048,2048]{1,0:T(8,128)(2,1)} %get-tuple-element.112), kind=kOutput, calls=%fused_computation.19 | convolution fusion | flops 17184063488 | bytes 25165824 | tf_op jit(solution)/shard_map/dot_general | solution.py:27
  817.9 17.7 %fusion.24 = f32[1024,2048]{1,0:T(8,128)} fusion(bf16[2048,2048]{1,0:T(8,128)(2,1)} %bitcast.106, bf16[2048,2048]{1,0:T(8,128)(2,1)} %get-tuple-element.112), kind=kOutput, calls=%fused_computation.53 | convolution fusion | flops 8589934592 | bytes 20971520 | tf_op jit(solution)/shard_map/dot_general | solution.py:27
  886.0 21.3 %convolution_convert_fusion.1 = bf16[2048,2048]{1,0:T(8,128)(2,1)S(1)} fusion(bf16[2048,2048]{1,0:T(8,128)(2,1)} %get-tuple-element.110, bf16[512,2048]{1,0:T(8,128)(2,1)S(1)} %copy-done.121, bf16[512,2048]{1,0:T(8,128)(2,1)S(1)} %copy-done.63, bf16[512,2048]{1,0:T(8,128)(2,1)S(1)} %copy-done.119, bf16[512,2048]{1,0:T(8,128)(2,1)S(1)} %get-tuple-element.254), kind=kOutput, calls=%fused_computation.20 | convolution fusion | flops 17217617920 | bytes 25165824 | tf_op jit(solution)/shard_map/dot_general | solution.py:27
  913.4 23.7 %convolution_convert_fusion.2 = bf16[2048,2048]{1,0:T(8,128)(2,1)} fusion(bf16[2048,2048]{1,0:T(8,128)(2,1)} %get-tuple-element.111, bf16[512,2048]{1,0:T(8,128)(2,1)} %copy-done.120, bf16[512,2048]{1,0:T(8,128)(2,1)S(1)} %copy-done.63, bf16[512,2048]{1,0:T(8,128)(2,1)} %copy-done.118, bf16[512,2048]{1,0:T(8,128)(2,1)S(1)} %get-tuple-element.254), kind=kOutput, calls=%fused_computation.21 | convolution fusion | flops 17217617920 | bytes 25165824 | tf_op jit(solution)/shard_map/dot_general | solution.py:27
  993.3 43.3 %collective-permute-done.85 = bf16[512,2048]{1,0:T(8,128)(2,1)S(1)} collective-permute-done((bf16[512,2048]{1,0:T(8,128)(2,1)S(1)}, bf16[512,2048]{1,0:T(8,128)(2,1)S(1)}, u32[]{:S(2)}, u32[]{:S(2)}) %collective-permute-start.85) | collective-permute-done | bytes 2097184 | tf_op jit(solution)/shard_map/ppermute | solution.py:154
  1075.7 18.3 %collective-permute-done.101 = bf16[256,2048]{1,0:T(8,128)(2,1)S(1)} collective-permute-done((bf16[256,2048]{1,0:T(8,128)(2,1)S(1)}, bf16[256,2048]{1,0:T(8,128)(2,1)S(1)}, u32[]{:S(2)}, u32[]{:S(2)}) %collective-permute-start.101) | collective-permute-done | bytes 1048608 | tf_op jit(solution)/shard_map/ppermute | solution.py:96
  1165.0 32.5 %tree_attention_back.3 = (f32[512,1024]{1,0:T(8,128)}, bf16[8,1024,256]{2,1,0:T(8,128)(2,1)}) custom-call(s32[4,32]{1,0:T(4,128)} %get-tuple-element.273.seen_ref, bf16[512,2048]{1,0:T(8,128)(2,1)} %bitcast.612, bf16[16,1024]{1,0:T(8,128)(2,1)} %copy-done.4, bf16[512,1024]{1,0:T(8,128)(2,1)} %copy-done.7, bf16[512,1024]{1,0:T(8,128)(2,1)} %fusion.81.grad_ref, ...), custom_call_target="tpu_custom_call" | custom-call | flops 60000002048 | bytes 20971520 | tf_op jit(solution)/shard_map/tree_attention_back/pallas_call | solution.py:443
  1203.9 24.5 %collective-permute-start.104 = (bf16[256,2048]{1,0:T(8,128)(2,1)S(1)}, bf16[256,2048]{1,0:T(8,128)(2,1)S(1)}, u32[]{:S(2)}, u32[]{:S(2)}) collective-permute-start(bf16[256,2048]{1,0:T(8,128)(2,1)S(1)} %pad_maximum_fusion.15), channel_id=1, source_target_pairs={{0,8},{8,16},{16,24},{24,28},{28,20},{20,12},{12,4},{4,0},{1,9},{9... | collective-permute-start | bytes 3145736 | tf_op jit(solution)/shard_map/ppermute | solution.py:93
  1230.1 32.4 %tree_attention_back.2 = (f32[512,1024]{1,0:T(8,128)}, bf16[8,1024,256]{2,1,0:T(8,128)(2,1)}) custom-call(s32[4,32]{1,0:T(4,128)} %get-tuple-element.272.seen_ref, bf16[512,2048]{1,0:T(8,128)(2,1)} %bitcast.613, bf16[16,1024]{1,0:T(8,128)(2,1)} %copy-done.3, bf16[512,1024]{1,0:T(8,128)(2,1)} %copy-done.5, bf16[512,1024]{1,0:T(8,128)(2,1)} %fusion.84.grad_ref, ...), custom_call_target="tpu_custom_call" | custom-call | flops 60000002048 | bytes 20971520 | tf_op jit(solution)/shard_map/tree_attention_back/pallas_call | solution.py:443
  1276.1 45.0 %collective-permute-start.105 = (bf16[256,2048]{1,0:T(8,128)(2,1)S(1)}, bf16[256,2048]{1,0:T(8,128)(2,1)S(1)}, u32[]{:S(2)}, u32[]{:S(2)}) collective-permute-start(bf16[256,2048]{1,0:T(8,128)(2,1)S(1)} %get-tuple-element.114), channel_id=1, source_target_pairs={{0,8},{8,16},{16,24},{24,28},{28,20},{20,12},{12,4},{4,0},{1,9},{9... | collective-permute-start | bytes 3145736 | tf_op jit(solution)/shard_map/ppermute | solution.py:93
  1339.4 34.1 %collective-permute-start.106 = (bf16[256,2048]{1,0:T(8,128)(2,1)S(1)}, bf16[256,2048]{1,0:T(8,128)(2,1)S(1)}, u32[]{:S(2)}, u32[]{:S(2)}) collective-permute-start(bf16[256,2048]{1,0:T(8,128)(2,1)S(1)} %fusion.71), channel_id=1, source_target_pairs={{0,8},{8,16},{16,24},{24,28},{28,20},{20,12},{12,4},{4,0},{1,9},{9... | collective-permute-start | bytes 3145736 | tf_op jit(solution)/shard_map/ppermute | solution.py:93
  1594.1 59.1 %collective-permute-done.120 = bf16[512,2048]{1,0:T(8,128)(2,1)} collective-permute-done((bf16[512,2048]{1,0:T(8,128)(2,1)}, bf16[512,2048]{1,0:T(8,128)(2,1)}, u32[]{:S(2)}, u32[]{:S(2)}) %collective-permute-start.120) | collective-permute-done | bytes 2097184 | tf_op jit(solution)/shard_map/ppermute | solution.py:154
  1653.2 43.1 %collective-permute-done.133 = bf16[512,2048]{1,0:T(8,128)(2,1)} collective-permute-done((bf16[512,2048]{1,0:T(8,128)(2,1)S(1)}, bf16[512,2048]{1,0:T(8,128)(2,1)}, u32[]{:S(2)}, u32[]{:S(2)}) %collective-permute-start.133) | collective-permute-done | bytes 2097184 | tf_op jit(solution)/shard_map/ppermute | solution.py:154
  (984 shorter events, 1070.2 us)
Async XLA Ops:
  2.0 70.3 %collective-permute-start.1 = (bf16[128,128]{1,0:T(8,128)(2,1)}, bf16[128,128]{1,0:T(8,128)(2,1)}, u32[]{:S(2)}, u32[]{:S(2)}) collective-permute-start(bf16[128,128]{1,0:T(8,128)(2,1)} %constant_dynamic-slice_fusion.35), channel_id=1, source_target_pairs={{0,2},{2,0},{1,3},{3,1},{4,6},{6,4},{5,7},{7,5},{8,10},{10,8},{9,1... | collective-permute-start | bytes 98312 | tf_op jit(solution)/shard_map/ppermute | solution.py:150
  3.2 70.5 %collective-permute-start.2 = (bf16[128,128]{1,0:T(8,128)(2,1)S(1)}, bf16[128,128]{1,0:T(8,128)(2,1)}, u32[]{:S(2)}, u32[]{:S(2)}) collective-permute-start(bf16[128,128]{1,0:T(8,128)(2,1)S(1)} %constant_dynamic-slice_fusion.33), channel_id=1, source_target_pairs={{0,2},{2,0},{1,3},{3,1},{4,6},{6,4},{5,7},{7,5},{8,10},{10,8},{9,1... | collective-permute-start | bytes 98312 | tf_op jit(solution)/shard_map/ppermute | solution.py:150
  4.9 69.9 %collective-permute-start = (bf16[128,512]{1,0:T(8,128)(2,1)}, bf16[128,512]{1,0:T(8,128)(2,1)}, u32[]{:S(2)}, u32[]{:S(2)}) collective-permute-start(bf16[128,512]{1,0:T(8,128)(2,1)} %constant_dynamic-slice_fusion.37), channel_id=1, source_target_pairs={{0,2},{2,0},{1,3},{3,1},{4,6},{6,4},{5,7},{7,5},{8,10},{10,8},{9,1... | collective-permute-start | bytes 393224 | tf_op jit(solution)/shard_map/ppermute | solution.py:150
  87.2 99.1 %collective-permute-start.83 = (bf16[2,512,2048]{2,1,0:T(8,128)(2,1)}, bf16[2,512,2048]{2,1,0:T(8,128)(2,1)}, u32[]{:S(2)}, u32[]{:S(2)}) collective-permute-start(bf16[2,512,2048]{2,1,0:T(8,128)(2,1)} %param.14), channel_id=1, source_target_pairs={{0,2},{2,0},{1,3},{3,1},{4,6},{6,4},{5,7},{7,5},{8,10},{10,8},{9,1... | collective-permute-start | bytes 12582920 | tf_op jit(solution)/shard_map/ppermute | solution.py:150
  88.5 106.2 %collective-permute-start.20 = (bf16[2,512,2048]{2,1,0:T(8,128)(2,1)}, bf16[2,512,2048]{2,1,0:T(8,128)(2,1)}, u32[]{:S(2)}, u32[]{:S(2)}) collective-permute-start(bf16[2,512,2048]{2,1,0:T(8,128)(2,1)} %get-tuple-element.144), channel_id=1, source_target_pairs={{0,2},{2,0},{1,3},{3,1},{4,6},{6,4},{5,7},{7,5},{8,10},{10,8},{9,1... | collective-permute-start | bytes 12582920 | tf_op jit(solution)/shard_map/ppermute | solution.py:150
  329.6 102.5 %collective-permute-start.38 = (bf16[512,2048]{1,0:T(8,128)(2,1)}, bf16[512,2048]{1,0:T(8,128)(2,1)}, u32[]{:S(2)}, u32[]{:S(2)}) collective-permute-start(bf16[512,2048]{1,0:T(8,128)(2,1)} %slice.891), channel_id=1, source_target_pairs={{0,2},{2,0},{1,3},{3,1},{4,6},{6,4},{5,7},{7,5},{8,10},{10,8},{9,1... | collective-permute-start | bytes 6291464 | tf_op jit(solution)/shard_map/ppermute | solution.py:150
  363.6 68.6 %collective-permute-start.54 = (bf16[256,2048]{1,0:T(8,128)(2,1)S(1)}, bf16[256,2048]{1,0:T(8,128)(2,1)}, u32[]{:S(2)}, u32[]{:S(2)}) collective-permute-start(bf16[256,2048]{1,0:T(8,128)(2,1)S(1)} %copy-done.47), channel_id=1, source_target_pairs={{8,0},{16,8},{24,16},{28,24},{20,28},{12,20},{4,12},{0,4},{9,1},{1... | collective-permute-start | bytes 3145736 | tf_op jit(solution)/shard_map/ppermute | solution.py:96
  435.8 119.9 %collective-permute-start.39 = (bf16[512,2048]{1,0:T(8,128)(2,1)S(1)}, bf16[512,2048]{1,0:T(8,128)(2,1)S(1)}, u32[]{:S(2)}, u32[]{:S(2)}) collective-permute-start(bf16[512,2048]{1,0:T(8,128)(2,1)S(1)} %fusion.31), channel_id=1, source_target_pairs={{0,1},{1,0},{2,3},{3,2},{4,5},{5,4},{6,7},{7,6},{8,9},{9,8},{10,11... | collective-permute-start | bytes 6291464 | tf_op jit(solution)/shard_map/ppermute | solution.py:154
  475.5 80.2 %collective-permute-start.50 = (bf16[512,2048]{1,0:T(8,128)(2,1)S(1)}, bf16[512,2048]{1,0:T(8,128)(2,1)S(1)}, u32[]{:S(2)}, u32[]{:S(2)}) collective-permute-start(bf16[512,2048]{1,0:T(8,128)(2,1)S(1)} %fusion.29), channel_id=1, source_target_pairs={{0,1},{1,0},{2,3},{3,2},{4,5},{5,4},{6,7},{7,6},{8,9},{9,8},{10,11... | collective-permute-start | bytes 6291464 | tf_op jit(solution)/shard_map/ppermute | solution.py:154
  575.2 67.2 %collective-permute-start.40 = (bf16[512,2048]{1,0:T(8,128)(2,1)S(1)}, bf16[512,2048]{1,0:T(8,128)(2,1)S(1)}, u32[]{:S(2)}, u32[]{:S(2)}) collective-permute-start(bf16[512,2048]{1,0:T(8,128)(2,1)S(1)} %get-tuple-element.254), channel_id=1, source_target_pairs={{0,2},{2,0},{1,3},{3,1},{4,6},{6,4},{5,7},{7,5},{8,10},{10,8},{9,1... | collective-permute-start | bytes 6291464 | tf_op jit(solution)/shard_map/ppermute | solution.py:150
  575.3 67.2 %collective-permute-start.51 = (bf16[512,2048]{1,0:T(8,128)(2,1)S(1)}, bf16[512,2048]{1,0:T(8,128)(2,1)S(1)}, u32[]{:S(2)}, u32[]{:S(2)}) collective-permute-start(bf16[512,2048]{1,0:T(8,128)(2,1)S(1)} %get-tuple-element.255), channel_id=1, source_target_pairs={{0,2},{2,0},{1,3},{3,1},{4,6},{6,4},{5,7},{7,5},{8,10},{10,8},{9,1... | collective-permute-start | bytes 6291464 | tf_op jit(solution)/shard_map/ppermute | solution.py:150
  858.6 82.0 %collective-permute-start.121 = (bf16[512,2048]{1,0:T(8,128)(2,1)}, bf16[512,2048]{1,0:T(8,128)(2,1)}, u32[]{:S(2)}, u32[]{:S(2)}) collective-permute-start(bf16[512,2048]{1,0:T(8,128)(2,1)} %slice.885), channel_id=1, source_target_pairs={{0,2},{2,0},{1,3},{3,1},{4,6},{6,4},{5,7},{7,5},{8,10},{10,8},{9,1... | collective-permute-start | bytes 6291464 | tf_op jit(solution)/shard_map/ppermute | solution.py:150
  878.3 66.2 %collective-permute-start.84 = (bf16[512,2048]{1,0:T(8,128)(2,1)}, bf16[512,2048]{1,0:T(8,128)(2,1)}, u32[]{:S(2)}, u32[]{:S(2)}) collective-permute-start(bf16[512,2048]{1,0:T(8,128)(2,1)} %slice.887), channel_id=1, source_target_pairs={{0,2},{2,0},{1,3},{3,1},{4,6},{6,4},{5,7},{7,5},{8,10},{10,8},{9,1... | collective-permute-start | bytes 6291464 | tf_op jit(solution)/shard_map/ppermute | solution.py:150
  882.9 101.4 %collective-permute-start.81 = (bf16[512,2048]{1,0:T(8,128)(2,1)}, bf16[512,2048]{1,0:T(8,128)(2,1)}, u32[]{:S(2)}, u32[]{:S(2)}) collective-permute-start(bf16[512,2048]{1,0:T(8,128)(2,1)} %slice.888), channel_id=1, source_target_pairs={{0,2},{2,0},{1,3},{3,1},{4,6},{6,4},{5,7},{7,5},{8,10},{10,8},{9,1... | collective-permute-start | bytes 6291464 | tf_op jit(solution)/shard_map/ppermute | solution.py:150
  948.1 88.5 %collective-permute-start.85 = (bf16[512,2048]{1,0:T(8,128)(2,1)S(1)}, bf16[512,2048]{1,0:T(8,128)(2,1)S(1)}, u32[]{:S(2)}, u32[]{:S(2)}) collective-permute-start(bf16[512,2048]{1,0:T(8,128)(2,1)S(1)} %fusion.18), channel_id=1, source_target_pairs={{0,1},{1,0},{2,3},{3,2},{4,5},{5,4},{6,7},{7,6},{8,9},{9,8},{10,11... | collective-permute-start | bytes 6291464 | tf_op jit(solution)/shard_map/ppermute | solution.py:154
  989.4 109.1 %collective-permute-start.82 = (bf16[512,2048]{1,0:T(8,128)(2,1)}, bf16[512,2048]{1,0:T(8,128)(2,1)}, u32[]{:S(2)}, u32[]{:S(2)}) collective-permute-start(bf16[512,2048]{1,0:T(8,128)(2,1)} %fusion.23), channel_id=1, source_target_pairs={{0,1},{1,0},{2,3},{3,2},{4,5},{5,4},{6,7},{7,6},{8,9},{9,8},{10,11... | collective-permute-start | bytes 6291464 | tf_op jit(solution)/shard_map/ppermute | solution.py:154
  1107.8 89.8 %collective-permute-start.86 = (bf16[512,2048]{1,0:T(8,128)(2,1)}, bf16[512,2048]{1,0:T(8,128)(2,1)}, u32[]{:S(2)}, u32[]{:S(2)}) collective-permute-start(bf16[512,2048]{1,0:T(8,128)(2,1)} %get-tuple-element.141), channel_id=1, source_target_pairs={{0,2},{2,0},{1,3},{3,1},{4,6},{6,4},{5,7},{7,5},{8,10},{10,8},{9,1... | collective-permute-start | bytes 6291464 | tf_op jit(solution)/shard_map/ppermute | solution.py:150
  1163.1 65.2 %collective-permute-start.108 = (bf16[256,2048]{1,0:T(8,128)(2,1)S(1)}, bf16[256,2048]{1,0:T(8,128)(2,1)S(1)}, u32[]{:S(2)}, u32[]{:S(2)}) collective-permute-start(bf16[256,2048]{1,0:T(8,128)(2,1)S(1)} %pad_maximum_fusion.16), channel_id=1, source_target_pairs={{8,0},{16,8},{24,16},{28,24},{20,28},{12,20},{4,12},{0,4},{9,1},{1... | collective-permute-start | bytes 3145736 | tf_op jit(solution)/shard_map/ppermute | solution.py:96
  1276.1 61.7 %collective-permute-start.105 = (bf16[256,2048]{1,0:T(8,128)(2,1)S(1)}, bf16[256,2048]{1,0:T(8,128)(2,1)S(1)}, u32[]{:S(2)}, u32[]{:S(2)}) collective-permute-start(bf16[256,2048]{1,0:T(8,128)(2,1)S(1)} %get-tuple-element.114), channel_id=1, source_target_pairs={{0,8},{8,16},{16,24},{24,28},{28,20},{20,12},{12,4},{4,0},{1,9},{9... | collective-permute-start | bytes 3145736 | tf_op jit(solution)/shard_map/ppermute | solution.py:93
  1483.3 72.9 %collective-permute-start.157 = (bf16[256,512]{1,0:T(8,128)(2,1)}, bf16[256,512]{1,0:T(8,128)(2,1)}, u32[]{:S(2)}, u32[]{:S(2)}) collective-permute-start(bf16[256,512]{1,0:T(8,128)(2,1)} %get-tuple-element.182), channel_id=1, source_target_pairs={{0,8},{8,16},{16,24},{24,28},{28,20},{20,12},{12,4},{4,0},{1,9},{9... | collective-permute-start | bytes 786440 | tf_op jit(solution)/shard_map/ppermute | solution.py:93
  1484.1 75.3 %collective-permute-start.161 = (bf16[256,512]{1,0:T(8,128)(2,1)}, bf16[256,512]{1,0:T(8,128)(2,1)}, u32[]{:S(2)}, u32[]{:S(2)}) collective-permute-start(bf16[256,512]{1,0:T(8,128)(2,1)} %fusion.144), channel_id=1, source_target_pairs={{8,0},{16,8},{24,16},{28,24},{20,28},{12,20},{4,12},{0,4},{9,1},{1... | collective-permute-start | bytes 786440 | tf_op jit(solution)/shard_map/ppermute | solution.py:96
  1559.4 148.8 %collective-permute-start.80 = (bf16[512,2048]{1,0:T(8,128)(2,1)}, bf16[512,2048]{1,0:T(8,128)(2,1)}, u32[]{:S(2)}, u32[]{:S(2)}) collective-permute-start(bf16[512,2048]{1,0:T(8,128)(2,1)} %fusion.26), channel_id=1, source_target_pairs={{0,1},{1,0},{2,3},{3,2},{4,5},{5,4},{6,7},{7,6},{8,9},{9,8},{10,11... | collective-permute-start | bytes 6291464 | tf_op jit(solution)/shard_map/ppermute | solution.py:154
  1571.8 81.4 %collective-permute-start.120 = (bf16[512,2048]{1,0:T(8,128)(2,1)}, bf16[512,2048]{1,0:T(8,128)(2,1)}, u32[]{:S(2)}, u32[]{:S(2)}) collective-permute-start(bf16[512,2048]{1,0:T(8,128)(2,1)} %fusion.53), channel_id=1, source_target_pairs={{0,1},{1,0},{2,3},{3,2},{4,5},{5,4},{6,7},{7,6},{8,9},{9,8},{10,11... | collective-permute-start | bytes 6291464 | tf_op jit(solution)/shard_map/ppermute | solution.py:154
  1581.7 114.5 %collective-permute-start.133 = (bf16[512,2048]{1,0:T(8,128)(2,1)S(1)}, bf16[512,2048]{1,0:T(8,128)(2,1)}, u32[]{:S(2)}, u32[]{:S(2)}) collective-permute-start(bf16[512,2048]{1,0:T(8,128)(2,1)S(1)} %fusion.54), channel_id=1, source_target_pairs={{0,1},{1,0},{2,3},{3,2},{4,5},{5,4},{6,7},{7,6},{8,9},{9,8},{10,11... | collective-permute-start | bytes 6291464 | tf_op jit(solution)/shard_map/ppermute | solution.py:154
  (284 other events, 7434.8 us)

commit v2 on v1

v2 whole, which is shorter than its diff:
```python
import functools
import math

import jax
import jax.numpy as jnp
from jax import lax
from jax.experimental import pallas as pl
from jax.experimental.pallas import tpu as pltpu
from jax.sharding import Mesh
from jax.sharding import PartitionSpec as P

QUERY_HEADS = 32
KEY_VALUE_HEADS = 8
HEAD_SIZE = 64
LEVELS = 3

EPS = 1e-05
THETA = 500000.0
NEG = -1e30
LN2 = math.log(2.0)
SWAP = [(0, 1), (1, 0)]
F32 = jnp.float32
BF16 = jnp.bfloat16
SMALL = pl.CostEstimate(flops=2**20, bytes_accessed=2**10, transcendentals=0)


def dot(left, right, left_dim=1, right_dim=0):
    return lax.dot_general(
        left, right, (((left_dim,), (right_dim,)), ((), ())), preferred_element_type=F32
    )


def row_scale_of(rows_in):
    return lax.rsqrt(jnp.mean(rows_in * rows_in, axis=-1, keepdims=True) + EPS)


def norm_back(grad_normed, normed, row_scale):
    return row_scale * (
        grad_normed - normed * jnp.mean(grad_normed * normed, axis=-1, keepdims=True)
    )


def rope_angles(position, head_dim):
    half_dim = head_dim // 2
    index_row = jnp.arange(half_dim, dtype=F32)
    inverse = THETA ** (-2.0 * index_row / head_dim)
    wavelen = 2.0 * math.pi / inverse
    smooth = jnp.clip((8192.0 / wavelen - 1.0) / 3.0, 0.0, 1.0)
    inverse = (1.0 - smooth) * inverse / 32.0 + smooth * inverse
    return inverse[:, None] * position.astype(F32)[None, :]


def turn(first_half, second_half, cosine, sine):
    return first_half * cosine - second_half * sine, second_half * cosine + first_half * sine


def tree_tables(parents_row, lengths):
    seg_count = parents_row.shape[0]
    labels = jnp.arange(seg_count, dtype=jnp.int32)
    ends_at = jnp.cumsum(lengths)
    starts_at = ends_at - lengths
    reaches = labels[:, None] == labels[None, :]
    climber = labels
    for _ in range(LEVELS - 1):
        climber = jnp.sum(
            jnp.where(climber[:, None] == labels[None, :], parents_row[None, :], 0), axis=1
        )
        reaches = reaches | (climber[:, None] == labels[None, :])
    before = jnp.sum(
        jnp.where(reaches & (labels[:, None] != labels[None, :]), lengths[None, :], 0), axis=1
    )
    return reaches, starts_at, ends_at, before


def after_all(values, others):
    if not others:
        return list(values)
    return list(lax.optimization_barrier(tuple(values) + tuple(others))[: len(values)])


def unwritten(like, shape):
    return pl.pallas_call(
        lambda like_ref, out_ref: None,
        in_specs=[pl.BlockSpec(memory_space=pl.ANY)],
        out_specs=pl.BlockSpec(memory_space=pl.ANY),
        out_shape=jax.ShapeDtypeStruct(shape, like.dtype),
        name="buffer",
    )(like)


class Ring:
    def __init__(self):
        self.count = lax.axis_size("zy")
        count = self.count
        place = [2 * i if i < count // 2 else 2 * (count - 1 - i) + 1 for i in range(count)]
        self.right = [(place[i], place[(i + 1) % count]) for i in range(count)]
        self.left = [(b, a) for a, b in self.right]
        me = lax.axis_index("zy")
        self.spot = jnp.where(me % 2 == 0, me // 2, count - 1 - me // 2)

    def chip(self, offset):
        spot = lax.rem(self.spot + offset + self.count, self.count)
        return jnp.where(spot < self.count // 2, 2 * spot, 2 * (self.count - 1 - spot) + 1)

    def go_right(self, value):
        return lax.ppermute(value, "zy", self.right)

    def go_left(self, value):
        return lax.ppermute(value, "zy", self.left)

    def put(self, whole, part, offset, row=0):
        at = (self.chip(offset), row) + (0,) * (part.ndim - 1)
        return lax.dynamic_update_slice(whole, part[None], at)


class Gather:
    def __init__(self, ring, pieces):
        self.ring, self.step = ring, 0
        self.cuts = [piece.shape[0] // 2 for piece in pieces]
        wholes = [unwritten(piece, (ring.count,) + piece.shape) for piece in pieces]
        self.wholes = [ring.put(whole, piece, 0) for whole, piece in zip(wholes, pieces)]
        self.rightward = self.leftward = list(pieces)

    def hop(self, *others):
        ring, count = self.ring, len(self.cuts)
        both = after_all(self.rightward + self.leftward, others)
        rightward, leftward = both[:count], both[count:]
        self.step += 1
        far = self.step == ring.count // 2
        if far:
            rightward = [part[:cut] for part, cut in zip(rightward, self.cuts)]
            leftward = [part[cut:] for part, cut in zip(leftward, self.cuts)]
        rightward = [ring.go_right(part) for part in rightward]
        leftward = [ring.go_left(part) for part in leftward]
        for i, cut in enumerate(self.cuts):
            whole = ring.put(self.wholes[i], rightward[i], -self.step)
            self.wholes[i] = ring.put(whole, leftward[i], self.step, cut if far else 0)
        self.rightward, self.leftward = rightward, leftward
        return tuple(rightward) + tuple(leftward)

    def finish(self, *others):
        while self.step < self.ring.count // 2:
            self.hop(*others)
        return self.wholes


class Reduce:
    def __init__(self, ring, terms):
        self.ring, self.terms, self.left = ring, list(terms), ring.count // 2
        self.cuts = [term.shape[1] // 2 for term in terms]
        self.rightward = self.leftward = None

    def each(self, offset):
        chip = self.ring.chip(offset)
        return [lax.dynamic_index_in_dim(term, chip, 0, keepdims=False) for term in self.terms]

    def hop(self, *others):
        ring, step, count = self.ring, self.left, len(self.cuts)
        if self.rightward is None:
            far = after_all(self.each(step), others)
            rightward = [part[:cut] for part, cut in zip(far, self.cuts)]
            leftward = [part[cut:] for part, cut in zip(far, self.cuts)]
        else:
            both = after_all(self.rightward + self.leftward, others)
            rightward, leftward = both[:count], both[count:]
            mine, other = self.each(step), self.each(-step)
            if step == ring.count // 2 - 1:
                for i, cut in enumerate(self.cuts):
                    parts = [add_low(mine[i][:cut], rightward[i]), mine[i][cut:]]
                    rightward[i] = jnp.concatenate(parts, axis=0)
                    parts = [other[i][:cut], add_low(other[i][cut:], leftward[i])]
                    leftward[i] = jnp.concatenate(parts, axis=0)
            else:
                rightward = [add_low(one, part) for one, part in zip(mine, rightward)]
                leftward = [add_low(one, part) for one, part in zip(other, leftward)]
        self.rightward = [ring.go_right(part) for part in rightward]
        self.leftward = [ring.go_left(part) for part in leftward]
        self.left -= 1
        return tuple(self.rightward) + tuple(self.leftward)

    def finish(self, *others):
        while self.left > 0:
            self.hop(*others)
        return [
            mine.astype(F32) + one.astype(F32) + two.astype(F32)
            for mine, one, two in zip(self.each(0), self.rightward, self.leftward)
        ]


def add_low(left, right):
    return (left.astype(F32) + right.astype(F32)).astype(BF16)


def other_core(value):
    return lax.ppermute(value, "core", SWAP)


def other_half(value):
    return lax.ppermute(value, "tp", SWAP)


def by_core(own, other, axis):
    first = lax.axis_index("core") == 0
    return jnp.concatenate(
        [jnp.where(first, own, other), jnp.where(first, other, own)], axis=axis
    )


def split_by_core(value, axis):
    core = lax.axis_index("core")
    size = value.shape[axis] // 2
    return (
        lax.dynamic_slice_in_dim(value, core * size, size, axis),
        lax.dynamic_slice_in_dim(value, (1 - core) * size, size, axis),
    )


def split3(value):
    high = value.astype(BF16)
    rest = value - high.astype(F32)
    middle = rest.astype(BF16)
    low = (rest - middle.astype(F32)).astype(BF16)
    return high, middle, low


def causal(scores, block):
    key_at = lax.broadcasted_iota(jnp.int32, scores.shape, 0)
    query_at = lax.rem(lax.broadcasted_iota(jnp.int32, scores.shape, 1), block)
    return jnp.where(key_at <= query_at, scores, NEG)


def block_of(ref, index, block, per_piece):
    piece = lax.div(index, per_piece)
    start = pl.multiple_of(lax.rem(index, per_piece) * block, block)
    return ref[piece, 0, pl.ds(start, block), :]


def attend_kernel(
    block, rep, per_piece, count_ref, list_ref, diag_ref, query_ref, mask_ref, kv_ref, hot_ref,
    out_ref, lse_ref, query_aug, turned,
):
    at = pl.program_id(1)
    key_blocks = hot_ref.shape[0] // block - 1

    @pl.when(at == 0)
    def _():
        rows = per_piece * block
        for piece in range(kv_ref.shape[0]):
            turned[:, piece * rows : (piece + 1) * rows] = kv_ref[piece, 0].T

    query_aug[HEAD_SIZE:, :] = jnp.zeros_like(query_aug[HEAD_SIZE:, :])
    for r in range(rep):
        columns = slice(r * block, (r + 1) * block)
        query_aug[:HEAD_SIZE, columns] = query_ref[r * HEAD_SIZE : (r + 1) * HEAD_SIZE, :]
        query_aug[128:144, columns] = mask_ref[...]

    def scores_of(index):
        keys = block_of(kv_ref, jnp.minimum(index, key_blocks - 1), block, per_piece)
        hot = hot_ref[pl.ds(pl.multiple_of(index * block, block), block), :]
        return jnp.dot(
            jnp.concatenate([keys, hot], axis=1), query_aug[...], preferred_element_type=F32
        )

    def values_of(index):
        index = jnp.minimum(index, key_blocks - 1)
        return turned[HEAD_SIZE:, pl.ds(pl.multiple_of(index * block, block), block)]

    diagonal = diag_ref[at]
    scores = causal(scores_of(diagonal), block)
    top = jnp.max(scores, axis=0, keepdims=True)
    probs = jnp.exp2(scores - top)
    total = jnp.sum(probs, axis=0, keepdims=True)
    mixed = jnp.dot(values_of(diagonal), probs.astype(BF16), preferred_element_type=F32)

    def step(j, carry):
        top, total, mixed = carry
        one, two = list_ref[at, 2 * j], list_ref[at, 2 * j + 1]
        first, second = scores_of(one), scores_of(two)
        new = jnp.maximum(top, jnp.max(first, axis=0, keepdims=True))
        new = jnp.maximum(new, jnp.max(second, axis=0, keepdims=True))
        factor = jnp.exp2(top - new)
        first, second = jnp.exp2(first - new), jnp.exp2(second - new)
        total = (
            total * factor
            + jnp.sum(first, axis=0, keepdims=True)
            + jnp.sum(second, axis=0, keepdims=True)
        )
        values = jnp.concatenate([values_of(one), values_of(two)], axis=1)
        probs = jnp.concatenate([first.astype(BF16), second.astype(BF16)], axis=0)
        mixed = mixed * factor + jnp.dot(values, probs, preferred_element_type=F32)
        return new, total, mixed

    pairs = lax.div(count_ref[at] + 1, 2)
    top, total, mixed = lax.fori_loop(0, pairs, step, (top, total, mixed))
    mixed = mixed * (1.0 / total)
    lse = top + jnp.log2(total)
    for r in range(rep):
        columns = slice(r * block, (r + 1) * block)
        out_ref[r * HEAD_SIZE : (r + 1) * HEAD_SIZE, :] = mixed[:, columns].astype(BF16)
        lse_ref[0, r : r + 1, :] = lse[:, columns]


def attend(tree, tables, query, mask, kv, rep, block):
    counts, lists, diagonals, hot = tables
    heads = query.shape[0]
    pieces, _, rows, _ = kv.shape
    groups, query_blocks = heads // (rep * HEAD_SIZE), rows // block
    keys = pieces * rows
    grid_spec = pltpu.PrefetchScalarGridSpec(
        num_scalar_prefetch=3,
        grid=(groups, query_blocks),
        in_specs=[
            pl.BlockSpec(
                (rep * HEAD_SIZE, block), lambda g, q, *_: (g, tree * query_blocks + q)
            ),
            pl.BlockSpec((16, block), lambda g, q, *_: (0, q)),
            pl.BlockSpec((pieces, 1, rows, 128), lambda g, q, *_: (0, tree, 0, g)),
            pl.BlockSpec((keys + block, 128), lambda g, q, *_: (0, 0)),
        ],
        out_specs=[
            pl.BlockSpec((rep * HEAD_SIZE, block), lambda g, q, *_: (g, q)),
            pl.BlockSpec((1, rep, block), lambda g, q, *_: (g, 0, q)),
        ],
        scratch_shapes=[
            pltpu.VMEM((256, rep * block), BF16),
            pltpu.VMEM((128, keys), BF16),
        ],
    )
    return pl.pallas_call(
        functools.partial(attend_kernel, block, rep, rows // block),
        grid_spec=grid_spec,
        out_shape=[
            jax.ShapeDtypeStruct((heads, rows), BF16),
            jax.ShapeDtypeStruct((groups, rep, rows), F32),
        ],
        compiler_params=pltpu.CompilerParams(vmem_limit_bytes=48 * 2**20),
        cost_estimate=SMALL,
        name="tree_attention",
    )(counts, lists, diagonals, query, mask, kv, hot)


def attend_back_kernel(
    block, rep, per_piece, seen_ref, query_ref, mask_ref, mixed_ref, grad_ref, lse_ref, kv_ref,
    hot_ref, cosine_ref, sine_ref, before_ref, grad_query_ref, grad_kv_ref, augs, turned_rows,
    key_turned, grad_query, grad_kv,
):
    rows = per_piece * block
    query_blocks = rows // block
    key_blocks = kv_ref.shape[0] * per_piece
    width = rep * block

    for piece in range(kv_ref.shape[0]):
        key_turned[:, piece * rows : (piece + 1) * rows] = kv_ref[piece, 0].T
    grad_kv[...] = jnp.zeros_like(grad_kv)
    grad_query[...] = jnp.zeros_like(grad_query)
    augs[...] = jnp.zeros_like(augs)
    none = jnp.zeros((HEAD_SIZE, block), BF16)
    for at in range(query_blocks):
        columns = slice(at * block, (at + 1) * block)
        for r in range(rep):
            here = slice(2 * at * width + r * block, 2 * at * width + (r + 1) * block)
            there = slice((2 * at + 1) * width + r * block, (2 * at + 1) * width + (r + 1) * block)
            head = slice(r * HEAD_SIZE, (r + 1) * HEAD_SIZE)
            query, grad = query_ref[head, columns], grad_ref[head, columns]
            augs[:HEAD_SIZE, here] = query
            augs[HEAD_SIZE : 2 * HEAD_SIZE, there] = grad
            delta = jnp.sum(
                grad.astype(F32) * mixed_ref[head, columns].astype(F32), axis=0, keepdims=True
            )
            empty = jnp.zeros((13, block), BF16)
            augs[128:160, here] = jnp.concatenate(
                [mask_ref[:, columns], *split3(-lse_ref[0, r : r + 1, columns]), empty], axis=0
            )
            augs[128:160, there] = jnp.concatenate(
                [jnp.zeros((16, block), BF16), *split3(-delta), empty], axis=0
            )
            turned_rows[here, :] = jnp.concatenate([none, grad], axis=0).T
            turned_rows[there, :] = jnp.concatenate([query, none], axis=0).T

    def over_keys(index, _):
        rows_at = pl.ds(pl.multiple_of(index * block, block), block)
        for at in range(query_blocks):
            columns = slice(2 * at * width, (2 * at + 2) * width)

            def work(on_diagonal):
                both = jnp.dot(
                    jnp.concatenate(
                        [block_of(kv_ref, index, block, per_piece), hot_ref[rows_at, :]], axis=1
                    ),
                    augs[:, columns],
                    preferred_element_type=F32,
                )
                scores, grad_probs = both[:, :width], both[:, width:]
                if on_diagonal:
                    scores = causal(scores, block)
                probs = jnp.exp2(scores)
                grad_scores = (probs * grad_probs).astype(BF16)
                grad_kv[rows_at, :] += jnp.dot(
                    jnp.concatenate([probs.astype(BF16), grad_scores], axis=1),
                    turned_rows[columns, :],
                    preferred_element_type=F32,
                )
                grad_query[:, at * width : (at + 1) * width] += jnp.dot(
                    key_turned[:HEAD_SIZE, rows_at], grad_scores, preferred_element_type=F32
                )

            seen = seen_ref[at, index]
            pl.when(seen == 1)(functools.partial(work, False))
            pl.when(seen == 2)(functools.partial(work, True))
        return 0

    lax.fori_loop(0, key_blocks, over_keys, 0)
    for at in range(query_blocks):
        columns = slice(at * block, (at + 1) * block)
        cosine = cosine_ref[:, columns] * HEAD_SIZE**-0.5
        sine = -sine_ref[:, columns] * HEAD_SIZE**-0.5
        for r in range(0, rep, 2):
            parts = []
            for head in (r, r + 1):
                here = slice(at * width + head * block, at * width + (head + 1) * block)
                grad = grad_query[:, here]
                half = HEAD_SIZE // 2
                parts += turn(grad[:half], grad[half:], cosine, sine)
            grad_query_ref[columns, r * HEAD_SIZE : (r + 2) * HEAD_SIZE] = (
                jnp.concatenate(parts, axis=0).T.astype(BF16)
            )
    for piece in range(kv_ref.shape[0]):
        grads = grad_kv[piece * rows : (piece + 1) * rows, :]
        lanes = lax.broadcasted_iota(jnp.int32, grads.shape, 1)
        grad_kv_ref[piece] = jnp.where(lanes < HEAD_SIZE, grads * LN2, grads).astype(BF16)


def attend_back(
    tree, group, seen, hot, query, mask, mixed, grad, lse, kv, cosine, sine, rep, block, before
):
    pieces, _, rows, _ = kv.shape
    keys = pieces * rows
    heads = rep * HEAD_SIZE
    head = pl.BlockSpec((heads, rows), lambda i, *_: (group, 0))
    table = pl.BlockSpec((HEAD_SIZE // 2, rows), lambda i, *_: (0, tree))
    grid_spec = pltpu.PrefetchScalarGridSpec(
        num_scalar_prefetch=1,
        grid=(1,),
        in_specs=[
            pl.BlockSpec((heads, rows), lambda i, *_: (group, tree)),
            pl.BlockSpec((16, rows), lambda i, *_: (0, 0)),
            head,
            head,
            pl.BlockSpec((1, rep, rows), lambda i, *_: (group, 0, 0)),
            pl.BlockSpec((pieces, 1, rows, 128), lambda i, *_: (0, tree, 0, group)),
            pl.BlockSpec((keys + block, 128), lambda i, *_: (0, 0)),
            table,
            table,
            pl.BlockSpec(memory_space=pl.ANY),
        ],
        out_specs=[
            pl.BlockSpec((rows, heads), lambda i, *_: (0, 0)),
            pl.BlockSpec((pieces, rows, 128), lambda i, *_: (0, 0, group)),
        ],
        scratch_shapes=[
            pltpu.VMEM((256, 2 * rep * rows), BF16),
            pltpu.VMEM((2 * rep * rows, 128), BF16),
            pltpu.VMEM((128, keys), BF16),
            pltpu.VMEM((HEAD_SIZE, rep * rows), F32),
            pltpu.VMEM((keys, 128), F32),
        ],
    )
    return pl.pallas_call(
        functools.partial(attend_back_kernel, block, rep, rows // block),
        grid_spec=grid_spec,
        out_shape=[
            jax.ShapeDtypeStruct((rows, heads), BF16),
            jax.ShapeDtypeStruct((pieces, rows, kv.shape[3]), BF16),
        ],
        input_output_aliases={10: 1} if group else {},
        compiler_params=pltpu.CompilerParams(vmem_limit_bytes=56 * 2**20),
        cost_estimate=SMALL,
        name="tree_attention_back",
    )(seen, query, mask, mixed, grad, lse, kv, hot, cosine, sine, cosine if before is None else before)


def project_kernel(
    heads, columns, own_ref, other_ref, gain_ref, weight_ref, cosine_ref, sine_ref, inner_ref, query_ref,
    kv_ref, rows,
):
    mine = lax.rem(pl.program_id(0), 2) == 0

    @pl.when(mine)
    def _():
        rows[...] = own_ref[0].astype(F32)

    @pl.when(jnp.logical_not(mine))
    def _():
        rows[...] = other_ref[0].astype(F32)

    x = rows[...]
    inner = (x * row_scale_of(x) * gain_ref[...]).astype(BF16)
    inner_ref[...] = inner
    made = jnp.dot(inner, weight_ref[:, :columns], preferred_element_type=F32)
    cosine, sine = cosine_ref[...], sine_ref[...]
    half = HEAD_SIZE // 2

    def turned(values):
        parts = []
        for start in range(0, values.shape[0], HEAD_SIZE):
            parts += turn(
                values[start : start + half], values[start + half : start + HEAD_SIZE], cosine, sine
            )
        return jnp.concatenate(parts, axis=0)

    query_ref[...] = (turned(made[:, :heads].T) * (HEAD_SIZE**-0.5 / LN2)).astype(BF16)
    kv = made[:, heads:].T
    parts = []
    for start in range(0, kv.shape[0], 128):
        parts += [turned(kv[start : start + HEAD_SIZE]), kv[start + HEAD_SIZE : start + 128]]
    kv_ref[...] = jnp.concatenate(parts, axis=0).T.astype(BF16)


def project(own, other, gain, weight, cosine, sine, heads, kv_columns, tile):
    trees, rows, width = own.shape
    tiles = rows // tile
    last = trees * tiles - 1

    def place(half):
        def index(t, j):
            tree, at = t // 2, t % 2
            same = at == half
            if half == 0:
                return (jnp.where(same, tree, tree), jnp.where(same, j, tiles - 1), 0)
            return (tree, jnp.where(same, j, 0), 0)

        return index

    flat = lambda t, j: (t * tiles + j, 0)
    lanes = lambda t, j: (0, t * tiles + j)
    tokens = 2 * trees * rows
    columns = heads + kv_columns
    return pl.pallas_call(
        functools.partial(project_kernel, heads, columns),
        grid=(2 * trees, tiles),
        in_specs=[
            pl.BlockSpec((1, tile, width), place(0)),
            pl.BlockSpec((1, tile, width), place(1)),
            pl.BlockSpec((1, width), lambda t, j: (0, 0)),
            pl.BlockSpec((width, columns), lambda t, j: (0, 0)),
            pl.BlockSpec((HEAD_SIZE // 2, tile), lanes),
            pl.BlockSpec((HEAD_SIZE // 2, tile), lanes),
        ],
        out_specs=[
            pl.BlockSpec((tile, width), flat),
            pl.BlockSpec((heads, tile), lanes),
            pl.BlockSpec((tile, columns - heads), flat),
        ],
        out_shape=[
            jax.ShapeDtypeStruct((tokens, width), BF16),
            jax.ShapeDtypeStruct((heads, tokens), BF16),
            jax.ShapeDtypeStruct((tokens, columns - heads), BF16),
        ],
        scratch_shapes=[pltpu.VMEM((tile, width), F32)],
        compiler_params=pltpu.CompilerParams(vmem_limit_bytes=48 * 2**20),
        cost_estimate=SMALL,
        name="project",
    )(own, other, gain, weight, cosine, sine)


def units_kernel(
    inner_ref, grad_ref, gate_ref, up_ref, down_ref, hidden_ref, grad_gate_ref, grad_up_ref
):
    inner = inner_ref[...]
    gate = jnp.dot(inner, gate_ref[...], preferred_element_type=F32)
    up = jnp.dot(inner, up_ref[...], preferred_element_type=F32)
    grad_hidden = jnp.dot(grad_ref[...], down_ref[...], preferred_element_type=F32)
    sigmoid = jax.nn.sigmoid(gate)
    activated = gate * sigmoid
    hidden_ref[...] = (activated * up).astype(BF16)
    grad_gate_ref[...] = (grad_hidden * up * sigmoid * (1.0 + gate * (1.0 - sigmoid))).astype(BF16)
    grad_up_ref[...] = (grad_hidden * activated).astype(BF16)


def hidden_units(inner, grad, gate_up, down):
    tokens, width = inner.shape
    units = down.shape[1]
    rows, columns = math.gcd(tokens, 512), math.gcd(units, 512)
    tiles = units // columns
    tall = pl.BlockSpec((rows, width), lambda j, i: (i, 0))
    wide = pl.BlockSpec((width, columns), lambda j, i: (0, j))
    second = pl.BlockSpec((width, columns), lambda j, i: (0, tiles + j))
    tile = pl.BlockSpec((rows, columns), lambda j, i: (i, j))
    made = jax.ShapeDtypeStruct((tokens, units), BF16)
    return pl.pallas_call(
        units_kernel,
        grid=(tiles, tokens // rows),
        in_specs=[tall, tall, wide, second, wide],
        out_specs=[tile, tile, tile],
        out_shape=[made, made, made],
        compiler_params=pltpu.CompilerParams(vmem_limit_bytes=56 * 2**20),
        cost_estimate=SMALL,
        name="hidden_units",
    )(inner, grad, gate_up, gate_up, down)


def back_units_kernel(grad_gate_ref, grad_up_ref, gate_ref, up_ref, out_ref):
    contract = (((1,), (1,)), ((), ()))
    out_ref[...] = (
        lax.dot_general(grad_gate_ref[...], gate_ref[...], contract, preferred_element_type=F32)
        + lax.dot_general(grad_up_ref[...], up_ref[...], contract, preferred_element_type=F32)
    ).astype(BF16)


def back_units(tree, tokens, grad_gate, grad_up, gate_up):
    width, units = gate_up.shape[0], grad_up.shape[1]
    rows, columns = math.gcd(tokens, 1024), math.gcd(width, 512)
    first = tree * (tokens // rows)
    tall = pl.BlockSpec((rows, units), lambda j, i: (first + i, 0))
    return pl.pallas_call(
        back_units_kernel,
        grid=(width // columns, tokens // rows),
        in_specs=[
            tall,
            tall,
            pl.BlockSpec((columns, units), lambda j, i: (j, 0)),
            pl.BlockSpec((columns, units), lambda j, i: (j, 1)),
        ],
        out_specs=pl.BlockSpec((rows, columns), lambda j, i: (i, j)),
        out_shape=jax.ShapeDtypeStruct((tokens, width), BF16),
        compiler_params=pltpu.CompilerParams(vmem_limit_bytes=56 * 2**20),
        cost_estimate=SMALL,
        name="back_units",
    )(grad_gate, grad_up, gate_up, gate_up)


def unit_grads_kernel(rows_ref, grad_ref, out_ref, turned):
    @pl.when(pl.program_id(1) == 0)
    def _():
        turned[...] = rows_ref[...].T

    out_ref[...] = jnp.dot(turned[...], grad_ref[...], preferred_element_type=F32).astype(BF16)


def unit_grads(rows_in, grad):
    tokens, width = rows_in.shape
    units = grad.shape[1]
    rows, columns = math.gcd(width, 1024), math.gcd(units, 1024)
    return pl.pallas_call(
        unit_grads_kernel,
        grid=(width // rows, units // columns),
        in_specs=[
            pl.BlockSpec((tokens, rows), lambda i, j: (0, i)),
            pl.BlockSpec((tokens, columns), lambda i, j: (0, j)),
        ],
        out_specs=pl.BlockSpec((rows, columns), lambda i, j: (i, j)),
        out_shape=jax.ShapeDtypeStruct((width, units), BF16),
        scratch_shapes=[pltpu.VMEM((rows, tokens), BF16)],
        compiler_params=pltpu.CompilerParams(vmem_limit_bytes=56 * 2**20),
        cost_estimate=SMALL,
        name="unit_grads",
    )(rows_in, grad)


def shards(
    layer_in,
    out_grad,
    parents,
    seg_len,
    attn_gain,
    w_query,
    key_weight,
    value_weight,
    w_out,
    ffn_gain,
    w_gate,
    w_up,
    w_down,
):
    trees, rows, width = layer_in.shape
    ring = Ring()
    chips = ring.count
    here, core = lax.axis_index("zy"), lax.axis_index("core")
    chip_rows = 2 * rows
    keys = chips * chip_rows
    groups = KEY_VALUE_HEADS // (2 * lax.axis_size("tp"))
    rep = QUERY_HEADS // KEY_VALUE_HEADS
    heads = groups * rep
    head_cols, kv_cols = heads * HEAD_SIZE, groups * HEAD_SIZE
    block = math.gcd(rows, 256)
    per_half = rows // block
    query_blocks, key_blocks = chip_rows // block, keys // block

    def column_piece(weight):
        keep, give = split_by_core(weight, 1)
        return by_core(keep, other_core(give), 0)

    def row_piece(weight):
        keep, give = split_by_core(weight, 0)
        return by_core(keep.T, other_core(give).T, 0)

    def column_grad(total):
        keep, give = split_by_core(total, 0)
        return by_core(keep, other_core(give), 1)

    def row_grad(total):
        keep, give = split_by_core(total, 0)
        return by_core(keep, other_core(give), 1).T

    def interleave(keys, values):
        parts = []
        for group in range(groups):
            at = slice(group * HEAD_SIZE, (group + 1) * HEAD_SIZE)
            parts += [keys[:, at], values[:, at]]
        return parts

    kv_pieces = interleave(column_piece(key_weight), column_piece(value_weight))
    gains = jnp.pad(jnp.stack([attn_gain, ffn_gain], axis=1), ((0, 0), (0, 126)))
    gain_piece = by_core(gains, other_core(gains), 0)
    qkv_piece = jnp.concatenate(
        [column_piece(w_query)] + kv_pieces + [gain_piece, row_piece(w_out)], axis=1
    )
    qkv_ring = Gather(ring, [qkv_piece])
    (first_in,) = after_all((layer_in,), (qkv_piece,))
    other_in = other_core(first_in)
    hops = [qkv_ring.hop() for _ in range(chips // 2)]
    (w_attn,) = qkv_ring.finish()
    w_attn = w_attn.reshape(width, -1)
    w_qkv, gain_all, w_o = jnp.split(
        w_attn, [head_cols + 2 * kv_cols, head_cols + 2 * kv_cols + 128], axis=1
    )
    gain_all = gain_all.T[:2].astype(F32)
    gain_a, gain_f = gain_all[0], gain_all[1]

    def token_order(chip):
        first = (chip * 2 + core) * rows
        second = (chip * 2 + 1 - core) * rows
        steps = jnp.arange(rows, dtype=jnp.int32)
        return jnp.concatenate(
            [first[..., None] + steps, second[..., None] + steps], axis=-1
        ).reshape(-1)

    own_tokens = token_order(here)
    key_tokens = token_order(jnp.arange(chips, dtype=jnp.int32))
    own_block = own_tokens[::block] // block
    key_block = key_tokens[::block] // block
    diagonals = here * query_blocks + jnp.arange(query_blocks, dtype=jnp.int32)
    labels = jnp.arange(16, dtype=jnp.int32)
    tables, positions, masks, seens = [], [], [], []
    for tree in range(trees):
        row = after_all((parents[tree], seg_len[tree]), hops[min(tree, len(hops) - 1)])
        reaches, starts_at, ends_at, before = tree_tables(*row)
        seg_count = ends_at.shape[0]
        extra = 16 - seg_count
        reach16 = jnp.pad(reaches, ((0, extra), (0, extra)))
        starts16 = jnp.pad(starts_at, (0, extra))
        before16 = jnp.pad(before, (0, extra))
        ends16 = jnp.pad(ends_at, (0, extra), constant_values=2**30)
        own_seg = jnp.sum((own_tokens[:, None] >= ends_at[None, :]).astype(jnp.int32), axis=1)
        key_seg = jnp.sum((key_tokens[:, None] >= ends_at[None, :]).astype(jnp.int32), axis=1)
        member = own_seg[None, :] == labels[:, None]
        positions.append(
            own_tokens + jnp.sum(jnp.where(member, (before16 - starts16)[:, None], 0), axis=0)
        )
        seen_by = jnp.sum(
            jnp.where(member[:, None, :], reach16.astype(jnp.int32)[:, :, None], 0), axis=0
        )
        masks.append(jnp.where(seen_by > 0, 0.0, NEG).astype(BF16))
        lanes = jnp.arange(128, dtype=jnp.int32)
        key_seg_all = jnp.concatenate([key_seg, jnp.full((block,), seg_count, jnp.int32)])
        hot = (lanes[None, :] == key_seg_all[:, None]) | ((lanes >= 16) & (lanes < 19))[None, :]
        hot = hot.astype(BF16)

        def holds(blocks):
            low = blocks[:, None] * block
            return ((starts_at[None, :] < low + block) & (ends_at[None, :] > low)).astype(F32)

        linked = dot(dot(holds(own_block), reaches.astype(F32)), holds(key_block), 1, 1) > 0.5
        seen = linked & (key_block[None, :] < own_block[:, None])
        rank = jnp.cumsum(seen.astype(jnp.int32), axis=1) - 1
        slots = jnp.arange(key_blocks + 2, dtype=jnp.int32)
        index = jnp.arange(key_blocks, dtype=jnp.int32)
        chosen = seen[:, :, None] & (rank[:, :, None] == slots[None, None, :])
        lists = key_blocks + jnp.sum(
            jnp.where(chosen, index[None, :, None] - key_blocks, 0), axis=1
        )
        counts = jnp.sum(seen.astype(jnp.int32), axis=1)
        tables.append((counts, lists, diagonals, hot))
        on_diagonal = index[None, :] == diagonals[:, None]
        seens.append(jnp.where(on_diagonal, 2, seen.astype(jnp.int32)))
    position = jnp.concatenate(positions)
    angles = rope_angles(position, HEAD_SIZE)
    cosine, sine = jnp.cos(angles), jnp.sin(angles)

    inner_a, query, key_value = project(
        first_in, other_in, gain_a[None], w_attn, cosine, sine, head_cols, 2 * kv_cols,
        math.gcd(rows, 256),
    )
    cosine_rows, sine_rows = cosine.T[:, None, :], sine.T[:, None, :]
    kv_ring = Gather(ring, [key_value.reshape(trees, chip_rows, 2 * kv_cols)])
    kv_hops = [kv_ring.hop()]
    w_gate, w_up, w_down, out_grad = after_all((w_gate, w_up, w_down, out_grad), (key_value,))
    other_grad = other_core(out_grad)
    units_piece = jnp.concatenate([column_piece(w_gate), column_piece(w_up)], axis=1)
    down_piece = row_piece(w_down)
    while kv_ring.step < chips // 2 - 1:
        kv_hops.append(kv_ring.hop())
    (layer_in,) = after_all((layer_in,), kv_hops[0])
    scale_a = row_scale_of(layer_in.astype(F32))
    (out_grad,) = after_all((out_grad,), kv_hops[1])
    grad_low = jnp.concatenate([out_grad, other_grad], axis=1).reshape(trees * chip_rows, width)
    kv_hops.append(kv_ring.hop(grad_low, scale_a, units_piece, down_piece))
    units_ring = Gather(ring, [units_piece])
    units_hop = units_ring.hop(*kv_hops[-2])
    (kvs,) = kv_ring.finish()

    def core_sum(part):
        if part.ndim == 2:
            part = part.reshape(2, rows, width)
        return part[0].astype(F32) + other_core(part[1].astype(BF16)).astype(F32)

    def laid(buffer, value, tree):
        return lax.dynamic_update_slice(buffer, value[None], (tree, 0, 0))

    mixes, lses, middles, inners, normeds_f, scales_f, lows = [], [], [], [], [], [], []
    for tree in range(trees):
        mixed, lse = attend(tree, tables[tree], query, masks[tree], kvs, rep, block)
        if tree:
            units_hop += (arrived,)
        (mixed,) = after_all((mixed,), units_hop)
        units_hop = units_ring.hop(mixed)
        mixes.append(mixed)
        lses.append(lse)
        lows.append(core_sum(dot(mixed, w_o, 0, 1)).astype(BF16))
        if tree == 0:
            arrived = other_half(lows[0])
            (query,) = after_all((query,), lows)
    arrived = [after_all((arrived,), lows[1:])[0]] + [other_half(low) for low in lows[1:]]
    (layer_in,) = after_all((layer_in,), lows)
    for tree in range(trees):
        rows_in = layer_in[tree].astype(F32)
        middle = rows_in + (lows[tree].astype(F32) + arrived[tree].astype(F32))
        scale_f = row_scale_of(middle)
        normed_f = middle * scale_f
        inner = (normed_f * gain_f).astype(BF16)
        inners += [inner, other_core(inner)]
        middles.append(middle)
        scales_f.append(scale_f)
        normeds_f.append(normed_f)
    inner_f = jnp.concatenate(inners, axis=0)

    while units_ring.step < chips // 2 - 1:
        units_hop = units_ring.hop()
    down_ring = Gather(ring, [down_piece])
    down_ring.hop(*units_hop)
    down_ring.hop(arrived[-1])
    (w_units,) = units_ring.finish()
    (w_d,) = down_ring.finish()
    w_units, w_d = w_units.reshape(width, -1), w_d.reshape(width, -1)
    hidden, grad_gate, grad_up = hidden_units(inner_f, grad_low, w_units, w_d)

    def pieces(term):
        return term.astype(BF16).reshape(chips, width // chips, -1)

    spans = [slice(tree * chip_rows, (tree + 1) * chip_rows) for tree in range(trees)]
    down_ring = Reduce(ring, [pieces(unit_grads(grad_low, hidden))])
    down_hop = down_ring.hop()
    core_sums = []
    (grad_gate,) = after_all((grad_gate,), (down_ring.terms[0],))
    for tree in range(trees):
        part = back_units(tree, chip_rows, grad_gate, grad_up, w_units)
        (part,) = after_all((part,), down_hop)
        down_hop = down_ring.hop(part)
        (grad_gate,) = after_all((grad_gate,), (part,))
        core_sums.append(core_sum(part))
    lows = [own.astype(BF16) for own in core_sums]
    arrived = [other_half(lows[0])]
    inner_f, hidden = after_all((inner_f, hidden), lows)
    gate_terms = unit_grads(inner_f, grad_gate)
    (grad_up,) = after_all((grad_up,), (gate_terms, *down_hop))
    up_terms = unit_grads(inner_f, grad_up)
    up_terms, arrived[0] = after_all((up_terms, arrived[0]), (gate_terms,))
    arrived.append(other_half(after_all(lows[1:], arrived)[0]))
    gate_sum, up_sum = (
        lax.psum_scatter(terms, "zy", scatter_dimension=0, tiled=True)
        for terms in (gate_terms, up_terms)
    )
    units_hop = down_ring.hop(up_terms)
    arrived[0] = after_all(arrived[:1], (up_terms,))[0]

    grads_middle, grads_low = [], []

    def backward_norm(tree):
        grad_inner = lows[tree].astype(F32) + arrived[tree].astype(F32)
        grad_middle = out_grad[tree].astype(F32) + norm_back(
            grad_inner * gain_f, normeds_f[tree], scales_f[tree]
        )
        low = grad_middle.astype(BF16)
        grads_middle.append(grad_middle)
        grads_low.append(low)
        return jnp.concatenate([low, other_core(low)], axis=0)

    mid_lows, out_lows, out_arrived = [backward_norm(0)], [], []
    kv_rings, grad_queries, grad_kvs = [], [], []
    for tree in range(trees):
        grad_mixed = dot(w_o, mid_lows[tree], 0, 1).astype(BF16)
        for group in range(groups):
            if len(out_lows) > len(out_arrived):
                beside = other_half(out_lows[len(out_arrived)])
                out_arrived.append(beside)
                units_hop += (beside,)
            grad_query, grad_kv = attend_back(
                tree,
                group,
                seens[tree],
                tables[tree][3],
                query,
                masks[tree],
                mixes[tree],
                grad_mixed,
                lses[tree],
                kvs,
                cosine,
                sine,
                rep,
                block,
                grad_kvs[-1] if group else None,
            )
            grad_query, grad_kv = after_all((grad_query, grad_kv), units_hop)
            grad_queries.append(grad_query)
            grad_kvs.append(grad_kv)
            units_hop = ()
            for each in [down_ring] + kv_rings:
                if each.left > 0:
                    units_hop += each.hop(grad_query)
            (grad_mixed,) = after_all((grad_mixed,), (grad_query,))
            if tree == 0 and group == 0:
                (hidden,) = after_all((hidden,), (grad_query,))
                out_parts = [dot(hidden[span], w_d, 1, 1) for span in spans]
                out_parts = after_all(out_parts, arrived[1:])
                out_lows = [core_sum(part).astype(BF16) for part in out_parts]
                (grad_mixed,) = after_all((grad_mixed,), out_lows)
        kv_rings.append(Reduce(ring, grad_kvs[-1:]))
        if tree == 0:
            arrived[-1] = after_all(arrived[-1:], (grad_query,))[0]
            mid_lows.append(backward_norm(1))
            out_terms = pieces(
                dot(jnp.concatenate(mid_lows, axis=0), jnp.concatenate(mixes, axis=1), 0, 1)
            )
            kv_rings[0].hop()
            mid_lows[1] = after_all(mid_lows[1:], (out_terms,))[0]
            units_hop += kv_rings[0].hop(mid_lows[1])
            out_ring = Reduce(ring, [out_terms])
            units_hop += out_ring.hop()
            kv_rings.append(out_ring)
    out_ring = kv_rings.pop(1)
    kv_rings[1].hop()
    (down_sum,) = down_ring.finish()
    gate_sum, up_sum = gate_sum.astype(F32), up_sum.astype(F32)
    outputs = unwritten(out_terms, (trees, rows, width))
    out_arrived = after_all(out_arrived, (grad_queries[-1],))
    for tree in range(trees):
        summed = out_lows[tree].astype(F32) + out_arrived[tree].astype(F32)
        outputs = laid(outputs, (middles[tree] + summed).astype(BF16), tree)

    grads_qkv, gain_a_terms, lows = [], [], []
    (layer_in,) = after_all((layer_in,), (grad_queries[-1],))
    normed_a = layer_in.astype(F32) * scale_a
    down_grad = row_grad(down_sum)
    for tree in range(trees):
        if tree:
            while kv_rings[tree].left > 1:
                kv_rings[tree].hop(*lows)
            arrived = [other_half(lows[0])]
            kv_rings[tree].hop(*arrived)
        (kv_sums,) = kv_rings[tree].finish()
        rows_of = (cosine_rows[spans[tree]], -sine_rows[spans[tree]])
        parts = grad_queries[groups * tree : groups * (tree + 1)]
        for group in range(groups):
            kv_sum = kv_sums[:, 128 * group : 128 * (group + 1)]
            grad_k = kv_sum[:, None, :HEAD_SIZE]
            half = HEAD_SIZE // 2
            first, second = turn(grad_k[..., :half], grad_k[..., half:], *rows_of)
            kv_parts = [first[:, 0], second[:, 0], kv_sum[:, HEAD_SIZE:]]
            parts.append(jnp.concatenate(kv_parts, axis=1).astype(BF16))
        grad_qkv = jnp.concatenate(parts, axis=1)
        grads_qkv.append(grad_qkv)
        own = core_sum(dot(grad_qkv, w_qkv, 1, 1))
        gain_a_terms.append(own)
        lows.append(own.astype(BF16))
    arrived += [other_half(low) for low in lows[1:]]
    (inner_a,) = after_all((inner_a,), lows)
    (out_sum,) = out_ring.finish()
    out_proj_grad = row_grad(out_sum)
    term_qkv = unit_grads(inner_a, jnp.concatenate(grads_qkv, axis=0))
    qkv_ring = Reduce(ring, [pieces(term_qkv)])
    qkv_hop = qkv_ring.hop()
    gate_grad, up_grad = column_grad(gate_sum), column_grad(up_sum)
    core_sums = after_all(core_sums + gain_a_terms, qkv_hop)
    gain_terms = jnp.stack(
        [
            sum(jnp.sum(core_sums[trees + i] * normed_a[i], axis=0) for i in range(trees)),
            sum(jnp.sum(core_sums[i] * normeds_f[i], axis=0) for i in range(trees)),
        ]
    )
    qkv_ring.hop(gain_terms, gate_grad, up_grad, out_proj_grad, down_grad)
    qkv_ring.hop(*arrived)
    (qkv_sum,) = qkv_ring.finish()
    kv_parts = qkv_sum[:, head_cols:].reshape(-1, groups, 2, HEAD_SIZE)
    key_sum, value_sum = (kv_parts[:, :, i].reshape(-1, kv_cols) for i in range(2))

    keep, give = split_by_core(gain_terms.reshape(2, chips, 2, -1), 2)
    gain_sums = gain_sum(ring, jnp.moveaxis(keep + other_core(give), 1, 0))
    gain_sums = (gain_sums + other_half(gain_sums)).reshape(2, -1)
    gain_a_grad, gain_f_grad = gain_sums[0], gain_sums[1]
    input_grad = unwritten(scale_a, (trees, rows, width))
    for tree in range(trees):
        (theirs,) = after_all((arrived[tree],), (gain_terms,) * tree)
        grad_inner = lows[tree].astype(F32) + theirs.astype(F32)
        input_grad = laid(
            input_grad,
            grads_middle[tree] + norm_back(grad_inner * gain_a, normed_a[tree], scale_a[tree]),
            tree,
        )

    return (
        outputs,
        input_grad,
        gain_a_grad,
        column_grad(qkv_sum[:, :head_cols]),
        column_grad(key_sum),
        column_grad(value_sum),
        out_proj_grad,
        gain_f_grad,
        gate_grad,
        up_grad,
        down_grad,
    )


def gain_sum(ring, terms):
    half = ring.count // 2

    def term(offset):
        return lax.dynamic_index_in_dim(terms, ring.chip(offset), 0, keepdims=False)

    rightward, leftward = ring.go_right(term(half)), None
    for step in range(half - 1, 0, -1):
        rightward = ring.go_right(rightward + term(step))
        leftward = ring.go_left(term(-step) if leftward is None else leftward + term(-step))
    total = term(0) + rightward
    return total if leftward is None else total + leftward


def solution(mesh):
    devices = mesh.devices
    mesh = Mesh(devices.reshape(-1, 2, devices.shape[1]), ("zy", "core", "tp"))
    fsdp = ("zy", "core")
    specs = (
        P(fsdp),
        P(fsdp, "tp"),
        P(fsdp, "tp"),
        P(fsdp, "tp"),
        P("tp", fsdp),
        P(fsdp),
        P(fsdp, "tp"),
        P(fsdp, "tp"),
        P("tp", fsdp),
    )
    tokens = P(None, fsdp, None)
    return jax.shard_map(
        shards,
        mesh=mesh,
        in_specs=(tokens, tokens, P(), P()) + specs,
        out_specs=(tokens, tokens) + specs,
        check_vma=False,
    )
```

time: 1750 us -> 1340 us (0.77)
  matrix products: 324 us -> 66.8 us
  Pallas kernels: 98.4 us -> 325 us
  starting transfers between devices: 324 us -> 132 us
  waiting for transfers between devices: 602 us -> 477 us
  local copies, waits for them, and re-layouts: 200 us -> 121 us
    dot_general x27 -> x11, matrix products: 324 us -> 66.8 us  [dot(): lax.dot_general(left, right, (((left_dim,), (right_dim,)), ((), ())), pre...]
    pallas_call x0 -> x14, Pallas kernels: none -> 223 us  [the longest x4 92.1 us: unit_grads(): pl.pallas_call(unit_grads_kernel, grid=(width // rows, units // columns),...]
    ppermute x68 -> x40, starting transfers between devices: 237 us -> 87.6 us  [go_right(): return lax.ppermute(value, 'zy', self.right)]
    ppermute x9, waiting for transfers between devices: 145 us -> 56.7 us  [other_half(): return lax.ppermute(value, 'tp', SWAP)]
    dynamic_update_slice x71 -> x34, local copies, waits for them, and re-layouts: 103 us -> 52.2 us  [put(): return lax.dynamic_update_slice(whole, part[None], at)]
    ppermute x66 -> x39, starting transfers between devices: 69.5 us -> 29 us  [go_left(): return lax.ppermute(value, 'zy', self.left)]
    another operation x13 -> x6, other arithmetic: 29.4 us -> 3.41 us  [the longest x3 19.8 us: shards(): jnp.stack(in_grads)]
    dynamic_update_slice x2 -> x6, other arithmetic: 0.79 us -> 25.9 us  [the longest x4 21.6 us: laid(): return lax.dynamic_update_slice(buffer, value[None], (tree, 0, 0))]
  transfers between devices with their start and end apart: 174 -> 120, of which waited for: 82 -> 51; matrix products, arithmetic and copies ran while one was open for 32% -> 26% of each run, Pallas kernels for 6% -> 16%
where the time goes in v2:
time: 1340 us; the launch traced here: 1330 us
  waiting for transfers between devices  477 us (36%)
  Pallas kernels  325 us (24%)
  other arithmetic  191 us (14%)
  starting transfers between devices  132 us (10%)
  local copies, waits for them, and re-layouts  121 us (9%)
  matrix products  66.8 us (5%)
  between operations  16.8 us (1%)
    ppermute x40, waiting for transfers between devices, go_right(): return lax.ppermute(value, 'zy', self.right)  295 us
    ppermute x39, waiting for transfers between devices, go_left(): return lax.ppermute(value, 'zy', self.left)  121 us
    pallas_call x4, Pallas kernels, unit_grads(): pl.pallas_call(unit_grads_kernel, grid=(width // rows, units // columns),...  92.1 us
    ppermute x40, starting transfers between devices, go_right(): return lax.ppermute(value, 'zy', self.right)  87.6 us
    pallas_call x4, Pallas kernels, attend_back(): pl.pallas_call(functools.partial(attend_back_kernel, block, rep, rows //...  69.1 us
    dot_general x11, matrix products, dot(): lax.dot_general(left, right, (((left_dim,), (right_dim,)), ((), ())), pre...  66.8 us
    pallas_call x1, Pallas kernels, hidden_units(): pl.pallas_call(units_kernel, grid=(tiles, tokens // rows), in_specs=[tall...  66.6 us
    ppermute x9, waiting for transfers between devices, other_half(): return lax.ppermute(value, 'tp', SWAP)  56.7 us
  transfers between devices with their start and end apart: 120, of which 51 were waited for; matrix products, arithmetic and copies ran while one was open for 26% of the time, Pallas kernels for 16%

profile of v2, /device:TPU:0, one launch (start us, length us, event | category | flops | bytes accessed | tf_op | source)
XLA Modules:
  0.0 1328.8 jit_solution(7996775716226601959)
XLA Ops:
  145.6 17.0 %collective-permute-done.15 = bf16[2,1024,256]{2,1,0:T(8,128)(2,1)S(1)} collective-permute-done((bf16[2,1024,256]{2,1,0:T(8,128)(2,1)}, bf16[2,1024,256]{2,1,0:T(8,128)(2,1)S(1)}, u32[]{:S(2)}, u32[]{:S(2)}) %collective-permute-start.15) | collective-permute-done | bytes 1048608 | tf_op jit(solution)/shard_map/ppermute | solution.py:106
  208.6 29.7 %collective-permute-done.24 = bf16[1,1024,256]{2,1,0:T(8,128)(2,1)S(1)} collective-permute-done((bf16[1,1024,256]{2,1,0:T(8,128)(2,1)S(1)}, bf16[1,1024,256]{2,1,0:T(8,128)(2,1)S(1)}, u32[]{:S(2)}, u32[]{:S(2)}) %collective-permute-start.24) | collective-permute-done | bytes 524320 | tf_op jit(solution)/shard_map/ppermute | solution.py:106
  240.3 16.4 %tree_attention.2 = (bf16[512,1024]{1,0:T(8,128)(2,1)S(1)}, f32[2,4,1024]{2,1,0:T(4,128)S(1)}) custom-call(s32[4]{0:T(128)S(1)} %get-tuple-element.444.count_ref, s32[4,34]{1,0:T(4,128)S(1)} %broadcast_add_fusion.1.list_ref, s32[4]{0:T(128)S(1)} %iota_add_fusion.4.diag_ref, bf16[512,2048]{1,0:T(8,128)(2,1)S(1)} %get-tuple-element.139.query_ref, ...), custom_call_target="tpu_custom_call" | custom-call | flops 1048576 | bytes 1024 | tf_op jit(solution)/shard_map/tree_attention/pallas_call | solution.py:329
  295.8 16.4 %tree_attention.3 = (bf16[512,1024]{1,0:T(8,128)(2,1)S(1)}, f32[2,4,1024]{2,1,0:T(4,128)S(1)}) custom-call(s32[4]{0:T(128)S(1)} %get-tuple-element.445.count_ref, s32[4,34]{1,0:T(4,128)S(1)} %broadcast_add_fusion.list_ref, s32[4]{0:T(128)S(1)} %iota_add_fusion.4.diag_ref, bf16[512,2048]{1,0:T(8,128)(2,1)S(1)} %get-tuple-element.139.query_ref, ...), custom_call_target="tpu_custom_call" | custom-call | flops 1048576 | bytes 1024 | tf_op jit(solution)/shard_map/tree_attention/pallas_call | solution.py:329
  327.3 20.4 %collective-permute-done.30 = bf16[256,4096]{1,0:T(8,128)(2,1)} collective-permute-done((bf16[256,4096]{1,0:T(8,128)(2,1)}, bf16[256,4096]{1,0:T(8,128)(2,1)}, u32[]{:S(2)}, u32[]{:S(2)}) %collective-permute-start.30) | collective-permute-done | bytes 2097184 | tf_op jit(solution)/shard_map/ppermute | solution.py:109
  368.5 34.7 %collective-permute-done.36 = bf16[256,4096]{1,0:T(8,128)(2,1)S(1)} collective-permute-done((bf16[256,4096]{1,0:T(8,128)(2,1)}, bf16[256,4096]{1,0:T(8,128)(2,1)S(1)}, u32[]{:S(2)}, u32[]{:S(2)}) %collective-permute-start.36) | collective-permute-done | bytes 2097184 | tf_op jit(solution)/shard_map/ppermute | solution.py:106
  403.2 16.9 %collective-permute-done.37 = bf16[256,4096]{1,0:T(8,128)(2,1)S(1)} collective-permute-done((bf16[256,4096]{1,0:T(8,128)(2,1)}, bf16[256,4096]{1,0:T(8,128)(2,1)S(1)}, u32[]{:S(2)}, u32[]{:S(2)}) %collective-permute-start.37) | collective-permute-done | bytes 2097184 | tf_op jit(solution)/shard_map/ppermute | solution.py:109
  428.9 17.4 %collective-permute-done.40 = bf16[256,2048]{1,0:T(8,128)(2,1)S(1)} collective-permute-done((bf16[256,2048]{1,0:T(8,128)(2,1)S(1)}, bf16[256,2048]{1,0:T(8,128)(2,1)S(1)}, u32[]{:S(2)}, u32[]{:S(2)}) %collective-permute-start.40) | collective-permute-done | bytes 1048608 | tf_op jit(solution)/shard_map/ppermute | solution.py:106
  447.4 19.2 %collective-permute-done.38 = bf16[128,4096]{1,0:T(8,128)(2,1)S(1)} collective-permute-done((bf16[128,4096]{1,0:T(8,128)(2,1)S(1)}, bf16[128,4096]{1,0:T(8,128)(2,1)S(1)}, u32[]{:S(2)}, u32[]{:S(2)}) %collective-permute-start.38) | collective-permute-done | bytes 1048608 | tf_op jit(solution)/shard_map/ppermute | solution.py:106
  527.2 66.6 %hidden_units.1 = (bf16[2048,2048]{1,0:T(8,128)(2,1)}, bf16[2048,2048]{1,0:T(8,128)(2,1)}, bf16[2048,2048]{1,0:T(8,128)(2,1)}) custom-call(bf16[2048,2048]{1,0:T(8,128)(2,1)} %pad_maximum_fusion.1.inner_ref.rows_ref, bf16[2048,2048]{1,0:T(8,128)(2,1)} %bitcast.465, bf16[2048,4096]{1,0:T(8,128)(2,1)} %bitcast.457, bf16[2048,4096]{1,0:T(8,128)(2,1)} %bitcast.458, ...), custom_call_target="tpu_custom_call" | custom-call | flops 1048576 | bytes 1024 | tf_op jit(solution)/shard_map/hidden_units/pallas_call | solution.py:590
  593.8 25.3 %unit_grads.4 = bf16[2048,2048]{1,0:T(8,128)(2,1)} custom-call(bf16[2048,2048]{1,0:T(8,128)(2,1)} %bitcast.466, bf16[2048,2048]{1,0:T(8,128)(2,1)} %get-tuple-element.178.grad_ref), custom_call_target="tpu_custom_call" | custom-call | flops 1048576 | bytes 1024 | tf_op jit(solution)/shard_map/unit_grads/pallas_call | solution.py:644
  623.0 23.8 %back_units.2 = bf16[1024,2048]{1,0:T(8,128)(2,1)} custom-call(bf16[2048,2048]{1,0:T(8,128)(2,1)} %get-tuple-element.162.grad_gate_ref.grad_ref, bf16[2048,2048]{1,0:T(8,128)(2,1)} %get-tuple-element.165.grad_up_ref.grad_ref, bf16[2048,4096]{1,0:T(8,128)(2,1)} %bitcast.459, bf16[2048,4096]{1,0:T(8,128)(2,1)} %bitcast.460), custom_call_target="tpu_custom_call" | custom-call | flops 1048576 | bytes 1024 | tf_op jit(solution)/shard_map/back_units/pallas_call | solution.py:615
  654.0 23.8 %back_units.3 = bf16[1024,2048]{1,0:T(8,128)(2,1)} custom-call(bf16[2048,2048]{1,0:T(8,128)(2,1)} %get-tuple-element.162.grad_gate_ref.grad_ref, bf16[2048,2048]{1,0:T(8,128)(2,1)} %get-tuple-element.165.grad_up_ref.grad_ref, bf16[2048,4096]{1,0:T(8,128)(2,1)} %bitcast.461, bf16[2048,4096]{1,0:T(8,128)(2,1)} %bitcast.462), custom_call_target="tpu_custom_call" | custom-call | flops 1048576 | bytes 1024 | tf_op jit(solution)/shard_map/back_units/pallas_call | solution.py:615
  694.8 26.1 %unit_grads.5 = bf16[2048,2048]{1,0:T(8,128)(2,1)} custom-call(bf16[2048,2048]{1,0:T(8,128)(2,1)} %pad_maximum_fusion.1.inner_ref.rows_ref, bf16[2048,2048]{1,0:T(8,128)(2,1)} %get-tuple-element.162.grad_gate_ref.grad_ref), custom_call_target="tpu_custom_call" | custom-call | flops 1048576 | bytes 1024 | tf_op jit(solution)/shard_map/unit_grads/pallas_call | solution.py:644
  721.1 25.3 %unit_grads.6 = bf16[2048,2048]{1,0:T(8,128)(2,1)} custom-call(bf16[2048,2048]{1,0:T(8,128)(2,1)} %pad_maximum_fusion.1.inner_ref.rows_ref, bf16[2048,2048]{1,0:T(8,128)(2,1)} %get-tuple-element.165.grad_up_ref.grad_ref), custom_call_target="tpu_custom_call" | custom-call | flops 1048576 | bytes 1024 | tf_op jit(solution)/shard_map/unit_grads/pallas_call | solution.py:644
  770.2 17.3 %tree_attention_back.4 = (bf16[1024,256]{1,0:T(8,128)(2,1)}, bf16[8,1024,256]{2,1,0:T(8,128)(2,1)}) custom-call(s32[4,32]{1,0:T(4,128)} %get-tuple-element.443.seen_ref, bf16[512,2048]{1,0:T(8,128)(2,1)} %copy-done, bf16[16,1024]{1,0:T(8,128)(2,1)} %copy-done.9, bf16[512,1024]{1,0:T(8,128)(2,1)} %copy-done.7, bf16[512,1024]{1,0:T(8,128)(2,1)} %fusion.41.grad_ref, ...), custom_call_target="tpu_custom_call" | custom-call | flops 1048576 | bytes 1024 | tf_op jit(solution)/shard_map/tree_attention_back/pallas_call | solution.py:468
  787.5 20.8 %collective-permute-done.59 = bf16[256,2048]{1,0:T(8,128)(2,1)S(1)} collective-permute-done((bf16[256,2048]{1,0:T(8,128)(2,1)}, bf16[256,2048]{1,0:T(8,128)(2,1)S(1)}, u32[]{:S(2)}, u32[]{:S(2)}) %collective-permute-start.59) | collective-permute-done | bytes 1048608 | tf_op jit(solution)/shard_map/ppermute | solution.py:106
  861.3 17.7 %tree_attention_back.5 = (bf16[1024,256]{1,0:T(8,128)(2,1)}, bf16[8,1024,256]{2,1,0:T(8,128)(2,1)}) custom-call(s32[4,32]{1,0:T(4,128)} %get-tuple-element.443.seen_ref, bf16[512,2048]{1,0:T(8,128)(2,1)} %copy-done, bf16[16,1024]{1,0:T(8,128)(2,1)} %copy-done.9, bf16[512,1024]{1,0:T(8,128)(2,1)} %copy-done.7, ...), custom_call_target="tpu_custom_call", output_to_operand_aliasing={{1}: (10, {})} | custom-call | flops 1048576 | bytes 1024 | tf_op jit(solution)/shard_map/tree_attention_back/pallas_call | solution.py:468
  879.1 26.8 %collective-permute-done.63 = bf16[512,2048]{1,0:T(8,128)(2,1)} collective-permute-done((bf16[512,2048]{1,0:T(8,128)(2,1)}, bf16[512,2048]{1,0:T(8,128)(2,1)}, u32[]{:S(2)}, u32[]{:S(2)}) %collective-permute-start.63) | collective-permute-done | bytes 2097184 | tf_op jit(solution)/shard_map/ppermute | solution.py:199
  942.5 17.1 %tree_attention_back.6 = (bf16[1024,256]{1,0:T(8,128)(2,1)}, bf16[8,1024,256]{2,1,0:T(8,128)(2,1)}) custom-call(s32[4,32]{1,0:T(4,128)} %get-tuple-element.442.seen_ref, bf16[512,2048]{1,0:T(8,128)(2,1)} %copy-done, bf16[16,1024]{1,0:T(8,128)(2,1)} %copy-done.10, bf16[512,1024]{1,0:T(8,128)(2,1)} %copy-done.5, ...), custom_call_target="tpu_custom_call" | custom-call | flops 1048576 | bytes 1024 | tf_op jit(solution)/shard_map/tree_attention_back/pallas_call | solution.py:468
  987.7 17.1 %tree_attention_back.7 = (bf16[1024,256]{1,0:T(8,128)(2,1)}, bf16[8,1024,256]{2,1,0:T(8,128)(2,1)}) custom-call(s32[4,32]{1,0:T(4,128)} %get-tuple-element.442.seen_ref, bf16[512,2048]{1,0:T(8,128)(2,1)} %copy-done, bf16[16,1024]{1,0:T(8,128)(2,1)} %copy-done.10, bf16[512,1024]{1,0:T(8,128)(2,1)} %copy-done.5, ...), custom_call_target="tpu_custom_call", output_to_operand_aliasing={{1}: (10, {})} | custom-call | flops 1048576 | bytes 1024 | tf_op jit(solution)/shard_map/tree_attention_back/pallas_call | solution.py:468
  1004.7 18.9 %collective-permute-done.75 = bf16[256,512]{1,0:T(8,128)(2,1)S(1)} collective-permute-done((bf16[256,512]{1,0:T(8,128)(2,1)S(1)}, bf16[256,512]{1,0:T(8,128)(2,1)S(1)}, u32[]{:S(2)}, u32[]{:S(2)}) %collective-permute-start.75) | collective-permute-done | bytes 262176 | tf_op jit(solution)/shard_map/ppermute | solution.py:109
  1030.6 16.4 %collective-permute-done.76 = bf16[1024,256]{1,0:T(8,128)(2,1)S(1)} collective-permute-done((bf16[1024,256]{1,0:T(8,128)(2,1)S(1)}, bf16[1024,256]{1,0:T(8,128)(2,1)S(1)}, u32[]{:S(2)}, u32[]{:S(2)}) %collective-permute-start.76) | collective-permute-done | bytes 524320 | tf_op jit(solution)/shard_map/ppermute | solution.py:106
  1260.8 27.5 %collective-permute-done.100 = f32[2,1,128]{2,1,0:T(1,128)S(1)} collective-permute-done((f32[2,1,128]{2,1,0:T(1,128)S(1)}, f32[2,1,128]{2,1,0:T(1,128)S(1)}, u32[]{:S(2)}, u32[]{:S(2)}) %collective-permute-start.100) | collective-permute-done | bytes 1056 | tf_op jit(solution)/shard_map/ppermute | solution.py:199
  (720 shorter events, 753.6 us)
Async XLA Ops:
  7.2 1176.3 %reduce-scatter.3.cloned.1.call-start = ((), (), s32[]{:S(2)}) async-start(), calls=%async_computation.2 | async-start | bytes 9437184 | tf_op jit(solution)/shard_map/reduce_scatter | solution.py:880
  20.7 78.5 %collective-permute-start.5 = (bf16[2,512,2048]{2,1,0:T(8,128)(2,1)}, bf16[2,512,2048]{2,1,0:T(8,128)(2,1)}, u32[]{:S(2)}, u32[]{:S(2)}) collective-permute-start(bf16[2,512,2048]{2,1,0:T(8,128)(2,1)} %own_ref), channel_id=1, source_target_pairs={{0,2},{2,0},{1,3},{3,1},{4,6},{6,4},{5,7},{7,5},{8,10},{10,8},{9,1... | collective-permute-start | bytes 12582920 | tf_op jit(solution)/shard_map/ppermute | solution.py:195
  122.4 68.8 %collective-permute-start.20 = (bf16[2,512,2048]{2,1,0:T(8,128)(2,1)}, bf16[2,512,2048]{2,1,0:T(8,128)(2,1)}, u32[]{:S(2)}, u32[]{:S(2)}) collective-permute-start(bf16[2,512,2048]{2,1,0:T(8,128)(2,1)} %param.14), channel_id=1, source_target_pairs={{0,2},{2,0},{1,3},{3,1},{4,6},{6,4},{5,7},{7,5},{8,10},{10,8},{9,1... | collective-permute-start | bytes 12582920 | tf_op jit(solution)/shard_map/ppermute | solution.py:195
  186.5 70.2 %collective-permute-start.26 = (bf16[256,4096]{1,0:T(8,128)(2,1)}, bf16[256,4096]{1,0:T(8,128)(2,1)}, u32[]{:S(2)}, u32[]{:S(2)}) collective-permute-start(bf16[256,4096]{1,0:T(8,128)(2,1)} %maximum_maximum_fusion.like_ref), channel_id=1, source_target_pairs={{0,8},{8,16},{16,24},{24,28},{28,20},{20,12},{12,4},{4,0},{1,9},{9... | collective-permute-start | bytes 6291464 | tf_op jit(solution)/shard_map/ppermute | solution.py:106
  187.6 69.2 %collective-permute-start.27 = (bf16[256,4096]{1,0:T(8,128)(2,1)}, bf16[256,4096]{1,0:T(8,128)(2,1)}, u32[]{:S(2)}, u32[]{:S(2)}) collective-permute-start(bf16[256,4096]{1,0:T(8,128)(2,1)} %maximum_maximum_fusion.like_ref), channel_id=1, source_target_pairs={{8,0},{16,8},{24,16},{28,24},{20,28},{12,20},{4,12},{0,4},{9,1},{1... | collective-permute-start | bytes 6291464 | tf_op jit(solution)/shard_map/ppermute | solution.py:109
  265.2 62.1 %collective-permute-start.29 = (bf16[256,4096]{1,0:T(8,128)(2,1)}, bf16[256,4096]{1,0:T(8,128)(2,1)}, u32[]{:S(2)}, u32[]{:S(2)}) collective-permute-start(bf16[256,4096]{1,0:T(8,128)(2,1)} %collective-permute-done.26), channel_id=1, source_target_pairs={{0,8},{8,16},{16,24},{24,28},{28,20},{20,12},{12,4},{4,0},{1,9},{9... | collective-permute-start | bytes 6291464 | tf_op jit(solution)/shard_map/ppermute | solution.py:106
  281.5 66.3 %collective-permute-start.30 = (bf16[256,4096]{1,0:T(8,128)(2,1)}, bf16[256,4096]{1,0:T(8,128)(2,1)}, u32[]{:S(2)}, u32[]{:S(2)}) collective-permute-start(bf16[256,4096]{1,0:T(8,128)(2,1)} %collective-permute-done.27), channel_id=1, source_target_pairs={{8,0},{16,8},{24,16},{28,24},{20,28},{12,20},{4,12},{0,4},{9,1},{1... | collective-permute-start | bytes 6291464 | tf_op jit(solution)/shard_map/ppermute | solution.py:109
  286.5 61.2 %collective-permute-start.31 = (bf16[512,2048]{1,0:T(8,128)(2,1)}, bf16[512,2048]{1,0:T(8,128)(2,1)}, u32[]{:S(2)}, u32[]{:S(2)}) collective-permute-start(bf16[512,2048]{1,0:T(8,128)(2,1)} %fusion.13), channel_id=1, source_target_pairs={{0,1},{1,0},{2,3},{3,2},{4,5},{5,4},{6,7},{7,6},{8,9},{9,8},{10,11... | collective-permute-start | bytes 6291464 | tf_op jit(solution)/shard_map/ppermute | solution.py:199
  351.7 51.5 %collective-permute-start.36 = (bf16[256,4096]{1,0:T(8,128)(2,1)}, bf16[256,4096]{1,0:T(8,128)(2,1)S(1)}, u32[]{:S(2)}, u32[]{:S(2)}) collective-permute-start(bf16[256,4096]{1,0:T(8,128)(2,1)} %collective-permute-done.29), channel_id=1, source_target_pairs={{0,8},{8,16},{16,24},{24,28},{28,20},{20,12},{12,4},{4,0},{1,9},{9... | collective-permute-start | bytes 6291464 | tf_op jit(solution)/shard_map/ppermute | solution.py:106
  358.5 61.6 %collective-permute-start.37 = (bf16[256,4096]{1,0:T(8,128)(2,1)}, bf16[256,4096]{1,0:T(8,128)(2,1)S(1)}, u32[]{:S(2)}, u32[]{:S(2)}) collective-permute-start(bf16[256,4096]{1,0:T(8,128)(2,1)} %collective-permute-done.30), channel_id=1, source_target_pairs={{8,0},{16,8},{24,16},{28,24},{20,28},{12,20},{4,12},{0,4},{9,1},{1... | collective-permute-start | bytes 6291464 | tf_op jit(solution)/shard_map/ppermute | solution.py:109
  358.8 63.4 %collective-permute-start.32 = (bf16[512,2048]{1,0:T(8,128)(2,1)S(1)}, bf16[512,2048]{1,0:T(8,128)(2,1)S(1)}, u32[]{:S(2)}, u32[]{:S(2)}) collective-permute-start(bf16[512,2048]{1,0:T(8,128)(2,1)S(1)} %slice.802), channel_id=1, source_target_pairs={{0,2},{2,0},{1,3},{3,1},{4,6},{6,4},{5,7},{7,5},{8,10},{10,8},{9,1... | collective-permute-start | bytes 6291464 | tf_op jit(solution)/shard_map/ppermute | solution.py:195
  425.5 54.6 %collective-permute-start.39 = (bf16[128,4096]{1,0:T(8,128)(2,1)S(1)}, bf16[128,4096]{1,0:T(8,128)(2,1)S(1)}, u32[]{:S(2)}, u32[]{:S(2)}) collective-permute-start(bf16[128,4096]{1,0:T(8,128)(2,1)S(1)} %slice.570), channel_id=1, source_target_pairs={{8,0},{16,8},{24,16},{28,24},{20,28},{12,20},{4,12},{0,4},{9,1},{1... | collective-permute-start | bytes 3145736 | tf_op jit(solution)/shard_map/ppermute | solution.py:109
  684.9 61.5 %collective-permute-start.56 = (bf16[512,2048]{1,0:T(8,128)(2,1)}, bf16[512,2048]{1,0:T(8,128)(2,1)}, u32[]{:S(2)}, u32[]{:S(2)}) collective-permute-start(bf16[512,2048]{1,0:T(8,128)(2,1)} %get-tuple-element.314), channel_id=1, source_target_pairs={{0,1},{1,0},{2,3},{3,2},{4,5},{5,4},{6,7},{7,6},{8,9},{9,8},{10,11... | collective-permute-start | bytes 6291464 | tf_op jit(solution)/shard_map/ppermute | solution.py:199
  720.9 508.8 %reduce-scatter.5.cloned.1.call-start = ((), (), s32[]{:S(2)}) async-start(), calls=%async_computation.3 | async-start | bytes 9437184 | tf_op jit(solution)/shard_map/reduce_scatter | solution.py:880
  761.2 47.1 %collective-permute-start.59 = (bf16[256,2048]{1,0:T(8,128)(2,1)}, bf16[256,2048]{1,0:T(8,128)(2,1)S(1)}, u32[]{:S(2)}, u32[]{:S(2)}) collective-permute-start(bf16[256,2048]{1,0:T(8,128)(2,1)} %get-tuple-element.302), channel_id=1, source_target_pairs={{0,8},{8,16},{16,24},{24,28},{28,20},{20,12},{12,4},{4,0},{1,9},{9... | collective-permute-start | bytes 3145736 | tf_op jit(solution)/shard_map/ppermute | solution.py:106
  762.3 56.1 %collective-permute-start.60 = (bf16[256,2048]{1,0:T(8,128)(2,1)}, bf16[256,2048]{1,0:T(8,128)(2,1)}, u32[]{:S(2)}, u32[]{:S(2)}) collective-permute-start(bf16[256,2048]{1,0:T(8,128)(2,1)} %get-tuple-element.301), channel_id=1, source_target_pairs={{8,0},{16,8},{24,16},{28,24},{20,28},{12,20},{4,12},{0,4},{9,1},{1... | collective-permute-start | bytes 3145736 | tf_op jit(solution)/shard_map/ppermute | solution.py:109
  763.2 82.9 %collective-permute-start.58 = (bf16[512,2048]{1,0:T(8,128)(2,1)S(1)}, bf16[512,2048]{1,0:T(8,128)(2,1)S(1)}, u32[]{:S(2)}, u32[]{:S(2)}) collective-permute-start(bf16[512,2048]{1,0:T(8,128)(2,1)S(1)} %get-tuple-element.169), channel_id=1, source_target_pairs={{0,1},{1,0},{2,3},{3,2},{4,5},{5,4},{6,7},{7,6},{8,9},{9,8},{10,11... | collective-permute-start | bytes 6291464 | tf_op jit(solution)/shard_map/ppermute | solution.py:199
  857.8 48.0 %collective-permute-start.63 = (bf16[512,2048]{1,0:T(8,128)(2,1)}, bf16[512,2048]{1,0:T(8,128)(2,1)}, u32[]{:S(2)}, u32[]{:S(2)}) collective-permute-start(bf16[512,2048]{1,0:T(8,128)(2,1)} %add_convert_fusion.3), channel_id=1, source_target_pairs={{0,1},{1,0},{2,3},{3,2},{4,5},{5,4},{6,7},{7,6},{8,9},{9,8},{10,11... | collective-permute-start | bytes 6291464 | tf_op jit(solution)/shard_map/ppermute | solution.py:199
  912.5 48.4 %collective-permute-start.65 = (bf16[512,2048]{1,0:T(8,128)(2,1)}, bf16[512,2048]{1,0:T(8,128)(2,1)}, u32[]{:S(2)}, u32[]{:S(2)}) collective-permute-start(bf16[512,2048]{1,0:T(8,128)(2,1)} %add_convert_fusion.2), channel_id=1, source_target_pairs={{0,1},{1,0},{2,3},{3,2},{4,5},{5,4},{6,7},{7,6},{8,9},{9,8},{10,11... | collective-permute-start | bytes 6291464 | tf_op jit(solution)/shard_map/ppermute | solution.py:199
  975.8 47.9 %collective-permute-start.72 = (bf16[1024,256]{1,0:T(8,128)(2,1)S(1)}, bf16[1024,256]{1,0:T(8,128)(2,1)S(1)}, u32[]{:S(2)}, u32[]{:S(2)}) collective-permute-start(bf16[1024,256]{1,0:T(8,128)(2,1)S(1)} %get-tuple-element.328), channel_id=1, source_target_pairs={{0,8},{8,16},{16,24},{24,28},{28,20},{20,12},{12,4},{4,0},{1,9},{9... | collective-permute-start | bytes 1572872 | tf_op jit(solution)/shard_map/ppermute | solution.py:106
  975.8 47.8 %collective-permute-start.73 = (bf16[1024,256]{1,0:T(8,128)(2,1)S(1)}, bf16[1024,256]{1,0:T(8,128)(2,1)S(1)}, u32[]{:S(2)}, u32[]{:S(2)}) collective-permute-start(bf16[1024,256]{1,0:T(8,128)(2,1)S(1)} %get-tuple-element.327), channel_id=1, source_target_pairs={{8,0},{16,8},{24,16},{28,24},{20,28},{12,20},{4,12},{0,4},{9,1},{1... | collective-permute-start | bytes 1572872 | tf_op jit(solution)/shard_map/ppermute | solution.py:109
  1068.4 64.7 %collective-permute-start.79 = (bf16[512,2048]{1,0:T(8,128)(2,1)S(1)}, bf16[512,2048]{1,0:T(8,128)(2,1)}, u32[]{:S(2)}, u32[]{:S(2)}) collective-permute-start(bf16[512,2048]{1,0:T(8,128)(2,1)S(1)} %get-tuple-element.289), channel_id=1, source_target_pairs={{0,1},{1,0},{2,3},{3,2},{4,5},{5,4},{6,7},{7,6},{8,9},{9,8},{10,11... | collective-permute-start | bytes 6291464 | tf_op jit(solution)/shard_map/ppermute | solution.py:199
  1070.0 48.7 %collective-permute-start.108 = (f32[128,2048]{1,0:T(8,128)}, f32[128,2048]{1,0:T(8,128)}, u32[]{:S(2)}, u32[]{:S(2)}) collective-permute-start(f32[128,2048]{1,0:T(8,128)} %constant_dynamic-slice_fusion.7), channel_id=1, source_target_pairs={{0,2},{2,0},{1,3},{3,1},{4,6},{6,4},{5,7},{7,5},{8,10},{10,8},{9,1... | collective-permute-start | bytes 3145736 | tf_op jit(solution)/shard_map/ppermute | solution.py:195
  1242.0 46.9 %collective-permute-start.89 = (bf16[512,2048]{1,0:T(8,128)(2,1)}, bf16[512,2048]{1,0:T(8,128)(2,1)}, u32[]{:S(2)}, u32[]{:S(2)}) collective-permute-start(bf16[512,2048]{1,0:T(8,128)(2,1)} %get-tuple-element.285), channel_id=1, source_target_pairs={{0,1},{1,0},{2,3},{3,2},{4,5},{5,4},{6,7},{7,6},{8,9},{9,8},{10,11... | collective-permute-start | bytes 6291464 | tf_op jit(solution)/shard_map/ppermute | solution.py:199
  (195 other events, 3841.9 us)
Sparse Core Ops, SparseCore 0:
  721.0 167.5 reduce-scatter.2
  912.6 196.1 reduce-scatter.4

commit v3 on v2

--- a/solution.py
+++ b/solution.py
@@ -114,8 +114,8 @@
 
 
 class Gather:
-    def __init__(self, ring, pieces):
-        self.ring, self.step = ring, 0
+    def __init__(self, ring, pieces, tidy=False):
+        self.ring, self.step, self.tidy, self.laid = ring, 0, tidy, ()
         self.cuts = [piece.shape[0] // 2 for piece in pieces]
         wholes = [unwritten(piece, (ring.count,) + piece.shape) for piece in pieces]
         self.wholes = [ring.put(whole, piece, 0) for whole, piece in zip(wholes, pieces)]
@@ -123,9 +123,10 @@
 
     def hop(self, *others):
         ring, count = self.ring, len(self.cuts)
-        both = after_all(self.rightward + self.leftward, others)
+        both = after_all(self.rightward + self.leftward, others + self.laid)
         rightward, leftward = both[:count], both[count:]
         self.step += 1
+        self.laid = tuple(self.wholes) if self.tidy else ()
         far = self.step == ring.count // 2
         if far:
             rightward = [part[:cut] for part, cut in zip(rightward, self.cuts)]
@@ -577,84 +578,227 @@
     grad_up_ref[...] = (grad_hidden * activated).astype(BF16)
 
 
-def hidden_units(inner, grad, gate_up, down):
+def hidden_units(inner, grad, weights, down):
     tokens, width = inner.shape
     units = down.shape[1]
     rows, columns = math.gcd(tokens, 512), math.gcd(units, 512)
     tiles = units // columns
     tall = pl.BlockSpec((rows, width), lambda j, i: (i, 0))
-    wide = pl.BlockSpec((width, columns), lambda j, i: (0, j))
-    second = pl.BlockSpec((width, columns), lambda j, i: (0, tiles + j))
+    wide = [
+        pl.BlockSpec((width, columns), lambda j, i, first=first: (0, first + j))
+        for first in (0, tiles, 0)
+    ]
     tile = pl.BlockSpec((rows, columns), lambda j, i: (i, j))
     made = jax.ShapeDtypeStruct((tokens, units), BF16)
     return pl.pallas_call(
         units_kernel,
         grid=(tiles, tokens // rows),
-        in_specs=[tall, tall, wide, second, wide],
+        in_specs=[tall, tall, *wide],
         out_specs=[tile, tile, tile],
         out_shape=[made, made, made],
         compiler_params=pltpu.CompilerParams(vmem_limit_bytes=56 * 2**20),
         cost_estimate=SMALL,
         name="hidden_units",
-    )(inner, grad, gate_up, gate_up, down)
-
-
-def back_units_kernel(grad_gate_ref, grad_up_ref, gate_ref, up_ref, out_ref):
+    )(inner, grad, weights, weights, down)
+
+
+def back_units_kernel(count, *refs):
+    *refs, out_ref = refs
     contract = (((1,), (1,)), ((), ()))
-    out_ref[...] = (
-        lax.dot_general(grad_gate_ref[...], gate_ref[...], contract, preferred_element_type=F32)
-        + lax.dot_general(grad_up_ref[...], up_ref[...], contract, preferred_element_type=F32)
-    ).astype(BF16)
-
-
-def back_units(tree, tokens, grad_gate, grad_up, gate_up):
-    width, units = gate_up.shape[0], grad_up.shape[1]
+    total = None
+    for units_ref, weight_ref in zip(refs[:count], refs[count:]):
+        term = lax.dot_general(
+            units_ref[...], weight_ref[...], contract, preferred_element_type=F32
+        )
+        total = term if total is None else total + term
+    out_ref[...] = total.astype(BF16)
+
+
+def back_units(tree, tokens, units, weights, places):
+    width, size = weights.shape[0], units[0].shape[1]
     rows, columns = math.gcd(tokens, 1024), math.gcd(width, 512)
     first = tree * (tokens // rows)
-    tall = pl.BlockSpec((rows, units), lambda j, i: (first + i, 0))
+    tall = pl.BlockSpec((rows, size), lambda j, i: (first + i, 0))
     return pl.pallas_call(
-        back_units_kernel,
+        functools.partial(back_units_kernel, len(units)),
         grid=(width // columns, tokens // rows),
-        in_specs=[
-            tall,
-            tall,
-            pl.BlockSpec((columns, units), lambda j, i: (j, 0)),
-            pl.BlockSpec((columns, units), lambda j, i: (j, 1)),
-        ],
+        in_specs=[tall] * len(units)
+        + [pl.BlockSpec((columns, size), lambda j, i, at=at: (j, at)) for at in places],
         out_specs=pl.BlockSpec((rows, columns), lambda j, i: (i, j)),
         out_shape=jax.ShapeDtypeStruct((tokens, width), BF16),
         compiler_params=pltpu.CompilerParams(vmem_limit_bytes=56 * 2**20),
         cost_estimate=SMALL,
         name="back_units",
-    )(grad_gate, grad_up, gate_up, gate_up)
-
-
-def unit_grads_kernel(rows_ref, grad_ref, out_ref, turned):
-    @pl.when(pl.program_id(1) == 0)
+    )(*units, *([weights] * len(units)))
+
+
+def unit_grads_kernel(tiles, rows_ref, *refs):
+    *grad_refs, out_ref, turned = refs
+    at = pl.program_id(1)
+
+    @pl.when(at == 0)
     def _():
         turned[...] = rows_ref[...].T
 
-    out_ref[...] = jnp.dot(turned[...], grad_ref[...], preferred_element_type=F32).astype(BF16)
-
-
-def unit_grads(rows_in, grad):
+    for i, grad_ref in enumerate(grad_refs):
+
+        @pl.when((at >= i * tiles) & (at < (i + 1) * tiles))
+        def _():
+            out_ref[...] = jnp.dot(
+                turned[...], grad_ref[...], preferred_element_type=F32
+            ).astype(BF16)
+
+
+def unit_grads(rows_in, *grads):
     tokens, width = rows_in.shape
-    units = grad.shape[1]
-    rows, columns = math.gcd(width, 1024), math.gcd(units, 1024)
+    units = grads[0].shape[1]
+    rows, columns = math.gcd(width, 1024), math.gcd(units, 1024 // len(grads))
+    tiles = units // columns
+
+    def place(i):
+        return lambda at, j: (0, jnp.clip(j - i * tiles, 0, tiles - 1))
+
     return pl.pallas_call(
-        unit_grads_kernel,
-        grid=(width // rows, units // columns),
-        in_specs=[
-            pl.BlockSpec((tokens, rows), lambda i, j: (0, i)),
-            pl.BlockSpec((tokens, columns), lambda i, j: (0, j)),
-        ],
+        functools.partial(unit_grads_kernel, tiles),
+        grid=(width // rows, tiles * len(grads)),
+        in_specs=[pl.BlockSpec((tokens, rows), lambda i, j: (0, i))]
+        + [pl.BlockSpec((tokens, columns), place(i)) for i in range(len(grads))],
         out_specs=pl.BlockSpec((rows, columns), lambda i, j: (i, j)),
-        out_shape=jax.ShapeDtypeStruct((width, units), BF16),
+        out_shape=jax.ShapeDtypeStruct((width, units * len(grads)), BF16),
         scratch_shapes=[pltpu.VMEM((rows, tokens), BF16)],
         compiler_params=pltpu.CompilerParams(vmem_limit_bytes=56 * 2**20),
         cost_estimate=SMALL,
         name="unit_grads",
-    )(rows_in, grad)
+    )(rows_in, *grads)
+
+
+def ring_place(spot, count):
+    spot = lax.rem(spot + count, count)
+    return jnp.where(spot < count // 2, 2 * spot, 2 * (count - 1 - spot) + 1)
+
+
+def ring_sum_kernel(count, arrays, swaps, *refs):
+    terms_refs, refs = refs[:arrays], refs[arrays:]
+    if swaps:
+        swap_ref, *refs, swap_send, swap_receive = refs
+    out_refs, refs = refs[:arrays], refs[arrays:]
+    if swaps:
+        theirs_ref, *refs = refs
+    helds, from_lefts, from_rights = (refs[i * arrays : (i + 1) * arrays] for i in range(3))
+    load_sems, send_sems, receive_sems = refs[3 * arrays :]
+    half = count // 2
+    me = lax.axis_index("zy")
+    spot = jnp.where(lax.rem(me, 2) == 0, lax.div(me, 2), count - 1 - lax.div(me, 2))
+    right, left = ring_place(spot + 1, count), ring_place(spot - 1, count)
+
+    barrier = pltpu.get_barrier_semaphore()
+    for neighbour in (right, left):
+        pl.semaphore_signal(
+            barrier, inc=1, device_id={"zy": neighbour}, device_id_type=pl.DeviceIdType.MESH
+        )
+    other = {"tp": 1 - lax.axis_index("tp")}
+    if swaps:
+        pl.semaphore_signal(
+            barrier, inc=1, device_id=other, device_id_type=pl.DeviceIdType.MESH
+        )
+    order = [half]
+    for step in range(half - 1, 0, -1):
+        order += [step, count - step]
+    order.append(0)
+    loads = {}
+    for k in order:
+        for i in range(arrays):
+            loads[i, k] = pltpu.make_async_copy(
+                terms_refs[i].at[ring_place(spot + k, count)], helds[i].at[k], load_sems.at[i, k]
+            )
+            loads[i, k].start()
+    pl.semaphore_wait(barrier, 3 if swaps else 2)
+    if swaps:
+        swap = pltpu.make_async_remote_copy(
+            src_ref=swap_ref,
+            dst_ref=theirs_ref,
+            send_sem=swap_send,
+            recv_sem=swap_receive,
+            device_id=other,
+            device_id_type=pl.DeviceIdType.MESH,
+        )
+        swap.start()
+
+    copies = {}
+
+    def send(i, hop, way, source, target):
+        copies[i, hop, way] = pltpu.make_async_remote_copy(
+            src_ref=source,
+            dst_ref=target,
+            send_sem=send_sems.at[i, way, hop],
+            recv_sem=receive_sems.at[i, way, hop],
+            device_id={"zy": (right, left)[way]},
+            device_id_type=pl.DeviceIdType.MESH,
+        )
+        copies[i, hop, way].start()
+
+    def halves(i):
+        cut = helds[i].shape[1] // 2
+        return pl.ds(0, cut), pl.ds(cut, cut)
+
+    for i in range(arrays):
+        loads[i, half].wait()
+        for way, arrived in enumerate((from_lefts[i], from_rights[i])):
+            at = halves(i)[way]
+            send(i, 0, way, helds[i].at[half, at], arrived.at[0, at])
+    for hop in range(1, half):
+        step = half - hop
+        for i in range(arrays):
+            for way, k in enumerate((step, count - step)):
+                held, arrived = helds[i], (from_lefts[i], from_rights[i])[way]
+                loads[i, k].wait()
+                copies[i, hop - 1, way].wait_recv()
+                at = halves(i)[way] if hop == 1 else slice(None)
+                held[k, at, :] = (
+                    held[k, at, :].astype(F32) + arrived[hop - 1, at, :].astype(F32)
+                ).astype(BF16)
+                send(i, hop, way, held.at[k], arrived.at[hop])
+    for i in range(arrays):
+        loads[i, 0].wait()
+        for way in range(2):
+            copies[i, half - 1, way].wait_recv()
+        out_refs[i][...] = (
+            helds[i][0].astype(F32)
+            + from_lefts[i][half - 1].astype(F32)
+            + from_rights[i][half - 1].astype(F32)
+        )
+    for copy in copies.values():
+        copy.wait_send()
+    if swaps:
+        swap.wait()
+
+
+def ring_sum(terms, collective_id, swap=None):
+    arrays, count = len(terms), terms[0].shape[0]
+    half = count // 2
+    swaps = swap is not None
+    anywhere = pl.BlockSpec(memory_space=pl.ANY)
+    shapes = [term.shape[1:] for term in terms]
+    return pl.pallas_call(
+        functools.partial(ring_sum_kernel, count, arrays, swaps),
+        in_specs=[anywhere] * (arrays + swaps),
+        out_specs=[pl.BlockSpec(memory_space=pltpu.VMEM)] * arrays + [anywhere] * swaps,
+        out_shape=[jax.ShapeDtypeStruct(shape, F32) for shape in shapes]
+        + ([jax.ShapeDtypeStruct(swap.shape, swap.dtype)] if swaps else []),
+        scratch_shapes=[pltpu.VMEM((count, *shape), BF16) for shape in shapes]
+        + [pltpu.VMEM((half, *shape), BF16) for shape in shapes + shapes]
+        + [
+            pltpu.SemaphoreType.DMA((arrays, count)),
+            pltpu.SemaphoreType.DMA((arrays, 2, half)),
+            pltpu.SemaphoreType.DMA((arrays, 2, half)),
+        ]
+        + [pltpu.SemaphoreType.DMA] * (2 * swaps),
+        compiler_params=pltpu.CompilerParams(
+            collective_id=collective_id, has_side_effects=True, vmem_limit_bytes=48 * 2**20
+        ),
+        cost_estimate=SMALL,
+        name="ring_sum",
+    )(*terms, *([swap] if swaps else []))
 
 
 def shards(
@@ -715,10 +859,20 @@
     qkv_piece = jnp.concatenate(
         [column_piece(w_query)] + kv_pieces + [gain_piece, row_piece(w_out)], axis=1
     )
-    qkv_ring = Gather(ring, [qkv_piece])
+    qkv_ring = Gather(ring, [qkv_piece], True)
     (first_in,) = after_all((layer_in,), (qkv_piece,))
     other_in = other_core(first_in)
-    hops = [qkv_ring.hop() for _ in range(chips // 2)]
+    hops = [qkv_ring.hop()]
+    w_gate, w_up, w_down = after_all((w_gate, w_up, w_down), hops[0])
+    down_piece = row_piece(w_down)
+    units_piece = unwritten(w_gate, (width // chips, w_gate.shape[1]))
+    for at, piece in enumerate((column_piece(w_gate), column_piece(w_up))):
+        units_piece = lax.dynamic_update_slice(units_piece, piece, (0, at * piece.shape[1]))
+    while qkv_ring.step < chips // 2 - 1:
+        hops.append(qkv_ring.hop())
+    down_ring = Gather(ring, [down_piece])
+    hops.append(qkv_ring.hop(down_piece))
+    down_hop = down_ring.hop(*hops[-1])
     (w_attn,) = qkv_ring.finish()
     w_attn = w_attn.reshape(width, -1)
     w_qkv, gain_all, w_o = jnp.split(
@@ -784,6 +938,7 @@
         on_diagonal = index[None, :] == diagonals[:, None]
         seens.append(jnp.where(on_diagonal, 2, seen.astype(jnp.int32)))
     position = jnp.concatenate(positions)
+    (position,) = after_all((position,), hops[-2])
     angles = rope_angles(position, HEAD_SIZE)
     cosine, sine = jnp.cos(angles), jnp.sin(angles)
 
@@ -791,22 +946,23 @@
         first_in, other_in, gain_a[None], w_attn, cosine, sine, head_cols, 2 * kv_cols,
         math.gcd(rows, 256),
     )
+    query, key_value = after_all((query, key_value), down_hop)
     cosine_rows, sine_rows = cosine.T[:, None, :], sine.T[:, None, :]
-    kv_ring = Gather(ring, [key_value.reshape(trees, chip_rows, 2 * kv_cols)])
+    kv_ring = Gather(ring, [key_value.reshape(trees, chip_rows, 2 * kv_cols)], True)
     kv_hops = [kv_ring.hop()]
-    w_gate, w_up, w_down, out_grad = after_all((w_gate, w_up, w_down, out_grad), (key_value,))
+    kv_hops.append(kv_ring.hop())
+    (out_grad,) = after_all((out_grad,), (key_value,))
     other_grad = other_core(out_grad)
-    units_piece = jnp.concatenate([column_piece(w_gate), column_piece(w_up)], axis=1)
-    down_piece = row_piece(w_down)
     while kv_ring.step < chips // 2 - 1:
         kv_hops.append(kv_ring.hop())
-    (layer_in,) = after_all((layer_in,), kv_hops[0])
+    (layer_in,) = after_all((layer_in,), (key_value,))
     scale_a = row_scale_of(layer_in.astype(F32))
-    (out_grad,) = after_all((out_grad,), kv_hops[1])
+    (out_grad,) = after_all((out_grad,), kv_hops[0])
     grad_low = jnp.concatenate([out_grad, other_grad], axis=1).reshape(trees * chip_rows, width)
-    kv_hops.append(kv_ring.hop(grad_low, scale_a, units_piece, down_piece))
+    kv_hops.append(kv_ring.hop(grad_low, scale_a))
     units_ring = Gather(ring, [units_piece])
-    units_hop = units_ring.hop(*kv_hops[-2])
+    units_hop = units_ring.hop(*kv_hops[-1])
+    units_hop += down_ring.hop(*kv_hops[-1])
     (kvs,) = kv_ring.finish()
 
     def core_sum(part):
@@ -820,10 +976,10 @@
     mixes, lses, middles, inners, normeds_f, scales_f, lows = [], [], [], [], [], [], []
     for tree in range(trees):
         mixed, lse = attend(tree, tables[tree], query, masks[tree], kvs, rep, block)
-        if tree:
-            units_hop += (arrived,)
-        (mixed,) = after_all((mixed,), units_hop)
+        (mixed,) = after_all((mixed,), units_hop + ((arrived,) if tree else ()))
         units_hop = units_ring.hop(mixed)
+        if down_ring.step < chips // 2:
+            units_hop += down_ring.hop(mixed)
         mixes.append(mixed)
         lses.append(lse)
         lows.append(core_sum(dot(mixed, w_o, 0, 1)).astype(BF16))
@@ -844,11 +1000,6 @@
         normeds_f.append(normed_f)
     inner_f = jnp.concatenate(inners, axis=0)
 
-    while units_ring.step < chips // 2 - 1:
-        units_hop = units_ring.hop()
-    down_ring = Gather(ring, [down_piece])
-    down_ring.hop(*units_hop)
-    down_ring.hop(arrived[-1])
     (w_units,) = units_ring.finish()
     (w_d,) = down_ring.finish()
     w_units, w_d = w_units.reshape(width, -1), w_d.reshape(width, -1)
@@ -863,7 +1014,7 @@
     core_sums = []
     (grad_gate,) = after_all((grad_gate,), (down_ring.terms[0],))
     for tree in range(trees):
-        part = back_units(tree, chip_rows, grad_gate, grad_up, w_units)
+        part = back_units(tree, chip_rows, [grad_gate, grad_up], w_units, [0, 1])
         (part,) = after_all((part,), down_hop)
         down_hop = down_ring.hop(part)
         (grad_gate,) = after_all((grad_gate,), (part,))
@@ -871,17 +1022,12 @@
     lows = [own.astype(BF16) for own in core_sums]
     arrived = [other_half(lows[0])]
     inner_f, hidden = after_all((inner_f, hidden), lows)
-    gate_terms = unit_grads(inner_f, grad_gate)
-    (grad_up,) = after_all((grad_up,), (gate_terms, *down_hop))
-    up_terms = unit_grads(inner_f, grad_up)
-    up_terms, arrived[0] = after_all((up_terms, arrived[0]), (gate_terms,))
+    units_terms = unit_grads(inner_f, grad_gate, grad_up)
+    units_terms, arrived[0] = after_all((units_terms, arrived[0]), down_hop)
     arrived.append(other_half(after_all(lows[1:], arrived)[0]))
-    gate_sum, up_sum = (
-        lax.psum_scatter(terms, "zy", scatter_dimension=0, tiled=True)
-        for terms in (gate_terms, up_terms)
-    )
-    units_hop = down_ring.hop(up_terms)
-    arrived[0] = after_all(arrived[:1], (up_terms,))[0]
+    units_ring = Reduce(ring, [pieces(units_terms)])
+    units_hop = units_ring.hop() + down_ring.hop(units_terms)
+    arrived[0] = after_all(arrived[:1], (units_terms,))[0]
 
     grads_middle, grads_low = [], []
 
@@ -896,14 +1042,27 @@
         return jnp.concatenate([low, other_core(low)], axis=0)
 
     mid_lows, out_lows, out_arrived = [backward_norm(0)], [], []
-    kv_rings, grad_queries, grad_kvs = [], [], []
+    grads_qkv, gain_a_terms = [], []
+
+    def back_part(tree, kv_sums):
+        rows_of = (cosine_rows[spans[tree]], -sine_rows[spans[tree]])
+        parts = grad_queries[groups * tree : groups * (tree + 1)]
+        for group in range(groups):
+            kv_sum = kv_sums[:, 128 * group : 128 * (group + 1)]
+            grad_k = kv_sum[:, None, :HEAD_SIZE]
+            half = HEAD_SIZE // 2
+            first, second = turn(grad_k[..., :half], grad_k[..., half:], *rows_of)
+            kv_parts = [first[:, 0], second[:, 0], kv_sum[:, HEAD_SIZE:]]
+            parts.append(jnp.concatenate(kv_parts, axis=1).astype(BF16))
+        grad_qkv = jnp.concatenate(parts, axis=1)
+        grads_qkv.append(grad_qkv)
+        gain_a_terms.append(core_sum(dot(grad_qkv, w_qkv, 1, 1)))
+        return gain_a_terms[-1].astype(BF16)
+
+    grad_queries, grad_kvs = [], []
     for tree in range(trees):
         grad_mixed = dot(w_o, mid_lows[tree], 0, 1).astype(BF16)
         for group in range(groups):
-            if len(out_lows) > len(out_arrived):
-                beside = other_half(out_lows[len(out_arrived)])
-                out_arrived.append(beside)
-                units_hop += (beside,)
             grad_query, grad_kv = attend_back(
                 tree,
                 group,
@@ -925,93 +1084,80 @@
             grad_queries.append(grad_query)
             grad_kvs.append(grad_kv)
             units_hop = ()
-            for each in [down_ring] + kv_rings:
-                if each.left > 0:
-                    units_hop += each.hop(grad_query)
+            if units_ring.left > 0 and group < groups - 1:
+                units_hop = units_ring.hop(grad_query)
             (grad_mixed,) = after_all((grad_mixed,), (grad_query,))
             if tree == 0 and group == 0:
                 (hidden,) = after_all((hidden,), (grad_query,))
-                out_parts = [dot(hidden[span], w_d, 1, 1) for span in spans]
+                out_parts = [
+                    back_units(tree, chip_rows, [hidden], w_d, [0]) for tree in range(trees)
+                ]
                 out_parts = after_all(out_parts, arrived[1:])
                 out_lows = [core_sum(part).astype(BF16) for part in out_parts]
                 (grad_mixed,) = after_all((grad_mixed,), out_lows)
-        kv_rings.append(Reduce(ring, grad_kvs[-1:]))
+                out_arrived.append(other_half(out_lows[0]))
+                units_hop += tuple(out_arrived)
+            elif tree and group < groups - 1:
+                while kv_ring.left > 0:
+                    units_hop += kv_ring.hop(grad_query)
         if tree == 0:
+            kv_ring = Reduce(ring, grad_kvs[-1:])
+            kv_ring.hop()
             arrived[-1] = after_all(arrived[-1:], (grad_query,))[0]
             mid_lows.append(backward_norm(1))
+            kv_hop = kv_ring.hop()
             out_terms = pieces(
                 dot(jnp.concatenate(mid_lows, axis=0), jnp.concatenate(mixes, axis=1), 0, 1)
             )
-            kv_rings[0].hop()
-            mid_lows[1] = after_all(mid_lows[1:], (out_terms,))[0]
-            units_hop += kv_rings[0].hop(mid_lows[1])
-            out_ring = Reduce(ring, [out_terms])
-            units_hop += out_ring.hop()
-            kv_rings.append(out_ring)
-    out_ring = kv_rings.pop(1)
-    kv_rings[1].hop()
-    (down_sum,) = down_ring.finish()
-    gate_sum, up_sum = gate_sum.astype(F32), up_sum.astype(F32)
+            mid_lows[1] = after_all(mid_lows[1:], (out_terms, *kv_hop))[0]
+            out_arrived.append(other_half(after_all(out_lows[1:], (grad_query,))[0]))
+            units_hop += units_ring.hop(*kv_hop) + kv_ring.hop(out_terms)
+            units_hop += tuple(out_arrived[1:])
+    out_arrived = after_all(out_arrived, (grad_queries[-1],))
+    (down_sum,), (units_sum,) = down_ring.finish(), units_ring.finish()
     outputs = unwritten(out_terms, (trees, rows, width))
     out_arrived = after_all(out_arrived, (grad_queries[-1],))
     for tree in range(trees):
         summed = out_lows[tree].astype(F32) + out_arrived[tree].astype(F32)
         outputs = laid(outputs, (middles[tree] + summed).astype(BF16), tree)
 
-    grads_qkv, gain_a_terms, lows = [], [], []
     (layer_in,) = after_all((layer_in,), (grad_queries[-1],))
     normed_a = layer_in.astype(F32) * scale_a
     down_grad = row_grad(down_sum)
-    for tree in range(trees):
-        if tree:
-            while kv_rings[tree].left > 1:
-                kv_rings[tree].hop(*lows)
-            arrived = [other_half(lows[0])]
-            kv_rings[tree].hop(*arrived)
-        (kv_sums,) = kv_rings[tree].finish()
-        rows_of = (cosine_rows[spans[tree]], -sine_rows[spans[tree]])
-        parts = grad_queries[groups * tree : groups * (tree + 1)]
-        for group in range(groups):
-            kv_sum = kv_sums[:, 128 * group : 128 * (group + 1)]
-            grad_k = kv_sum[:, None, :HEAD_SIZE]
-            half = HEAD_SIZE // 2
-            first, second = turn(grad_k[..., :half], grad_k[..., half:], *rows_of)
-            kv_parts = [first[:, 0], second[:, 0], kv_sum[:, HEAD_SIZE:]]
-            parts.append(jnp.concatenate(kv_parts, axis=1).astype(BF16))
-        grad_qkv = jnp.concatenate(parts, axis=1)
-        grads_qkv.append(grad_qkv)
-        own = core_sum(dot(grad_qkv, w_qkv, 1, 1))
-        gain_a_terms.append(own)
-        lows.append(own.astype(BF16))
-    arrived += [other_half(low) for low in lows[1:]]
-    (inner_a,) = after_all((inner_a,), lows)
-    (out_sum,) = out_ring.finish()
-    out_proj_grad = row_grad(out_sum)
-    term_qkv = unit_grads(inner_a, jnp.concatenate(grads_qkv, axis=0))
-    qkv_ring = Reduce(ring, [pieces(term_qkv)])
-    qkv_hop = qkv_ring.hop()
-    gate_grad, up_grad = column_grad(gate_sum), column_grad(up_sum)
-    core_sums = after_all(core_sums + gain_a_terms, qkv_hop)
+    lows = [back_part(0, kv_ring.finish()[0])]
+    arrived = [other_half(lows[0])]
+    (kv_terms,) = after_all(grad_kvs[-1:], lows)
+    (kv_sums,) = after_all(ring_sum([kv_terms], 1), arrived)
+    lows.append(back_part(1, kv_sums))
+    (inner_a,) = after_all((inner_a,), (grads_qkv[-1],))
+    gate_grad, up_grad = (
+        column_grad(part) for part in jnp.split(units_sum, 2, axis=1)
+    )
+    core_sums = after_all(core_sums + gain_a_terms, lows)
     gain_terms = jnp.stack(
         [
             sum(jnp.sum(core_sums[trees + i] * normed_a[i], axis=0) for i in range(trees)),
             sum(jnp.sum(core_sums[i] * normeds_f[i], axis=0) for i in range(trees)),
-        ]
-    )
-    qkv_ring.hop(gain_terms, gate_grad, up_grad, out_proj_grad, down_grad)
-    qkv_ring.hop(*arrived)
-    (qkv_sum,) = qkv_ring.finish()
+        ],
+        axis=1,
+    )
+    gain_terms = jnp.pad(gain_terms, ((0, 0), (0, 126))).astype(BF16)
+    term_qkv = unit_grads(inner_a, jnp.concatenate(grads_qkv, axis=0))
+    term_qkv = jnp.concatenate([term_qkv, gain_terms], axis=1)
+    qkv_sum, out_sum, theirs = ring_sum([pieces(term_qkv), out_terms], 2, lows[1])
+    arrived.append(theirs)
+    out_proj_grad = row_grad(out_sum)
+    qkv_sum, gain_sums = qkv_sum[:, : head_cols + 2 * kv_cols], qkv_sum[:, -128:]
     kv_parts = qkv_sum[:, head_cols:].reshape(-1, groups, 2, HEAD_SIZE)
     key_sum, value_sum = (kv_parts[:, :, i].reshape(-1, kv_cols) for i in range(2))
 
-    keep, give = split_by_core(gain_terms.reshape(2, chips, 2, -1), 2)
-    gain_sums = gain_sum(ring, jnp.moveaxis(keep + other_core(give), 1, 0))
-    gain_sums = (gain_sums + other_half(gain_sums)).reshape(2, -1)
+    keep, give = split_by_core(gain_sums, 0)
+    gain_sums = (keep + other_core(give)).T[:8]
+    gain_sums = gain_sums + other_half(gain_sums)
     gain_a_grad, gain_f_grad = gain_sums[0], gain_sums[1]
     input_grad = unwritten(scale_a, (trees, rows, width))
     for tree in range(trees):
-        (theirs,) = after_all((arrived[tree],), (gain_terms,) * tree)
-        grad_inner = lows[tree].astype(F32) + theirs.astype(F32)
+        grad_inner = lows[tree].astype(F32) + arrived[tree].astype(F32)
         input_grad = laid(
             input_grad,
             grads_middle[tree] + norm_back(grad_inner * gain_a, normed_a[tree], scale_a[tree]),
@@ -1031,20 +1177,6 @@
         up_grad,
         down_grad,
     )
-
-
-def gain_sum(ring, terms):
-    half = ring.count // 2
-
-    def term(offset):
-        return lax.dynamic_index_in_dim(terms, ring.chip(offset), 0, keepdims=False)
-
-    rightward, leftward = ring.go_right(term(half)), None
-    for step in range(half - 1, 0, -1):
-        rightward = ring.go_right(rightward + term(step))
-        leftward = ring.go_left(term(-step) if leftward is None else leftward + term(-step))
-    total = term(0) + rightward
-    return total if leftward is None else total + leftward
 
 
 def solution(mesh):

time: 1340 us -> 1260 us (0.940)
  waiting for transfers between devices: 477 us -> 308 us
  Pallas kernels: 325 us -> 461 us
  starting transfers between devices: 132 us -> 85.5 us
  matrix products: 66.8 us -> 37.1 us
  local copies, waits for them, and re-layouts: 121 us -> 149 us
  between operations: 16.8 us -> 3.09 us
    pallas_call x6 -> x9, Pallas kernels: 140 us -> 277 us  [the longest x2 115 us: ring_sum(): pl.pallas_call(functools.partial(ring_sum_kernel, count, arrays, swaps),...]
    ppermute x39 -> x28, waiting for transfers between devices: 121 us -> 37.7 us  [go_left(): return lax.ppermute(value, 'zy', self.left)]
    ppermute x9 -> x8, waiting for transfers between devices: 56.7 us -> 0.48 us  [other_half(): return lax.ppermute(value, 'tp', SWAP)]
    ppermute x40 -> x28, starting transfers between devices: 87.6 us -> 33.1 us  [go_right(): return lax.ppermute(value, 'zy', self.right)]
    dot_general x11 -> x9, matrix products: 66.8 us -> 37.1 us  [dot(): lax.dot_general(left, right, (((left_dim,), (right_dim,)), ((), ())), pre...]
    ppermute x40 -> x28, waiting for transfers between devices: 295 us -> 269 us  [go_right(): return lax.ppermute(value, 'zy', self.right)]
    unnamed x207 -> x279, local copies, waits for them, and re-layouts: 21.1 us -> 33.6 us
    ppermute x39 -> x28, starting transfers between devices: 29 us -> 37.8 us  [go_left(): return lax.ppermute(value, 'zy', self.left)]
  transfers between devices with their start and end apart: 120 -> 94, of which waited for: 51 -> 36; matrix products, arithmetic and copies ran while one was open for 26% -> 25% of each run, Pallas kernels for 16% -> 25%
where the time goes in v3:
time: 1260 us; the launch traced here: 1240 us
  Pallas kernels  461 us (37%)
  waiting for transfers between devices  308 us (24%)
  other arithmetic  201 us (16%)
  local copies, waits for them, and re-layouts  149 us (12%)
  starting transfers between devices  85.5 us (7%)
  matrix products  37.1 us (3%)
    ppermute x28, waiting for transfers between devices, go_right(): return lax.ppermute(value, 'zy', self.right)  269 us
    pallas_call x2, Pallas kernels, ring_sum(): pl.pallas_call(functools.partial(ring_sum_kernel, count, arrays, swaps),...  115 us
    pallas_call x3, Pallas kernels, unit_grads(): pl.pallas_call(functools.partial(unit_grads_kernel, tiles), grid=(width /...  87.7 us
    pallas_call x4, Pallas kernels, back_units(): pl.pallas_call(functools.partial(back_units_kernel, len(units)), grid=(wi...  74.3 us
    pallas_call x4, Pallas kernels, attend_back(): pl.pallas_call(functools.partial(attend_back_kernel, block, rep, rows //...  68.9 us
    pallas_call x1, Pallas kernels, hidden_units(): pl.pallas_call(units_kernel, grid=(tiles, tokens // rows), in_specs=[tall...  66.6 us
    dynamic_update_slice x35, local copies, waits for them, and re-layouts, put(): return lax.dynamic_update_slice(whole, part[None], at)  57.4 us
    ppermute x28, starting transfers between devices, go_left(): return lax.ppermute(value, 'zy', self.left)  37.8 us
  transfers between devices with their start and end apart: 94, of which 36 were waited for; matrix products, arithmetic and copies ran while one was open for 25% of the time, Pallas kernels for 25%

profile of v3, /device:TPU:0, one launch (start us, length us, event | category | flops | bytes accessed | tf_op | source)
XLA Modules:
  0.0 1244.0 jit_solution(12113234515083554022)
XLA Ops:
  20.6 14.0 %collective-permute-done.6 = bf16[256,1408]{1,0:T(8,128)(2,1)} collective-permute-done((bf16[256,1408]{1,0:T(8,128)(2,1)S(1)}, bf16[256,1408]{1,0:T(8,128)(2,1)}, u32[]{:S(2)}, u32[]{:S(2)}) %collective-permute-start.6) | collective-permute-done | bytes 720928 | tf_op jit(solution)/shard_map/ppermute | solution.py:106
  89.0 16.3 %project.1 = (bf16[2048,2048]{1,0:T(8,128)(2,1)}, bf16[512,2048]{1,0:T(8,128)(2,1)S(1)}, bf16[2048,256]{1,0:T(8,128)(2,1)S(1)}) custom-call(bf16[2,512,2048]{2,1,0:T(8,128)(2,1)} %own_ref, bf16[2,512,2048]{2,1,0:T(8,128)(2,1)} %collective-permute-done.5.other_ref, f32[1,2048]{1,0:T(1,128)S(1)} %copy.74.gain_ref, bf16[2048,1408]{1,0:T(8,128)(2,1)} %bitcast.400, ...), custom_call_target="tpu_custom_call" | custom-call | flops 1048576 | bytes 1024 | tf_op jit(solution)/shard_map/project/pallas_call | solution.py:539
  116.7 17.8 %collective-permute-done.17 = bf16[2,1024,256]{2,1,0:T(8,128)(2,1)} collective-permute-done((bf16[2,1024,256]{2,1,0:T(8,128)(2,1)}, bf16[2,1024,256]{2,1,0:T(8,128)(2,1)}, u32[]{:S(2)}, u32[]{:S(2)}) %collective-permute-start.17) | collective-permute-done | bytes 1048608 | tf_op jit(solution)/shard_map/ppermute | solution.py:106
  145.1 14.4 %collective-permute-done.19 = bf16[2,1024,256]{2,1,0:T(8,128)(2,1)} collective-permute-done((bf16[2,1024,256]{2,1,0:T(8,128)(2,1)}, bf16[2,1024,256]{2,1,0:T(8,128)(2,1)}, u32[]{:S(2)}, u32[]{:S(2)}) %collective-permute-start.19) | collective-permute-done | bytes 1048608 | tf_op jit(solution)/shard_map/ppermute | solution.py:106
  209.8 16.4 %tree_attention.2 = (bf16[512,1024]{1,0:T(8,128)(2,1)S(1)}, f32[2,4,1024]{2,1,0:T(4,128)S(1)}) custom-call(s32[4]{0:T(128)S(1)} %get-tuple-element.446.count_ref, s32[4,34]{1,0:T(4,128)S(1)} %broadcast_add_fusion.1.list_ref, s32[4]{0:T(128)S(1)} %iota_add_fusion.4.diag_ref, bf16[512,2048]{1,0:T(8,128)(2,1)S(1)} %get-tuple-element.169.query_ref, ...), custom_call_target="tpu_custom_call" | custom-call | flops 1048576 | bytes 1024 | tf_op jit(solution)/shard_map/tree_attention/pallas_call | solution.py:330
  226.2 38.2 %collective-permute-done.30 = bf16[256,2048]{1,0:T(8,128)(2,1)S(1)} collective-permute-done((bf16[256,2048]{1,0:T(8,128)(2,1)}, bf16[256,2048]{1,0:T(8,128)(2,1)S(1)}, u32[]{:S(2)}, u32[]{:S(2)}) %collective-permute-start.30) | collective-permute-done | bytes 1048608 | tf_op jit(solution)/shard_map/ppermute | solution.py:106
  297.9 16.5 %tree_attention.3 = (bf16[512,1024]{1,0:T(8,128)(2,1)S(1)}, f32[2,4,1024]{2,1,0:T(4,128)S(1)}) custom-call(s32[4]{0:T(128)S(1)} %get-tuple-element.447.count_ref, s32[4,34]{1,0:T(4,128)S(1)} %broadcast_add_fusion.list_ref, s32[4]{0:T(128)S(1)} %iota_add_fusion.4.diag_ref, bf16[512,2048]{1,0:T(8,128)(2,1)S(1)} %get-tuple-element.169.query_ref, ...), custom_call_target="tpu_custom_call" | custom-call | flops 1048576 | bytes 1024 | tf_op jit(solution)/shard_map/tree_attention/pallas_call | solution.py:330
  314.4 38.6 %collective-permute-done.35 = bf16[256,2048]{1,0:T(8,128)(2,1)S(1)} collective-permute-done((bf16[256,2048]{1,0:T(8,128)(2,1)S(1)}, bf16[256,2048]{1,0:T(8,128)(2,1)S(1)}, u32[]{:S(2)}, u32[]{:S(2)}) %collective-permute-start.35) | collective-permute-done | bytes 1048608 | tf_op jit(solution)/shard_map/ppermute | solution.py:106
  382.6 42.0 %collective-permute-done.42 = bf16[256,4096]{1,0:T(8,128)(2,1)S(1)} collective-permute-done((bf16[256,4096]{1,0:T(8,128)(2,1)}, bf16[256,4096]{1,0:T(8,128)(2,1)S(1)}, u32[]{:S(2)}, u32[]{:S(2)}) %collective-permute-start.42) | collective-permute-done | bytes 2097184 | tf_op jit(solution)/shard_map/ppermute | solution.py:106
  457.3 66.6 %hidden_units.1 = (bf16[2048,2048]{1,0:T(8,128)(2,1)}, bf16[2048,2048]{1,0:T(8,128)(2,1)}, bf16[2048,2048]{1,0:T(8,128)(2,1)}) custom-call(bf16[2048,2048]{1,0:T(8,128)(2,1)} %pad_maximum_fusion.1.inner_ref.rows_ref, bf16[2048,2048]{1,0:T(8,128)(2,1)} %bitcast.387, bf16[2048,4096]{1,0:T(8,128)(2,1)} %bitcast.49.gate_ref.up_ref.refs_2_.refs_3_, ...), custom_call_target="tpu_custom_call" | custom-call | flops 1048576 | bytes 1024 | tf_op jit(solution)/shard_map/hidden_units/pallas_call | solution.py:593
  523.9 25.4 %unit_grads.3 = bf16[2048,2048]{1,0:T(8,128)(2,1)} custom-call(bf16[2048,2048]{1,0:T(8,128)(2,1)} %bitcast.388, bf16[2048,2048]{1,0:T(8,128)(2,1)} %get-tuple-element.207.refs_0_), custom_call_target="tpu_custom_call" | custom-call | flops 1048576 | bytes 1024 | tf_op jit(solution)/shard_map/unit_grads/pallas_call | solution.py:661
  553.3 23.8 %back_units.4 = bf16[1024,2048]{1,0:T(8,128)(2,1)} custom-call(bf16[2048,2048]{1,0:T(8,128)(2,1)} %get-tuple-element.192.refs_0_, bf16[2048,2048]{1,0:T(8,128)(2,1)} %get-tuple-element.185.refs_1_, bf16[2048,4096]{1,0:T(8,128)(2,1)} %bitcast.49.gate_ref.up_ref.refs_2_.refs_3_, bf16[2048,4096]{1,0:T(8,128)(2,1)} %bitcast.49.gate_ref.up_ref.refs_2_.refs_3_), custom_call_target="tpu_custom_call" | custom-call | flops 1048576 | bytes 1024 | tf_op jit(solution)/shard_map/back_units/pallas_call | solution.py:622
  584.1 23.8 %back_units.5 = bf16[1024,2048]{1,0:T(8,128)(2,1)} custom-call(bf16[2048,2048]{1,0:T(8,128)(2,1)} %get-tuple-element.192.refs_0_, bf16[2048,2048]{1,0:T(8,128)(2,1)} %get-tuple-element.185.refs_1_, bf16[2048,4096]{1,0:T(8,128)(2,1)} %bitcast.49.gate_ref.up_ref.refs_2_.refs_3_, bf16[2048,4096]{1,0:T(8,128)(2,1)} %bitcast.49.gate_ref.up_ref.refs_2_.refs_3_), custom_call_target="tpu_custom_call" | custom-call | flops 1048576 | bytes 1024 | tf_op jit(solution)/shard_map/back_units/pallas_call | solution.py:622
  627.8 47.1 %unit_grads.4 = bf16[2048,4096]{1,0:T(8,128)(2,1)} custom-call(bf16[2048,2048]{1,0:T(8,128)(2,1)} %pad_maximum_fusion.1.inner_ref.rows_ref, bf16[2048,2048]{1,0:T(8,128)(2,1)} %get-tuple-element.192.refs_0_, bf16[2048,2048]{1,0:T(8,128)(2,1)} %get-tuple-element.185.refs_1_), custom_call_target="tpu_custom_call" | custom-call | flops 1048576 | bytes 1024 | tf_op jit(solution)/shard_map/unit_grads/pallas_call | solution.py:661
  699.0 17.2 %tree_attention_back.4 = (bf16[1024,256]{1,0:T(8,128)(2,1)}, bf16[8,1024,256]{2,1,0:T(8,128)(2,1)}) custom-call(s32[4,32]{1,0:T(4,128)} %get-tuple-element.445.seen_ref, bf16[512,2048]{1,0:T(8,128)(2,1)} %copy-done, bf16[16,1024]{1,0:T(8,128)(2,1)} %copy-done.14, bf16[512,1024]{1,0:T(8,128)(2,1)} %copy-done.9, bf16[512,1024]{1,0:T(8,128)(2,1)} %fusion.46.grad_ref, ...), custom_call_target="tpu_custom_call" | custom-call | flops 1048576 | bytes 1024 | tf_op jit(solution)/shard_map/tree_attention_back/pallas_call | solution.py:469
  716.2 18.1 %collective-permute-done.59 = bf16[128,4096]{1,0:T(8,128)(2,1)} collective-permute-done((bf16[128,4096]{1,0:T(8,128)(2,1)S(1)}, bf16[128,4096]{1,0:T(8,128)(2,1)}, u32[]{:S(2)}, u32[]{:S(2)}) %collective-permute-start.59) | collective-permute-done | bytes 1048608 | tf_op jit(solution)/shard_map/ppermute | solution.py:106
  735.1 13.4 %back_units.7 = bf16[1024,2048]{1,0:T(8,128)(2,1)} custom-call(bf16[2048,2048]{1,0:T(8,128)(2,1)} %get-tuple-element.207.refs_0_, bf16[2048,2048]{1,0:T(8,128)(2,1)} %bitcast.383), custom_call_target="tpu_custom_call" | custom-call | flops 1048576 | bytes 1024 | tf_op jit(solution)/shard_map/back_units/pallas_call | solution.py:622
  796.9 17.6 %tree_attention_back.5 = (bf16[1024,256]{1,0:T(8,128)(2,1)}, bf16[8,1024,256]{2,1,0:T(8,128)(2,1)}) custom-call(s32[4,32]{1,0:T(4,128)} %get-tuple-element.445.seen_ref, bf16[512,2048]{1,0:T(8,128)(2,1)} %copy-done, bf16[16,1024]{1,0:T(8,128)(2,1)} %copy-done.14, bf16[512,1024]{1,0:T(8,128)(2,1)} %copy-done.9, ...), custom_call_target="tpu_custom_call", output_to_operand_aliasing={{1}: (10, {})} | custom-call | flops 1048576 | bytes 1024 | tf_op jit(solution)/shard_map/tree_attention_back/pallas_call | solution.py:469
  900.7 17.0 %tree_attention_back.6 = (bf16[1024,256]{1,0:T(8,128)(2,1)}, bf16[8,1024,256]{2,1,0:T(8,128)(2,1)}) custom-call(s32[4,32]{1,0:T(4,128)} %get-tuple-element.444.seen_ref, bf16[512,2048]{1,0:T(8,128)(2,1)} %copy-done, bf16[16,1024]{1,0:T(8,128)(2,1)} %copy-done.13, bf16[512,1024]{1,0:T(8,128)(2,1)} %copy-done.7, ...), custom_call_target="tpu_custom_call" | custom-call | flops 1048576 | bytes 1024 | tf_op jit(solution)/shard_map/tree_attention_back/pallas_call | solution.py:469
  917.8 24.2 %collective-permute-done.76 = bf16[1024,256]{1,0:T(8,128)(2,1)S(1)} collective-permute-done((bf16[1024,256]{1,0:T(8,128)(2,1)S(1)}, bf16[1024,256]{1,0:T(8,128)(2,1)S(1)}, u32[]{:S(2)}, u32[]{:S(2)}) %collective-permute-start.76) | collective-permute-done | bytes 524320 | tf_op jit(solution)/shard_map/ppermute | solution.py:106
  960.4 17.1 %tree_attention_back.7 = (bf16[1024,256]{1,0:T(8,128)(2,1)}, bf16[8,1024,256]{2,1,0:T(8,128)(2,1)}) custom-call(s32[4,32]{1,0:T(4,128)} %get-tuple-element.444.seen_ref, bf16[512,2048]{1,0:T(8,128)(2,1)} %copy-done, bf16[16,1024]{1,0:T(8,128)(2,1)} %copy-done.13, bf16[512,1024]{1,0:T(8,128)(2,1)} %copy-done.7, ...), custom_call_target="tpu_custom_call", output_to_operand_aliasing={{1}: (10, {})} | custom-call | flops 1048576 | bytes 1024 | tf_op jit(solution)/shard_map/tree_attention_back/pallas_call | solution.py:469
  1027.5 59.2 %ring_sum.2 = f32[1024,256]{1,0:T(8,128)S(1)} custom-call(bf16[8,1024,256]{2,1,0:T(8,128)(2,1)S(1)} %copy-done.4), custom_call_target="tpu_custom_call" | custom-call | flops 1048576 | bytes 1024 | tf_op jit(solution)/shard_map/ring_sum/pallas_call | solution.py:782
  1109.4 15.2 %unit_grads.5 = bf16[2048,768]{1,0:T(8,128)(2,1)} custom-call(bf16[2048,2048]{1,0:T(8,128)(2,1)} %get-tuple-element.247.rows_ref, bf16[2048,768]{1,0:T(8,128)(2,1)} %pad_maximum_fusion.3.refs_0_), custom_call_target="tpu_custom_call" | custom-call | flops 1048576 | bytes 1024 | tf_op jit(solution)/shard_map/unit_grads/pallas_call | solution.py:661
  1145.5 55.5 %ring_sum.3 = (f32[256,896]{1,0:T(8,128)S(1)}, f32[256,512]{1,0:T(8,128)S(1)}, bf16[512,2048]{1,0:T(8,128)(2,1)S(1)}) custom-call(bf16[8,256,896]{2,1,0:T(8,128)(2,1)} %bitcast.407, bf16[8,256,512]{2,1,0:T(8,128)(2,1)S(1)} %bitcast.377, bf16[512,2048]{1,0:T(8,128)(2,1)} %get-tuple-element.313.refs_2_), custom_call_target="tpu_custom_call" | custom-call | flops 1048576 | bytes 1024 | tf_op jit(solution)/shard_map/ring_sum/pallas_call | solution.py:782
  (725 shorter events, 585.6 us)
Async XLA Ops:
  18.3 70.7 %collective-permute-start.5 = (bf16[2,512,2048]{2,1,0:T(8,128)(2,1)}, bf16[2,512,2048]{2,1,0:T(8,128)(2,1)}, u32[]{:S(2)}, u32[]{:S(2)}) collective-permute-start(bf16[2,512,2048]{2,1,0:T(8,128)(2,1)} %own_ref), channel_id=1, source_target_pairs={{0,2},{2,0},{1,3},{3,1},{4,6},{6,4},{5,7},{7,5},{8,10},{10,8},{9,1... | collective-permute-start | bytes 12582920 | tf_op jit(solution)/shard_map/ppermute | solution.py:196
  42.4 64.7 %collective-permute-start.26 = (bf16[128,2048]{1,0:T(8,128)(2,1)}, bf16[128,2048]{1,0:T(8,128)(2,1)}, u32[]{:S(2)}, u32[]{:S(2)}) collective-permute-start(bf16[128,2048]{1,0:T(8,128)(2,1)} %constant_dynamic-slice_fusion.11), channel_id=1, source_target_pairs={{0,2},{2,0},{1,3},{3,1},{4,6},{6,4},{5,7},{7,5},{8,10},{10,8},{9,1... | collective-permute-start | bytes 1572872 | tf_op jit(solution)/shard_map/ppermute | solution.py:196
  48.9 63.0 %collective-permute-start.27 = (bf16[128,2048]{1,0:T(8,128)(2,1)}, bf16[128,2048]{1,0:T(8,128)(2,1)}, u32[]{:S(2)}, u32[]{:S(2)}) collective-permute-start(bf16[128,2048]{1,0:T(8,128)(2,1)} %constant_dynamic-slice_fusion.10), channel_id=1, source_target_pairs={{0,2},{2,0},{1,3},{3,1},{4,6},{6,4},{5,7},{7,5},{8,10},{10,8},{9,1... | collective-permute-start | bytes 1572872 | tf_op jit(solution)/shard_map/ppermute | solution.py:196
  106.3 60.9 %collective-permute-start.23 = (bf16[2,512,2048]{2,1,0:T(8,128)(2,1)}, bf16[2,512,2048]{2,1,0:T(8,128)(2,1)}, u32[]{:S(2)}, u32[]{:S(2)}) collective-permute-start(bf16[2,512,2048]{2,1,0:T(8,128)(2,1)} %param.14), channel_id=1, source_target_pairs={{0,2},{2,0},{1,3},{3,1},{4,6},{6,4},{5,7},{7,5},{8,10},{10,8},{9,1... | collective-permute-start | bytes 12582920 | tf_op jit(solution)/shard_map/ppermute | solution.py:196
  198.2 67.6 %collective-permute-start.28 = (bf16[256,4096]{1,0:T(8,128)(2,1)}, bf16[256,4096]{1,0:T(8,128)(2,1)S(1)}, u32[]{:S(2)}, u32[]{:S(2)}) collective-permute-start(bf16[256,4096]{1,0:T(8,128)(2,1)} %maximum_dynamic-update-slice_fusion.1.like_ref), channel_id=1, source_target_pairs={{0,8},{8,16},{16,24},{24,28},{28,20},{20,12},{12,4},{4,0},{1,9},{9... | collective-permute-start | bytes 6291464 | tf_op jit(solution)/shard_map/ppermute | solution.py:106
  199.5 66.3 %collective-permute-start.29 = (bf16[256,4096]{1,0:T(8,128)(2,1)}, bf16[256,4096]{1,0:T(8,128)(2,1)S(1)}, u32[]{:S(2)}, u32[]{:S(2)}) collective-permute-start(bf16[256,4096]{1,0:T(8,128)(2,1)} %maximum_dynamic-update-slice_fusion.1.like_ref), channel_id=1, source_target_pairs={{8,0},{16,8},{24,16},{28,24},{20,28},{12,20},{4,12},{0,4},{9,1},{1... | collective-permute-start | bytes 6291464 | tf_op jit(solution)/shard_map/ppermute | solution.py:109
  200.6 63.8 %collective-permute-start.30 = (bf16[256,2048]{1,0:T(8,128)(2,1)}, bf16[256,2048]{1,0:T(8,128)(2,1)S(1)}, u32[]{:S(2)}, u32[]{:S(2)}) collective-permute-start(bf16[256,2048]{1,0:T(8,128)(2,1)} %collective-permute-done.15), channel_id=1, source_target_pairs={{0,8},{8,16},{16,24},{24,28},{28,20},{20,12},{12,4},{4,0},{1,9},{9... | collective-permute-start | bytes 3145736 | tf_op jit(solution)/shard_map/ppermute | solution.py:106
  202.0 63.8 %collective-permute-start.31 = (bf16[256,2048]{1,0:T(8,128)(2,1)}, bf16[256,2048]{1,0:T(8,128)(2,1)S(1)}, u32[]{:S(2)}, u32[]{:S(2)}) collective-permute-start(bf16[256,2048]{1,0:T(8,128)(2,1)} %collective-permute-done.16), channel_id=1, source_target_pairs={{8,0},{16,8},{24,16},{28,24},{20,28},{12,20},{4,12},{0,4},{9,1},{1... | collective-permute-start | bytes 3145736 | tf_op jit(solution)/shard_map/ppermute | solution.py:109
  282.5 71.4 %collective-permute-start.33 = (bf16[256,4096]{1,0:T(8,128)(2,1)S(1)}, bf16[256,4096]{1,0:T(8,128)(2,1)}, u32[]{:S(2)}, u32[]{:S(2)}) collective-permute-start(bf16[256,4096]{1,0:T(8,128)(2,1)S(1)} %copy-done.71), channel_id=1, source_target_pairs={{0,8},{8,16},{16,24},{24,28},{28,20},{20,12},{12,4},{4,0},{1,9},{9... | collective-permute-start | bytes 6291464 | tf_op jit(solution)/shard_map/ppermute | solution.py:106
  283.7 70.2 %collective-permute-start.34 = (bf16[256,4096]{1,0:T(8,128)(2,1)S(1)}, bf16[256,4096]{1,0:T(8,128)(2,1)}, u32[]{:S(2)}, u32[]{:S(2)}) collective-permute-start(bf16[256,4096]{1,0:T(8,128)(2,1)S(1)} %copy-done.69), channel_id=1, source_target_pairs={{8,0},{16,8},{24,16},{28,24},{20,28},{12,20},{4,12},{0,4},{9,1},{1... | collective-permute-start | bytes 6291464 | tf_op jit(solution)/shard_map/ppermute | solution.py:109
  288.1 65.8 %collective-permute-start.37 = (bf16[512,2048]{1,0:T(8,128)(2,1)S(1)}, bf16[512,2048]{1,0:T(8,128)(2,1)}, u32[]{:S(2)}, u32[]{:S(2)}) collective-permute-start(bf16[512,2048]{1,0:T(8,128)(2,1)S(1)} %fusion.14), channel_id=1, source_target_pairs={{0,1},{1,0},{2,3},{3,2},{4,5},{5,4},{6,7},{7,6},{8,9},{9,8},{10,11... | collective-permute-start | bytes 6291464 | tf_op jit(solution)/shard_map/ppermute | solution.py:200
  292.8 60.2 %collective-permute-start.35 = (bf16[256,2048]{1,0:T(8,128)(2,1)S(1)}, bf16[256,2048]{1,0:T(8,128)(2,1)S(1)}, u32[]{:S(2)}, u32[]{:S(2)}) collective-permute-start(bf16[256,2048]{1,0:T(8,128)(2,1)S(1)} %copy-done.73), channel_id=1, source_target_pairs={{0,8},{8,16},{16,24},{24,28},{28,20},{20,12},{12,4},{4,0},{1,9},{9... | collective-permute-start | bytes 3145736 | tf_op jit(solution)/shard_map/ppermute | solution.py:106
  294.4 59.5 %collective-permute-start.36 = (bf16[256,2048]{1,0:T(8,128)(2,1)S(1)}, bf16[256,2048]{1,0:T(8,128)(2,1)S(1)}, u32[]{:S(2)}, u32[]{:S(2)}) collective-permute-start(bf16[256,2048]{1,0:T(8,128)(2,1)S(1)} %copy-done.75), channel_id=1, source_target_pairs={{8,0},{16,8},{24,16},{28,24},{20,28},{12,20},{4,12},{0,4},{9,1},{1... | collective-permute-start | bytes 3145736 | tf_op jit(solution)/shard_map/ppermute | solution.py:109
  367.5 57.1 %collective-permute-start.42 = (bf16[256,4096]{1,0:T(8,128)(2,1)}, bf16[256,4096]{1,0:T(8,128)(2,1)S(1)}, u32[]{:S(2)}, u32[]{:S(2)}) collective-permute-start(bf16[256,4096]{1,0:T(8,128)(2,1)} %collective-permute-done.33), channel_id=1, source_target_pairs={{0,8},{8,16},{16,24},{24,28},{28,20},{20,12},{12,4},{4,0},{1,9},{9... | collective-permute-start | bytes 6291464 | tf_op jit(solution)/shard_map/ppermute | solution.py:106
  369.0 57.3 %collective-permute-start.43 = (bf16[256,4096]{1,0:T(8,128)(2,1)}, bf16[256,4096]{1,0:T(8,128)(2,1)S(1)}, u32[]{:S(2)}, u32[]{:S(2)}) collective-permute-start(bf16[256,4096]{1,0:T(8,128)(2,1)} %collective-permute-done.34), channel_id=1, source_target_pairs={{8,0},{16,8},{24,16},{28,24},{20,28},{12,20},{4,12},{0,4},{9,1},{1... | collective-permute-start | bytes 6291464 | tf_op jit(solution)/shard_map/ppermute | solution.py:109
  370.3 59.3 %collective-permute-start.40 = (bf16[512,2048]{1,0:T(8,128)(2,1)S(1)}, bf16[512,2048]{1,0:T(8,128)(2,1)S(1)}, u32[]{:S(2)}, u32[]{:S(2)}) collective-permute-start(bf16[512,2048]{1,0:T(8,128)(2,1)S(1)} %fusion.13), channel_id=1, source_target_pairs={{0,1},{1,0},{2,3},{3,2},{4,5},{5,4},{6,7},{7,6},{8,9},{9,8},{10,11... | collective-permute-start | bytes 6291464 | tf_op jit(solution)/shard_map/ppermute | solution.py:200
  615.2 59.6 %collective-permute-start.54 = (bf16[512,2048]{1,0:T(8,128)(2,1)S(1)}, bf16[512,2048]{1,0:T(8,128)(2,1)}, u32[]{:S(2)}, u32[]{:S(2)}) collective-permute-start(bf16[512,2048]{1,0:T(8,128)(2,1)S(1)} %get-tuple-element.350), channel_id=1, source_target_pairs={{0,1},{1,0},{2,3},{3,2},{4,5},{5,4},{6,7},{7,6},{8,9},{9,8},{10,11... | collective-permute-start | bytes 6291464 | tf_op jit(solution)/shard_map/ppermute | solution.py:200
  681.2 80.5 %collective-permute-start.58 = (bf16[512,2048]{1,0:T(8,128)(2,1)}, bf16[512,2048]{1,0:T(8,128)(2,1)S(1)}, u32[]{:S(2)}, u32[]{:S(2)}) collective-permute-start(bf16[512,2048]{1,0:T(8,128)(2,1)} %get-tuple-element.198), channel_id=1, source_target_pairs={{0,1},{1,0},{2,3},{3,2},{4,5},{5,4},{6,7},{7,6},{8,9},{9,8},{10,11... | collective-permute-start | bytes 6291464 | tf_op jit(solution)/shard_map/ppermute | solution.py:200
  793.0 69.1 %collective-permute-start.93 = (f32[128,2048]{1,0:T(8,128)}, f32[128,2048]{1,0:T(8,128)}, u32[]{:S(2)}, u32[]{:S(2)}) collective-permute-start(f32[128,2048]{1,0:T(8,128)} %constant_dynamic-slice_fusion), channel_id=1, source_target_pairs={{0,2},{2,0},{1,3},{3,1},{4,6},{6,4},{5,7},{7,5},{8,10},{10,8},{9,1... | collective-permute-start | bytes 3145736 | tf_op jit(solution)/shard_map/ppermute | solution.py:196
  883.4 58.6 %collective-permute-start.74 = (bf16[256,4096]{1,0:T(8,128)(2,1)}, bf16[256,4096]{1,0:T(8,128)(2,1)}, u32[]{:S(2)}, u32[]{:S(2)}) collective-permute-start(bf16[256,4096]{1,0:T(8,128)(2,1)} %get-tuple-element.330), channel_id=1, source_target_pairs={{0,8},{8,16},{16,24},{24,28},{28,20},{20,12},{12,4},{4,0},{1,9},{9... | collective-permute-start | bytes 6291464 | tf_op jit(solution)/shard_map/ppermute | solution.py:106
  883.6 58.5 %collective-permute-start.75 = (bf16[256,4096]{1,0:T(8,128)(2,1)}, bf16[256,4096]{1,0:T(8,128)(2,1)}, u32[]{:S(2)}, u32[]{:S(2)}) collective-permute-start(bf16[256,4096]{1,0:T(8,128)(2,1)} %get-tuple-element.329), channel_id=1, source_target_pairs={{8,0},{16,8},{24,16},{28,24},{20,28},{12,20},{4,12},{0,4},{9,1},{1... | collective-permute-start | bytes 6291464 | tf_op jit(solution)/shard_map/ppermute | solution.py:109
  1008.1 89.7 %collective-permute-start.92 = (f32[128,2048]{1,0:T(8,128)}, f32[128,2048]{1,0:T(8,128)}, u32[]{:S(2)}, u32[]{:S(2)}) collective-permute-start(f32[128,2048]{1,0:T(8,128)} %constant_dynamic-slice_fusion.1), channel_id=1, source_target_pairs={{0,2},{2,0},{1,3},{3,1},{4,6},{6,4},{5,7},{7,5},{8,10},{10,8},{9,1... | collective-permute-start | bytes 3145736 | tf_op jit(solution)/shard_map/ppermute | solution.py:196
  1009.6 94.9 %collective-permute-start.91 = (f32[128,2048]{1,0:T(8,128)}, f32[128,2048]{1,0:T(8,128)}, u32[]{:S(2)}, u32[]{:S(2)}) collective-permute-start(f32[128,2048]{1,0:T(8,128)} %constant_dynamic-slice_fusion.2), channel_id=1, source_target_pairs={{0,2},{2,0},{1,3},{3,1},{4,6},{6,4},{5,7},{7,5},{8,10},{10,8},{9,1... | collective-permute-start | bytes 3145736 | tf_op jit(solution)/shard_map/ppermute | solution.py:196
  1012.5 74.2 %collective-permute-start.83 = (bf16[512,2048]{1,0:T(8,128)(2,1)S(1)}, bf16[512,2048]{1,0:T(8,128)(2,1)S(1)}, u32[]{:S(2)}, u32[]{:S(2)}) collective-permute-start(bf16[512,2048]{1,0:T(8,128)(2,1)S(1)} %get-tuple-element.315), channel_id=1, source_target_pairs={{0,1},{1,0},{2,3},{3,2},{4,5},{5,4},{6,7},{7,6},{8,9},{9,8},{10,11... | collective-permute-start | bytes 6291464 | tf_op jit(solution)/shard_map/ppermute | solution.py:200
  (205 other events, 4931.6 us)

commit v4 on v3

--- a/solution.py
+++ b/solution.py
@@ -315,7 +315,7 @@
                 (rep * HEAD_SIZE, block), lambda g, q, *_: (g, tree * query_blocks + q)
             ),
             pl.BlockSpec((16, block), lambda g, q, *_: (0, q)),
-            pl.BlockSpec((pieces, 1, rows, 128), lambda g, q, *_: (0, tree, 0, g)),
+            pl.BlockSpec((pieces, 1, rows, 128), lambda g, q, *_: (0, 0, 0, g)),
             pl.BlockSpec((keys + block, 128), lambda g, q, *_: (0, 0)),
         ],
         out_specs=[
@@ -448,7 +448,7 @@
             head,
             head,
             pl.BlockSpec((1, rep, rows), lambda i, *_: (group, 0, 0)),
-            pl.BlockSpec((pieces, 1, rows, 128), lambda i, *_: (0, tree, 0, group)),
+            pl.BlockSpec((pieces, 1, rows, 128), lambda i, *_: (0, 0, 0, group)),
             pl.BlockSpec((keys + block, 128), lambda i, *_: (0, 0)),
             table,
             table,
@@ -564,46 +564,59 @@
     )(own, other, gain, weight, cosine, sine)
 
 
-def units_kernel(
-    inner_ref, grad_ref, gate_ref, up_ref, down_ref, hidden_ref, grad_gate_ref, grad_up_ref
-):
+def units_kernel(inner_ref, gate_ref, up_ref, hidden_ref, slope_ref, activated_ref):
     inner = inner_ref[...]
     gate = jnp.dot(inner, gate_ref[...], preferred_element_type=F32)
     up = jnp.dot(inner, up_ref[...], preferred_element_type=F32)
-    grad_hidden = jnp.dot(grad_ref[...], down_ref[...], preferred_element_type=F32)
     sigmoid = jax.nn.sigmoid(gate)
     activated = gate * sigmoid
     hidden_ref[...] = (activated * up).astype(BF16)
-    grad_gate_ref[...] = (grad_hidden * up * sigmoid * (1.0 + gate * (1.0 - sigmoid))).astype(BF16)
-    grad_up_ref[...] = (grad_hidden * activated).astype(BF16)
-
-
-def hidden_units(inner, grad, weights, down):
-    tokens, width = inner.shape
-    units = down.shape[1]
-    rows, columns = math.gcd(tokens, 512), math.gcd(units, 512)
+    slope_ref[...] = (up * sigmoid * (1.0 + gate * (1.0 - sigmoid))).astype(BF16)
+    activated_ref[...] = activated.astype(BF16)
+
+
+def back_hidden_kernel(grad_ref, down_ref, slope_ref, activated_ref, grad_gate_ref, grad_up_ref):
+    grad_hidden = jnp.dot(grad_ref[...], down_ref[...], preferred_element_type=F32)
+    grad_gate_ref[...] = (grad_hidden * slope_ref[...].astype(F32)).astype(BF16)
+    grad_up_ref[...] = (grad_hidden * activated_ref[...].astype(F32)).astype(BF16)
+
+
+def over_units(kernel, rows_in, weights, firsts, units, tiles_in, made, name):
+    tokens, width = rows_in.shape
+    rows, columns = math.gcd(tokens, 2048 // len(firsts)), math.gcd(units, 512)
     tiles = units // columns
-    tall = pl.BlockSpec((rows, width), lambda j, i: (i, 0))
+    tile = pl.BlockSpec((rows, columns), lambda j, i: (i, j))
     wide = [
-        pl.BlockSpec((width, columns), lambda j, i, first=first: (0, first + j))
-        for first in (0, tiles, 0)
+        pl.BlockSpec((width, columns), lambda j, i, first=first: (0, first * tiles + j))
+        for first in firsts
     ]
-    tile = pl.BlockSpec((rows, columns), lambda j, i: (i, j))
-    made = jax.ShapeDtypeStruct((tokens, units), BF16)
     return pl.pallas_call(
-        units_kernel,
+        kernel,
         grid=(tiles, tokens // rows),
-        in_specs=[tall, tall, *wide],
-        out_specs=[tile, tile, tile],
-        out_shape=[made, made, made],
+        in_specs=[pl.BlockSpec((rows, width), lambda j, i: (i, 0)), *wide]
+        + [tile] * len(tiles_in),
+        out_specs=[tile] * made,
+        out_shape=[jax.ShapeDtypeStruct((tokens, units), BF16)] * made,
         compiler_params=pltpu.CompilerParams(vmem_limit_bytes=56 * 2**20),
         cost_estimate=SMALL,
-        name="hidden_units",
-    )(inner, grad, weights, weights, down)
+        name=name,
+    )(rows_in, *([weights] * len(firsts)), *tiles_in)
+
+
+def hidden_units(inner, weights):
+    units = weights.shape[1] // 2
+    return over_units(units_kernel, inner, weights, (0, 1), units, (), 3, "hidden_units")
+
+
+def back_hidden(grad, down, slope, activated):
+    units = down.shape[1]
+    return over_units(
+        back_hidden_kernel, grad, down, (0,), units, (slope, activated), 2, "back_hidden"
+    )
 
 
 def back_units_kernel(count, *refs):
-    *refs, out_ref = refs
+    *refs, own_ref, other_ref = refs
     contract = (((1,), (1,)), ((), ()))
     total = None
     for units_ref, weight_ref in zip(refs[:count], refs[count:]):
@@ -611,21 +624,23 @@
             units_ref[...], weight_ref[...], contract, preferred_element_type=F32
         )
         total = term if total is None else total + term
-    out_ref[...] = total.astype(BF16)
+    half = own_ref.shape[0]
+    own_ref[...] = total[:half].astype(BF16)
+    other_ref[...] = total[half:].astype(BF16)
 
 
 def back_units(tree, tokens, units, weights, places):
     width, size = weights.shape[0], units[0].shape[1]
-    rows, columns = math.gcd(tokens, 1024), math.gcd(width, 512)
-    first = tree * (tokens // rows)
-    tall = pl.BlockSpec((rows, size), lambda j, i: (first + i, 0))
+    columns = math.gcd(width, 512)
+    tall = pl.BlockSpec((tokens, size), lambda j: (tree, 0))
+    made = jax.ShapeDtypeStruct((tokens // 2, width), BF16)
     return pl.pallas_call(
         functools.partial(back_units_kernel, len(units)),
-        grid=(width // columns, tokens // rows),
+        grid=(width // columns,),
         in_specs=[tall] * len(units)
-        + [pl.BlockSpec((columns, size), lambda j, i, at=at: (j, at)) for at in places],
-        out_specs=pl.BlockSpec((rows, columns), lambda j, i: (i, j)),
-        out_shape=jax.ShapeDtypeStruct((tokens, width), BF16),
+        + [pl.BlockSpec((columns, size), lambda j, at=at: (j, at)) for at in places],
+        out_specs=[pl.BlockSpec((tokens // 2, columns), lambda j: (0, j))] * 2,
+        out_shape=[made, made],
         compiler_params=pltpu.CompilerParams(vmem_limit_bytes=56 * 2**20),
         cost_estimate=SMALL,
         name="back_units",
@@ -947,47 +962,55 @@
         math.gcd(rows, 256),
     )
     query, key_value = after_all((query, key_value), down_hop)
-    cosine_rows, sine_rows = cosine.T[:, None, :], sine.T[:, None, :]
-    kv_ring = Gather(ring, [key_value.reshape(trees, chip_rows, 2 * kv_cols)], True)
-    kv_hops = [kv_ring.hop()]
-    kv_hops.append(kv_ring.hop())
+    kv_rings = [
+        Gather(ring, [key_value[tree * chip_rows : (tree + 1) * chip_rows]], True)
+        for tree in range(trees)
+    ]
     (out_grad,) = after_all((out_grad,), (key_value,))
     other_grad = other_core(out_grad)
-    while kv_ring.step < chips // 2 - 1:
-        kv_hops.append(kv_ring.hop())
-    (layer_in,) = after_all((layer_in,), (key_value,))
-    scale_a = row_scale_of(layer_in.astype(F32))
-    (out_grad,) = after_all((out_grad,), kv_hops[0])
-    grad_low = jnp.concatenate([out_grad, other_grad], axis=1).reshape(trees * chip_rows, width)
-    kv_hops.append(kv_ring.hop(grad_low, scale_a))
+    while kv_rings[0].step < chips // 2:
+        mark, kv_hop = kv_hop if kv_rings[0].step else None, kv_rings[0].hop()
+    kv_hop = kv_rings[1].hop(*mark)
     units_ring = Gather(ring, [units_piece])
-    units_hop = units_ring.hop(*kv_hops[-1])
-    units_hop += down_ring.hop(*kv_hops[-1])
-    (kvs,) = kv_ring.finish()
-
-    def core_sum(part):
-        if part.ndim == 2:
-            part = part.reshape(2, rows, width)
-        return part[0].astype(F32) + other_core(part[1].astype(BF16)).astype(F32)
+    units_hop = units_ring.hop(*kv_rings[0].rightward, *kv_rings[0].leftward) + kv_hop
+    kvs = [kv_rings[0].finish()[0].reshape(chips, 1, chip_rows, 2 * kv_cols)]
+
+    def core_sum(own, other):
+        return own.astype(F32) + other_core(other.astype(BF16)).astype(F32)
 
     def laid(buffer, value, tree):
         return lax.dynamic_update_slice(buffer, value[None], (tree, 0, 0))
 
     mixes, lses, middles, inners, normeds_f, scales_f, lows = [], [], [], [], [], [], []
     for tree in range(trees):
-        mixed, lse = attend(tree, tables[tree], query, masks[tree], kvs, rep, block)
-        (mixed,) = after_all((mixed,), units_hop + ((arrived,) if tree else ()))
-        units_hop = units_ring.hop(mixed)
-        if down_ring.step < chips // 2:
-            units_hop += down_ring.hop(mixed)
+        mixed, lse = attend(tree, tables[tree], query, masks[tree], kvs[tree], rep, block)
+        (mixed,) = after_all((mixed,), units_hop)
+        part_hop = ()
+        if tree == 0:
+            while kv_rings[1].step < chips // 2 - 1:
+                kv_hop = kv_rings[1].hop(mixed)
+            last_hop = kv_rings[1].hop()
+            down_hop = down_ring.hop(*kv_hop)
+            units_hop = units_ring.hop(*last_hop)
+        else:
+            units_ring.hop(mixed)
+            part_hop = down_hop
         mixes.append(mixed)
         lses.append(lse)
-        lows.append(core_sum(dot(mixed, w_o, 0, 1)).astype(BF16))
+        (part,) = after_all((dot(mixed, w_o, 0, 1),), part_hop)
+        lows.append(core_sum(part[:rows], part[rows:]).astype(BF16))
         if tree == 0:
             arrived = other_half(lows[0])
+            units_hop += (arrived,)
             (query,) = after_all((query,), lows)
+            kvs.append(kv_rings[1].finish()[0].reshape(chips, 1, chip_rows, 2 * kv_cols))
     arrived = [after_all((arrived,), lows[1:])[0]] + [other_half(low) for low in lows[1:]]
-    (layer_in,) = after_all((layer_in,), lows)
+    layer_in, out_grad, position = after_all((layer_in, out_grad, position), lows)
+    scale_a = row_scale_of(layer_in.astype(F32))
+    grad_low = jnp.concatenate([out_grad, other_grad], axis=1).reshape(trees * chip_rows, width)
+    cosine_rows, sine_rows = (
+        table(rope_angles(position, HEAD_SIZE)).T[:, None, :] for table in (jnp.cos, jnp.sin)
+    )
     for tree in range(trees):
         rows_in = layer_in[tree].astype(F32)
         middle = rows_in + (lows[tree].astype(F32) + arrived[tree].astype(F32))
@@ -1000,25 +1023,33 @@
         normeds_f.append(normed_f)
     inner_f = jnp.concatenate(inners, axis=0)
 
-    (w_units,) = units_ring.finish()
+    (w_units,) = units_ring.finish(*arrived[1:], grad_low, cosine_rows, sine_rows, scale_a)
+    w_units = w_units.reshape(width, -1)
+    down_hop = ()
+    while down_ring.step < chips // 2 - 1:
+        down_hop += down_ring.hop(*arrived[1:])
+    hidden, gate_slope, activated = after_all(hidden_units(inner_f, w_units), down_hop)
+    down_hop = down_ring.hop(hidden)
+    down_terms, grad_low = after_all((unit_grads(grad_low, hidden), grad_low), down_hop)
     (w_d,) = down_ring.finish()
-    w_units, w_d = w_units.reshape(width, -1), w_d.reshape(width, -1)
-    hidden, grad_gate, grad_up = hidden_units(inner_f, grad_low, w_units, w_d)
+    w_d = w_d.reshape(width, -1)
+    (grad_low,) = after_all((grad_low,), (down_terms,))
+    grad_gate, grad_up = back_hidden(grad_low, w_d, gate_slope, activated)
 
     def pieces(term):
         return term.astype(BF16).reshape(chips, width // chips, -1)
 
     spans = [slice(tree * chip_rows, (tree + 1) * chip_rows) for tree in range(trees)]
-    down_ring = Reduce(ring, [pieces(unit_grads(grad_low, hidden))])
+    down_ring = Reduce(ring, [pieces(down_terms)])
     down_hop = down_ring.hop()
     core_sums = []
     (grad_gate,) = after_all((grad_gate,), (down_ring.terms[0],))
     for tree in range(trees):
         part = back_units(tree, chip_rows, [grad_gate, grad_up], w_units, [0, 1])
-        (part,) = after_all((part,), down_hop)
-        down_hop = down_ring.hop(part)
-        (grad_gate,) = after_all((grad_gate,), (part,))
-        core_sums.append(core_sum(part))
+        part = after_all(part, down_hop)
+        down_hop = down_ring.hop(part[0])
+        (grad_gate,) = after_all((grad_gate,), part)
+        core_sums.append(core_sum(*part))
     lows = [own.astype(BF16) for own in core_sums]
     arrived = [other_half(lows[0])]
     inner_f, hidden = after_all((inner_f, hidden), lows)
@@ -1056,7 +1087,8 @@
             parts.append(jnp.concatenate(kv_parts, axis=1).astype(BF16))
         grad_qkv = jnp.concatenate(parts, axis=1)
         grads_qkv.append(grad_qkv)
-        gain_a_terms.append(core_sum(dot(grad_qkv, w_qkv, 1, 1)))
+        part = dot(grad_qkv, w_qkv, 1, 1)
+        gain_a_terms.append(core_sum(part[:rows], part[rows:]))
         return gain_a_terms[-1].astype(BF16)
 
     grad_queries, grad_kvs = [], []
@@ -1073,7 +1105,7 @@
                 mixes[tree],
                 grad_mixed,
                 lses[tree],
-                kvs,
+                kvs[tree],
                 cosine,
                 sine,
                 rep,
@@ -1092,8 +1124,8 @@
                 out_parts = [
                     back_units(tree, chip_rows, [hidden], w_d, [0]) for tree in range(trees)
                 ]
-                out_parts = after_all(out_parts, arrived[1:])
-                out_lows = [core_sum(part).astype(BF16) for part in out_parts]
+                out_parts[0] = after_all(out_parts[0], arrived[1:])
+                out_lows = [core_sum(*part).astype(BF16) for part in out_parts]
                 (grad_mixed,) = after_all((grad_mixed,), out_lows)
                 out_arrived.append(other_half(out_lows[0]))
                 units_hop += tuple(out_arrived)
@@ -1138,21 +1170,21 @@
         [
             sum(jnp.sum(core_sums[trees + i] * normed_a[i], axis=0) for i in range(trees)),
             sum(jnp.sum(core_sums[i] * normeds_f[i], axis=0) for i in range(trees)),
-        ],
-        axis=1,
-    )
-    gain_terms = jnp.pad(gain_terms, ((0, 0), (0, 126))).astype(BF16)
+        ]
+    )
+    gain_terms = jnp.moveaxis(gain_terms.astype(BF16).reshape(2, chips, width // chips), 1, 0)
+    gain_terms = jnp.pad(gain_terms, ((0, 0), (0, 30), (0, 0)))
     term_qkv = unit_grads(inner_a, jnp.concatenate(grads_qkv, axis=0))
-    term_qkv = jnp.concatenate([term_qkv, gain_terms], axis=1)
-    qkv_sum, out_sum, theirs = ring_sum([pieces(term_qkv), out_terms], 2, lows[1])
+    qkv_sum, out_sum, gain_sums, theirs = ring_sum(
+        [pieces(term_qkv), out_terms, gain_terms], 2, lows[1]
+    )
     arrived.append(theirs)
     out_proj_grad = row_grad(out_sum)
-    qkv_sum, gain_sums = qkv_sum[:, : head_cols + 2 * kv_cols], qkv_sum[:, -128:]
     kv_parts = qkv_sum[:, head_cols:].reshape(-1, groups, 2, HEAD_SIZE)
     key_sum, value_sum = (kv_parts[:, :, i].reshape(-1, kv_cols) for i in range(2))
 
-    keep, give = split_by_core(gain_sums, 0)
-    gain_sums = (keep + other_core(give)).T[:8]
+    keep, give = split_by_core(gain_sums[:8], 1)
+    gain_sums = keep + other_core(give)
     gain_sums = gain_sums + other_half(gain_sums)
     gain_a_grad, gain_f_grad = gain_sums[0], gain_sums[1]
     input_grad = unwritten(scale_a, (trees, rows, width))

time: 1260 us -> 1220 us (0.968)
  waiting for transfers between devices: 308 us -> 279 us
  other arithmetic: 201 us -> 185 us
    ppermute x28 -> x32, waiting for transfers between devices: 269 us -> 220 us  [go_right(): return lax.ppermute(value, 'zy', self.right)]
    ppermute x8, waiting for transfers between devices: 0.48 us -> 15.6 us  [other_half(): return lax.ppermute(value, 'tp', SWAP)]
    ppermute x28 -> x32, starting transfers between devices: 33.1 us -> 47.8 us  [go_right(): return lax.ppermute(value, 'zy', self.right)]
    dynamic_update_slice x35 -> x43, local copies, waits for them, and re-layouts: 57.4 us -> 68.9 us  [put(): return lax.dynamic_update_slice(whole, part[None], at)]
    ppermute x28 -> x32, starting transfers between devices: 37.8 us -> 29.4 us  [go_left(): return lax.ppermute(value, 'zy', self.left)]
    unnamed x279 -> x187, local copies, waits for them, and re-layouts: 33.6 us -> 27.7 us
    ppermute x28 -> x32, waiting for transfers between devices: 37.7 us -> 43.4 us  [go_left(): return lax.ppermute(value, 'zy', self.left)]
    pallas_call x1 -> x2, Pallas kernels: 66.6 us -> 72 us  [over_units(): pl.pallas_call(kernel, grid=(tiles, tokens // rows), in_specs=[pl.BlockSp...]
  transfers between devices with their start and end apart: 94 -> 102, of which waited for: 36 -> 39; matrix products, arithmetic and copies ran while one was open for 25% -> 26% of each run, Pallas kernels for 25% -> 34%
where the time goes in v4:
time: 1220 us; the launch traced here: 1210 us
  Pallas kernels  468 us (38%)
  waiting for transfers between devices  279 us (23%)
  other arithmetic  185 us (15%)
  local copies, waits for them, and re-layouts  141 us (12%)
  starting transfers between devices  92.6 us (8%)
  matrix products  36.6 us (3%)
    ppermute x32, waiting for transfers between devices, go_right(): return lax.ppermute(value, 'zy', self.right)  220 us
    pallas_call x2, Pallas kernels, ring_sum(): pl.pallas_call(functools.partial(ring_sum_kernel, count, arrays, swaps),...  115 us
    pallas_call x3, Pallas kernels, unit_grads(): pl.pallas_call(functools.partial(unit_grads_kernel, tiles), grid=(width /...  88.3 us
    pallas_call x4, Pallas kernels, back_units(): pl.pallas_call(functools.partial(back_units_kernel, len(units)), grid=(wi...  74.2 us
    pallas_call x2, Pallas kernels, over_units(): pl.pallas_call(kernel, grid=(tiles, tokens // rows), in_specs=[pl.BlockSp...  72 us
    pallas_call x4, Pallas kernels, attend_back(): pl.pallas_call(functools.partial(attend_back_kernel, block, rep, rows //...  69.1 us
    dynamic_update_slice x43, local copies, waits for them, and re-layouts, put(): return lax.dynamic_update_slice(whole, part[None], at)  68.9 us
    ppermute x32, starting transfers between devices, go_right(): return lax.ppermute(value, 'zy', self.right)  47.8 us
  transfers between devices with their start and end apart: 102, of which 39 were waited for; matrix products, arithmetic and copies ran while one was open for 26% of the time, Pallas kernels for 34%

profile of v4, /device:TPU:0, one launch (start us, length us, event | category | flops | bytes accessed | tf_op | source)
XLA Modules:
  0.0 1205.6 jit_solution(12546928241026367153)
XLA Ops:
  16.5 14.5 %collective-permute-done.6 = bf16[256,1408]{1,0:T(8,128)(2,1)} collective-permute-done((bf16[256,1408]{1,0:T(8,128)(2,1)S(1)}, bf16[256,1408]{1,0:T(8,128)(2,1)}, u32[]{:S(2)}, u32[]{:S(2)}) %collective-permute-start.6) | collective-permute-done | bytes 720928 | tf_op jit(solution)/shard_map/ppermute | solution.py:106
  93.1 16.3 %project.1 = (bf16[2048,2048]{1,0:T(8,128)(2,1)}, bf16[512,2048]{1,0:T(8,128)(2,1)S(1)}, bf16[2048,256]{1,0:T(8,128)(2,1)S(1)}) custom-call(bf16[2,512,2048]{2,1,0:T(8,128)(2,1)} %own_ref, bf16[2,512,2048]{2,1,0:T(8,128)(2,1)} %collective-permute-done.5.other_ref, f32[1,2048]{1,0:T(1,128)S(1)} %copy.75.gain_ref, bf16[2048,1408]{1,0:T(8,128)(2,1)} %bitcast.421, ...), custom_call_target="tpu_custom_call" | custom-call | flops 1048576 | bytes 1024 | tf_op jit(solution)/shard_map/project/pallas_call | solution.py:539
  170.1 16.3 %tree_attention.2 = (bf16[512,1024]{1,0:T(8,128)(2,1)S(1)}, f32[2,4,1024]{2,1,0:T(4,128)S(1)}) custom-call(s32[4]{0:T(128)S(1)} %get-tuple-element.510.count_ref, s32[4,34]{1,0:T(4,128)S(1)} %broadcast_add_fusion.1.list_ref, s32[4]{0:T(128)S(1)} %iota_add_fusion.4.diag_ref, bf16[512,2048]{1,0:T(8,128)(2,1)S(1)} %get-tuple-element.197.query_ref, ...), custom_call_target="tpu_custom_call" | custom-call | flops 1048576 | bytes 1024 | tf_op jit(solution)/shard_map/tree_attention/pallas_call | solution.py:330
  186.4 25.9 %collective-permute-done.29 = bf16[1024,256]{1,0:T(8,128)(2,1)S(1)} collective-permute-done((bf16[1024,256]{1,0:T(8,128)(2,1)S(1)}, bf16[1024,256]{1,0:T(8,128)(2,1)S(1)}, u32[]{:S(2)}, u32[]{:S(2)}) %collective-permute-start.29) | collective-permute-done | bytes 524320 | tf_op jit(solution)/shard_map/ppermute | solution.py:106
  275.8 16.7 %tree_attention.3 = (bf16[512,1024]{1,0:T(8,128)(2,1)S(1)}, f32[2,4,1024]{2,1,0:T(4,128)S(1)}) custom-call(s32[4]{0:T(128)S(1)} %get-tuple-element.511.count_ref, s32[4,34]{1,0:T(4,128)S(1)} %broadcast_add_fusion.list_ref, s32[4]{0:T(128)S(1)} %iota_add_fusion.4.diag_ref, bf16[512,2048]{1,0:T(8,128)(2,1)S(1)} %get-tuple-element.197.query_ref, ...), custom_call_target="tpu_custom_call" | custom-call | flops 1048576 | bytes 1024 | tf_op jit(solution)/shard_map/tree_attention/pallas_call | solution.py:330
  292.5 16.3 %collective-permute-done.38 = bf16[256,4096]{1,0:T(8,128)(2,1)} collective-permute-done((bf16[256,4096]{1,0:T(8,128)(2,1)}, bf16[256,4096]{1,0:T(8,128)(2,1)}, u32[]{:S(2)}, u32[]{:S(2)}) %collective-permute-start.38) | collective-permute-done | bytes 2097184 | tf_op jit(solution)/shard_map/ppermute | solution.py:106
  313.4 13.8 %collective-permute-done.41 = bf16[256,2048]{1,0:T(8,128)(2,1)S(1)} collective-permute-done((bf16[256,2048]{1,0:T(8,128)(2,1)}, bf16[256,2048]{1,0:T(8,128)(2,1)S(1)}, u32[]{:S(2)}, u32[]{:S(2)}) %collective-permute-start.41) | collective-permute-done | bytes 1048608 | tf_op jit(solution)/shard_map/ppermute | solution.py:106
  353.5 31.2 %collective-permute-done.48 = bf16[256,4096]{1,0:T(8,128)(2,1)} collective-permute-done((bf16[256,4096]{1,0:T(8,128)(2,1)}, bf16[256,4096]{1,0:T(8,128)(2,1)}, u32[]{:S(2)}, u32[]{:S(2)}) %collective-permute-start.48) | collective-permute-done | bytes 2097184 | tf_op jit(solution)/shard_map/ppermute | solution.py:106
  422.7 43.6 %hidden_units.1 = (bf16[2048,2048]{1,0:T(8,128)(2,1)}, bf16[2048,2048]{1,0:T(8,128)(2,1)}, bf16[2048,2048]{1,0:T(8,128)(2,1)}) custom-call(bf16[2048,2048]{1,0:T(8,128)(2,1)} %pad_maximum_fusion.1.inner_ref.rows_ref, bf16[2048,4096]{1,0:T(8,128)(2,1)} %bitcast.59.gate_ref.up_ref.refs_2_.refs_3_, bf16[2048,4096]{1,0:T(8,128)(2,1)} %bitcast.59.gate_ref.up_ref.refs_2_.refs_3_), custom_call_target="tpu_custom_call" | custom-call | flops 1048576 | bytes 1024 | tf_op jit(solution)/shard_map/hidden_units/pallas_call | solution.py:593
  470.7 25.4 %unit_grads.3 = bf16[2048,2048]{1,0:T(8,128)(2,1)} custom-call(bf16[2048,2048]{1,0:T(8,128)(2,1)} %bitcast.406, bf16[2048,2048]{1,0:T(8,128)(2,1)} %get-tuple-element.261.refs_0_), custom_call_target="tpu_custom_call" | custom-call | flops 1048576 | bytes 1024 | tf_op jit(solution)/shard_map/unit_grads/pallas_call | solution.py:676
  502.9 28.4 %back_hidden.1 = (bf16[2048,2048]{1,0:T(8,128)(2,1)}, bf16[2048,2048]{1,0:T(8,128)(2,1)}) custom-call(bf16[2048,2048]{1,0:T(8,128)(2,1)} %bitcast.407, bf16[2048,2048]{1,0:T(8,128)(2,1)} %bitcast.403, bf16[2048,2048]{1,0:T(8,128)(2,1)} %get-tuple-element.229.slope_ref, bf16[2048,2048]{1,0:T(8,128)(2,1)} %get-tuple-element.230.activated_ref), custom_call_target="tpu_custom_call" | custom-call | flops 1048576 | bytes 1024 | tf_op jit(solution)/shard_map/back_hidden/pallas_call | solution.py:593
  531.3 23.7 %back_units.4 = (bf16[512,2048]{1,0:T(8,128)(2,1)}, bf16[512,2048]{1,0:T(8,128)(2,1)}) custom-call(bf16[2048,2048]{1,0:T(8,128)(2,1)} %get-tuple-element.246.refs_0_, bf16[2048,2048]{1,0:T(8,128)(2,1)} %get-tuple-element.233.refs_1_, bf16[2048,4096]{1,0:T(8,128)(2,1)} %bitcast.59.gate_ref.up_ref.refs_2_.refs_3_, ...), custom_call_target="tpu_custom_call" | custom-call | flops 1048576 | bytes 1024 | tf_op jit(solution)/shard_map/back_units/pallas_call | solution.py:637
  560.2 23.7 %back_units.5 = (bf16[512,2048]{1,0:T(8,128)(2,1)}, bf16[512,2048]{1,0:T(8,128)(2,1)}) custom-call(bf16[2048,2048]{1,0:T(8,128)(2,1)} %get-tuple-element.246.refs_0_, bf16[2048,2048]{1,0:T(8,128)(2,1)} %get-tuple-element.233.refs_1_, bf16[2048,4096]{1,0:T(8,128)(2,1)} %bitcast.59.gate_ref.up_ref.refs_2_.refs_3_, ...), custom_call_target="tpu_custom_call" | custom-call | flops 1048576 | bytes 1024 | tf_op jit(solution)/shard_map/back_units/pallas_call | solution.py:637
  601.5 47.8 %unit_grads.4 = bf16[2048,4096]{1,0:T(8,128)(2,1)} custom-call(bf16[2048,2048]{1,0:T(8,128)(2,1)} %pad_maximum_fusion.1.inner_ref.rows_ref, bf16[2048,2048]{1,0:T(8,128)(2,1)} %get-tuple-element.246.refs_0_, bf16[2048,2048]{1,0:T(8,128)(2,1)} %get-tuple-element.233.refs_1_), custom_call_target="tpu_custom_call" | custom-call | flops 1048576 | bytes 1024 | tf_op jit(solution)/shard_map/unit_grads/pallas_call | solution.py:676
  673.9 17.1 %tree_attention_back.4 = (bf16[1024,256]{1,0:T(8,128)(2,1)}, bf16[8,1024,256]{2,1,0:T(8,128)(2,1)}) custom-call(s32[4,32]{1,0:T(4,128)} %get-tuple-element.509.seen_ref, bf16[512,2048]{1,0:T(8,128)(2,1)} %copy-done, bf16[16,1024]{1,0:T(8,128)(2,1)} %copy-done.16, bf16[512,1024]{1,0:T(8,128)(2,1)} %copy-done.9, bf16[512,1024]{1,0:T(8,128)(2,1)} %fusion.43.grad_ref, ...), custom_call_target="tpu_custom_call" | custom-call | flops 1048576 | bytes 1024 | tf_op jit(solution)/shard_map/tree_attention_back/pallas_call | solution.py:469
  691.0 18.1 %collective-permute-done.67 = bf16[128,4096]{1,0:T(8,128)(2,1)} collective-permute-done((bf16[128,4096]{1,0:T(8,128)(2,1)S(1)}, bf16[128,4096]{1,0:T(8,128)(2,1)}, u32[]{:S(2)}, u32[]{:S(2)}) %collective-permute-start.67) | collective-permute-done | bytes 1048608 | tf_op jit(solution)/shard_map/ppermute | solution.py:106
  765.3 17.9 %tree_attention_back.5 = (bf16[1024,256]{1,0:T(8,128)(2,1)}, bf16[8,1024,256]{2,1,0:T(8,128)(2,1)}) custom-call(s32[4,32]{1,0:T(4,128)} %get-tuple-element.509.seen_ref, bf16[512,2048]{1,0:T(8,128)(2,1)} %copy-done, bf16[16,1024]{1,0:T(8,128)(2,1)} %copy-done.16, bf16[512,1024]{1,0:T(8,128)(2,1)} %copy-done.9, ...), custom_call_target="tpu_custom_call", output_to_operand_aliasing={{1}: (10, {})} | custom-call | flops 1048576 | bytes 1024 | tf_op jit(solution)/shard_map/tree_attention_back/pallas_call | solution.py:469
  784.1 15.6 %collective-permute-done.75 = bf16[512,2048]{1,0:T(8,128)(2,1)} collective-permute-done((bf16[512,2048]{1,0:T(8,128)(2,1)}, bf16[512,2048]{1,0:T(8,128)(2,1)}, u32[]{:S(2)}, u32[]{:S(2)}) %collective-permute-start.75) | collective-permute-done | bytes 2097184 | tf_op jit(solution)/shard_map/ppermute | solution.py:200
  867.1 17.1 %tree_attention_back.6 = (bf16[1024,256]{1,0:T(8,128)(2,1)}, bf16[8,1024,256]{2,1,0:T(8,128)(2,1)}) custom-call(s32[4,32]{1,0:T(4,128)} %get-tuple-element.508.seen_ref, bf16[512,2048]{1,0:T(8,128)(2,1)} %copy-done, bf16[16,1024]{1,0:T(8,128)(2,1)} %copy-done.15, bf16[512,1024]{1,0:T(8,128)(2,1)} %copy-done.11, ...), custom_call_target="tpu_custom_call" | custom-call | flops 1048576 | bytes 1024 | tf_op jit(solution)/shard_map/tree_attention_back/pallas_call | solution.py:469
  884.2 23.6 %collective-permute-done.84 = bf16[1024,256]{1,0:T(8,128)(2,1)S(1)} collective-permute-done((bf16[1024,256]{1,0:T(8,128)(2,1)S(1)}, bf16[1024,256]{1,0:T(8,128)(2,1)S(1)}, u32[]{:S(2)}, u32[]{:S(2)}) %collective-permute-start.84) | collective-permute-done | bytes 524320 | tf_op jit(solution)/shard_map/ppermute | solution.py:106
  928.2 17.1 %tree_attention_back.7 = (bf16[1024,256]{1,0:T(8,128)(2,1)}, bf16[8,1024,256]{2,1,0:T(8,128)(2,1)}) custom-call(s32[4,32]{1,0:T(4,128)} %get-tuple-element.508.seen_ref, bf16[512,2048]{1,0:T(8,128)(2,1)} %copy-done, bf16[16,1024]{1,0:T(8,128)(2,1)} %copy-done.15, bf16[512,1024]{1,0:T(8,128)(2,1)} %copy-done.11, ...), custom_call_target="tpu_custom_call", output_to_operand_aliasing={{1}: (10, {})} | custom-call | flops 1048576 | bytes 1024 | tf_op jit(solution)/shard_map/tree_attention_back/pallas_call | solution.py:469
  995.9 62.9 %ring_sum.2 = f32[1024,256]{1,0:T(8,128)S(1)} custom-call(bf16[8,1024,256]{2,1,0:T(8,128)(2,1)S(1)} %copy-done.4), custom_call_target="tpu_custom_call" | custom-call | flops 1048576 | bytes 1024 | tf_op jit(solution)/shard_map/ring_sum/pallas_call | solution.py:797
  1081.6 15.2 %unit_grads.5 = bf16[2048,768]{1,0:T(8,128)(2,1)} custom-call(bf16[2048,2048]{1,0:T(8,128)(2,1)} %get-tuple-element.306.rows_ref, bf16[2048,768]{1,0:T(8,128)(2,1)} %pad_maximum_fusion.3.refs_0_), custom_call_target="tpu_custom_call" | custom-call | flops 1048576 | bytes 1024 | tf_op jit(solution)/shard_map/unit_grads/pallas_call | solution.py:676
  1113.5 52.0 %ring_sum.3 = (f32[256,768]{1,0:T(8,128)S(1)}, f32[256,512]{1,0:T(8,128)S(1)}, f32[32,256]{1,0:T(8,128)S(1)}, bf16[512,2048]{1,0:T(8,128)(2,1)S(1)}) custom-call(bf16[8,256,768]{2,1,0:T(8,128)(2,1)} %bitcast.428, bf16[8,256,512]{2,1,0:T(8,128)(2,1)S(1)} %bitcast.400, bf16[8,32,256]{2,1,0:T(8,128)(2,1)S(1)} %pad.37.refs_2_, ...), custom_call_target="tpu_custom_call" | custom-call | flops 1048576 | bytes 1024 | tf_op jit(solution)/shard_map/ring_sum/pallas_call | solution.py:797
  (658 shorter events, 602.5 us)
Async XLA Ops:
  14.2 79.0 %collective-permute-start.5 = (bf16[2,512,2048]{2,1,0:T(8,128)(2,1)}, bf16[2,512,2048]{2,1,0:T(8,128)(2,1)}, u32[]{:S(2)}, u32[]{:S(2)}) collective-permute-start(bf16[2,512,2048]{2,1,0:T(8,128)(2,1)} %own_ref), channel_id=1, source_target_pairs={{0,2},{2,0},{1,3},{3,1},{4,6},{6,4},{5,7},{7,5},{8,10},{10,8},{9,1... | collective-permute-start | bytes 12582920 | tf_op jit(solution)/shard_map/ppermute | solution.py:196
  161.2 51.5 %collective-permute-start.27 = (bf16[256,4096]{1,0:T(8,128)(2,1)}, bf16[256,4096]{1,0:T(8,128)(2,1)}, u32[]{:S(2)}, u32[]{:S(2)}) collective-permute-start(bf16[256,4096]{1,0:T(8,128)(2,1)} %copy-done.43), channel_id=1, source_target_pairs={{0,8},{8,16},{16,24},{24,28},{28,20},{20,12},{12,4},{4,0},{1,9},{9... | collective-permute-start | bytes 6291464 | tf_op jit(solution)/shard_map/ppermute | solution.py:106
  161.5 51.1 %collective-permute-start.28 = (bf16[256,4096]{1,0:T(8,128)(2,1)}, bf16[256,4096]{1,0:T(8,128)(2,1)S(1)}, u32[]{:S(2)}, u32[]{:S(2)}) collective-permute-start(bf16[256,4096]{1,0:T(8,128)(2,1)} %copy-done.43), channel_id=1, source_target_pairs={{8,0},{16,8},{24,16},{28,24},{20,28},{12,20},{4,12},{0,4},{9,1},{1... | collective-permute-start | bytes 6291464 | tf_op jit(solution)/shard_map/ppermute | solution.py:109
  260.0 48.9 %collective-permute-start.38 = (bf16[256,4096]{1,0:T(8,128)(2,1)}, bf16[256,4096]{1,0:T(8,128)(2,1)}, u32[]{:S(2)}, u32[]{:S(2)}) collective-permute-start(bf16[256,4096]{1,0:T(8,128)(2,1)} %collective-permute-done.27), channel_id=1, source_target_pairs={{0,8},{8,16},{16,24},{24,28},{28,20},{20,12},{12,4},{4,0},{1,9},{9... | collective-permute-start | bytes 6291464 | tf_op jit(solution)/shard_map/ppermute | solution.py:106
  270.2 57.0 %collective-permute-start.41 = (bf16[256,2048]{1,0:T(8,128)(2,1)}, bf16[256,2048]{1,0:T(8,128)(2,1)S(1)}, u32[]{:S(2)}, u32[]{:S(2)}) collective-permute-start(bf16[256,2048]{1,0:T(8,128)(2,1)} %collective-permute-done.15), channel_id=1, source_target_pairs={{0,8},{8,16},{16,24},{24,28},{28,20},{20,12},{12,4},{4,0},{1,9},{9... | collective-permute-start | bytes 3145736 | tf_op jit(solution)/shard_map/ppermute | solution.py:106
  270.9 56.9 %collective-permute-start.42 = (bf16[256,2048]{1,0:T(8,128)(2,1)}, bf16[256,2048]{1,0:T(8,128)(2,1)}, u32[]{:S(2)}, u32[]{:S(2)}) collective-permute-start(bf16[256,2048]{1,0:T(8,128)(2,1)} %collective-permute-done.16), channel_id=1, source_target_pairs={{8,0},{16,8},{24,16},{28,24},{20,28},{12,20},{4,12},{0,4},{9,1},{1... | collective-permute-start | bytes 3145736 | tf_op jit(solution)/shard_map/ppermute | solution.py:109
  337.0 50.8 %collective-permute-start.49 = (bf16[256,4096]{1,0:T(8,128)(2,1)}, bf16[256,4096]{1,0:T(8,128)(2,1)}, u32[]{:S(2)}, u32[]{:S(2)}) collective-permute-start(bf16[256,4096]{1,0:T(8,128)(2,1)} %collective-permute-done.39), channel_id=1, source_target_pairs={{8,0},{16,8},{24,16},{28,24},{20,28},{12,20},{4,12},{0,4},{9,1},{1... | collective-permute-start | bytes 6291464 | tf_op jit(solution)/shard_map/ppermute | solution.py:109
  402.7 63.5 %collective-permute-start.52 = (bf16[256,2048]{1,0:T(8,128)(2,1)S(1)}, bf16[256,2048]{1,0:T(8,128)(2,1)S(1)}, u32[]{:S(2)}, u32[]{:S(2)}) collective-permute-start(bf16[256,2048]{1,0:T(8,128)(2,1)S(1)} %collective-permute-done.41), channel_id=1, source_target_pairs={{0,8},{8,16},{16,24},{24,28},{28,20},{20,12},{12,4},{4,0},{1,9},{9... | collective-permute-start | bytes 3145736 | tf_op jit(solution)/shard_map/ppermute | solution.py:106
  415.3 51.0 %collective-permute-start.53 = (bf16[256,2048]{1,0:T(8,128)(2,1)}, bf16[256,2048]{1,0:T(8,128)(2,1)S(1)}, u32[]{:S(2)}, u32[]{:S(2)}) collective-permute-start(bf16[256,2048]{1,0:T(8,128)(2,1)} %collective-permute-done.42), channel_id=1, source_target_pairs={{8,0},{16,8},{24,16},{28,24},{20,28},{12,20},{4,12},{0,4},{9,1},{1... | collective-permute-start | bytes 3145736 | tf_op jit(solution)/shard_map/ppermute | solution.py:109
  497.9 57.1 %collective-permute-start.56 = (bf16[128,2048]{1,0:T(8,128)(2,1)S(1)}, bf16[128,2048]{1,0:T(8,128)(2,1)S(1)}, u32[]{:S(2)}, u32[]{:S(2)}) collective-permute-start(bf16[128,2048]{1,0:T(8,128)(2,1)S(1)} %get-tuple-element.400), channel_id=1, source_target_pairs={{0,8},{8,16},{16,24},{24,28},{28,20},{20,12},{12,4},{4,0},{1,9},{9... | collective-permute-start | bytes 1572872 | tf_op jit(solution)/shard_map/ppermute | solution.py:106
  498.9 56.1 %collective-permute-start.57 = (bf16[128,2048]{1,0:T(8,128)(2,1)S(1)}, bf16[128,2048]{1,0:T(8,128)(2,1)S(1)}, u32[]{:S(2)}, u32[]{:S(2)}) collective-permute-start(bf16[128,2048]{1,0:T(8,128)(2,1)S(1)} %get-tuple-element.402), channel_id=1, source_target_pairs={{8,0},{16,8},{24,16},{28,24},{20,28},{12,20},{4,12},{0,4},{9,1},{1... | collective-permute-start | bytes 1572872 | tf_op jit(solution)/shard_map/ppermute | solution.py:109
  590.2 59.1 %collective-permute-start.62 = (bf16[512,2048]{1,0:T(8,128)(2,1)}, bf16[512,2048]{1,0:T(8,128)(2,1)}, u32[]{:S(2)}, u32[]{:S(2)}) collective-permute-start(bf16[512,2048]{1,0:T(8,128)(2,1)} %get-tuple-element.410), channel_id=1, source_target_pairs={{0,1},{1,0},{2,3},{3,2},{4,5},{5,4},{6,7},{7,6},{8,9},{9,8},{10,11... | collective-permute-start | bytes 6291464 | tf_op jit(solution)/shard_map/ppermute | solution.py:200
  596.1 53.2 %collective-permute-start.63 = (bf16[256,2048]{1,0:T(8,128)(2,1)}, bf16[256,2048]{1,0:T(8,128)(2,1)S(1)}, u32[]{:S(2)}, u32[]{:S(2)}) collective-permute-start(bf16[256,2048]{1,0:T(8,128)(2,1)} %get-tuple-element.398), channel_id=1, source_target_pairs={{0,8},{8,16},{16,24},{24,28},{28,20},{20,12},{12,4},{4,0},{1,9},{9... | collective-permute-start | bytes 3145736 | tf_op jit(solution)/shard_map/ppermute | solution.py:106
  597.1 52.1 %collective-permute-start.64 = (bf16[256,2048]{1,0:T(8,128)(2,1)}, bf16[256,2048]{1,0:T(8,128)(2,1)}, u32[]{:S(2)}, u32[]{:S(2)}) collective-permute-start(bf16[256,2048]{1,0:T(8,128)(2,1)} %get-tuple-element.397), channel_id=1, source_target_pairs={{8,0},{16,8},{24,16},{28,24},{20,28},{12,20},{4,12},{0,4},{9,1},{1... | collective-permute-start | bytes 3145736 | tf_op jit(solution)/shard_map/ppermute | solution.py:109
  656.4 66.7 %collective-permute-start.66 = (bf16[512,2048]{1,0:T(8,128)(2,1)S(1)}, bf16[512,2048]{1,0:T(8,128)(2,1)S(1)}, u32[]{:S(2)}, u32[]{:S(2)}) collective-permute-start(bf16[512,2048]{1,0:T(8,128)(2,1)S(1)} %get-tuple-element.252), channel_id=1, source_target_pairs={{0,1},{1,0},{2,3},{3,2},{4,5},{5,4},{6,7},{7,6},{8,9},{9,8},{10,11... | collective-permute-start | bytes 6291464 | tf_op jit(solution)/shard_map/ppermute | solution.py:200
  730.3 52.8 %collective-permute-start.74 = (bf16[256,4096]{1,0:T(8,128)(2,1)}, bf16[256,4096]{1,0:T(8,128)(2,1)}, u32[]{:S(2)}, u32[]{:S(2)}) collective-permute-start(bf16[256,4096]{1,0:T(8,128)(2,1)} %pad_maximum_fusion.5), channel_id=1, source_target_pairs={{8,0},{16,8},{24,16},{28,24},{20,28},{12,20},{4,12},{0,4},{9,1},{1... | collective-permute-start | bytes 6291464 | tf_op jit(solution)/shard_map/ppermute | solution.py:109
  732.8 51.2 %collective-permute-start.73 = (bf16[256,4096]{1,0:T(8,128)(2,1)}, bf16[256,4096]{1,0:T(8,128)(2,1)}, u32[]{:S(2)}, u32[]{:S(2)}) collective-permute-start(bf16[256,4096]{1,0:T(8,128)(2,1)} %pad_maximum_fusion.4), channel_id=1, source_target_pairs={{0,8},{8,16},{16,24},{24,28},{28,20},{20,12},{12,4},{4,0},{1,9},{9... | collective-permute-start | bytes 6291464 | tf_op jit(solution)/shard_map/ppermute | solution.py:106
  763.0 68.0 %collective-permute-start.101 = (f32[128,2048]{1,0:T(8,128)}, f32[128,2048]{1,0:T(8,128)}, u32[]{:S(2)}, u32[]{:S(2)}) collective-permute-start(f32[128,2048]{1,0:T(8,128)} %constant_dynamic-slice_fusion), channel_id=1, source_target_pairs={{0,2},{2,0},{1,3},{3,1},{4,6},{6,4},{5,7},{7,5},{8,10},{10,8},{9,1... | collective-permute-start | bytes 3145736 | tf_op jit(solution)/shard_map/ppermute | solution.py:196
  832.5 51.6 %collective-permute-start.77 = (bf16[512,2048]{1,0:T(8,128)(2,1)S(1)}, bf16[512,2048]{1,0:T(8,128)(2,1)}, u32[]{:S(2)}, u32[]{:S(2)}) collective-permute-start(bf16[512,2048]{1,0:T(8,128)(2,1)S(1)} %copy-done.46), channel_id=1, source_target_pairs={{0,1},{1,0},{2,3},{3,2},{4,5},{5,4},{6,7},{7,6},{8,9},{9,8},{10,11... | collective-permute-start | bytes 6291464 | tf_op jit(solution)/shard_map/ppermute | solution.py:200
  849.8 59.2 %collective-permute-start.82 = (bf16[256,4096]{1,0:T(8,128)(2,1)}, bf16[256,4096]{1,0:T(8,128)(2,1)}, u32[]{:S(2)}, u32[]{:S(2)}) collective-permute-start(bf16[256,4096]{1,0:T(8,128)(2,1)} %get-tuple-element.388), channel_id=1, source_target_pairs={{0,8},{8,16},{16,24},{24,28},{28,20},{20,12},{12,4},{4,0},{1,9},{9... | collective-permute-start | bytes 6291464 | tf_op jit(solution)/shard_map/ppermute | solution.py:106
  851.7 57.4 %collective-permute-start.83 = (bf16[256,4096]{1,0:T(8,128)(2,1)}, bf16[256,4096]{1,0:T(8,128)(2,1)}, u32[]{:S(2)}, u32[]{:S(2)}) collective-permute-start(bf16[256,4096]{1,0:T(8,128)(2,1)} %get-tuple-element.387), channel_id=1, source_target_pairs={{8,0},{16,8},{24,16},{28,24},{20,28},{12,20},{4,12},{0,4},{9,1},{1... | collective-permute-start | bytes 6291464 | tf_op jit(solution)/shard_map/ppermute | solution.py:109
  976.2 93.7 %collective-permute-start.100 = (f32[128,2048]{1,0:T(8,128)}, f32[128,2048]{1,0:T(8,128)}, u32[]{:S(2)}, u32[]{:S(2)}) collective-permute-start(f32[128,2048]{1,0:T(8,128)} %constant_dynamic-slice_fusion.1), channel_id=1, source_target_pairs={{0,2},{2,0},{1,3},{3,1},{4,6},{6,4},{5,7},{7,5},{8,10},{10,8},{9,1... | collective-permute-start | bytes 3145736 | tf_op jit(solution)/shard_map/ppermute | solution.py:196
  977.7 98.9 %collective-permute-start.99 = (f32[128,2048]{1,0:T(8,128)}, f32[128,2048]{1,0:T(8,128)}, u32[]{:S(2)}, u32[]{:S(2)}) collective-permute-start(f32[128,2048]{1,0:T(8,128)} %constant_dynamic-slice_fusion.2), channel_id=1, source_target_pairs={{0,2},{2,0},{1,3},{3,1},{4,6},{6,4},{5,7},{7,5},{8,10},{10,8},{9,1... | collective-permute-start | bytes 3145736 | tf_op jit(solution)/shard_map/ppermute | solution.py:196
  980.8 78.0 %collective-permute-start.91 = (bf16[512,2048]{1,0:T(8,128)(2,1)S(1)}, bf16[512,2048]{1,0:T(8,128)(2,1)S(1)}, u32[]{:S(2)}, u32[]{:S(2)}) collective-permute-start(bf16[512,2048]{1,0:T(8,128)(2,1)S(1)} %get-tuple-element.373), channel_id=1, source_target_pairs={{0,1},{1,0},{2,3},{3,2},{4,5},{5,4},{6,7},{7,6},{8,9},{9,8},{10,11... | collective-permute-start | bytes 6291464 | tf_op jit(solution)/shard_map/ppermute | solution.py:200
  (167 other events, 3906.7 us)

commit v5 on v4

--- a/solution.py
+++ b/solution.py
@@ -158,12 +158,11 @@
     def hop(self, *others):
         ring, step, count = self.ring, self.left, len(self.cuts)
         if self.rightward is None:
-            far = after_all(self.each(step), others)
+            far = self.each(step)
             rightward = [part[:cut] for part, cut in zip(far, self.cuts)]
             leftward = [part[cut:] for part, cut in zip(far, self.cuts)]
         else:
-            both = after_all(self.rightward + self.leftward, others)
-            rightward, leftward = both[:count], both[count:]
+            rightward, leftward = list(self.rightward), list(self.leftward)
             mine, other = self.each(step), self.each(-step)
             if step == ring.count // 2 - 1:
                 for i, cut in enumerate(self.cuts):
@@ -174,6 +173,8 @@
             else:
                 rightward = [add_low(one, part) for one, part in zip(mine, rightward)]
                 leftward = [add_low(one, part) for one, part in zip(other, leftward)]
+        both = after_all(rightward + leftward, others)
+        rightward, leftward = both[:count], both[count:]
         self.rightward = [ring.go_right(part) for part in rightward]
         self.leftward = [ring.go_left(part) for part in leftward]
         self.left -= 1
@@ -1050,7 +1051,7 @@
         down_hop = down_ring.hop(part[0])
         (grad_gate,) = after_all((grad_gate,), part)
         core_sums.append(core_sum(*part))
-    lows = [own.astype(BF16) for own in core_sums]
+    lows = unit_lows = [own.astype(BF16) for own in core_sums]
     arrived = [other_half(lows[0])]
     inner_f, hidden = after_all((inner_f, hidden), lows)
     units_terms = unit_grads(inner_f, grad_gate, grad_up)
@@ -1073,7 +1074,7 @@
         return jnp.concatenate([low, other_core(low)], axis=0)
 
     mid_lows, out_lows, out_arrived = [backward_norm(0)], [], []
-    grads_qkv, gain_a_terms = [], []
+    grads_qkv = []
 
     def back_part(tree, kv_sums):
         rows_of = (cosine_rows[spans[tree]], -sine_rows[spans[tree]])
@@ -1088,8 +1089,7 @@
         grad_qkv = jnp.concatenate(parts, axis=1)
         grads_qkv.append(grad_qkv)
         part = dot(grad_qkv, w_qkv, 1, 1)
-        gain_a_terms.append(core_sum(part[:rows], part[rows:]))
-        return gain_a_terms[-1].astype(BF16)
+        return core_sum(part[:rows], part[rows:]).astype(BF16)
 
     grad_queries, grad_kvs = [], []
     for tree in range(trees):
@@ -1154,7 +1154,10 @@
         outputs = laid(outputs, (middles[tree] + summed).astype(BF16), tree)
 
     (layer_in,) = after_all((layer_in,), (grad_queries[-1],))
-    normed_a = layer_in.astype(F32) * scale_a
+
+    def normed_rows(tree, *others):
+        return after_all((layer_in,), others)[0][tree].astype(F32) * scale_a[tree]
+
     down_grad = row_grad(down_sum)
     lows = [back_part(0, kv_ring.finish()[0])]
     arrived = [other_half(lows[0])]
@@ -1165,11 +1168,10 @@
     gate_grad, up_grad = (
         column_grad(part) for part in jnp.split(units_sum, 2, axis=1)
     )
-    core_sums = after_all(core_sums + gain_a_terms, lows)
     gain_terms = jnp.stack(
         [
-            sum(jnp.sum(core_sums[trees + i] * normed_a[i], axis=0) for i in range(trees)),
-            sum(jnp.sum(core_sums[i] * normeds_f[i], axis=0) for i in range(trees)),
+            sum(jnp.sum(low * normed_rows(i, lows[0]), axis=0) for i, low in enumerate(lows)),
+            sum(jnp.sum(low * normeds_f[i], axis=0) for i, low in enumerate(unit_lows)),
         ]
     )
     gain_terms = jnp.moveaxis(gain_terms.astype(BF16).reshape(2, chips, width // chips), 1, 0)
@@ -1190,9 +1192,10 @@
     input_grad = unwritten(scale_a, (trees, rows, width))
     for tree in range(trees):
         grad_inner = lows[tree].astype(F32) + arrived[tree].astype(F32)
+        normed_a = normed_rows(tree, arrived[1])
         input_grad = laid(
             input_grad,
-            grads_middle[tree] + norm_back(grad_inner * gain_a, normed_a[tree], scale_a[tree]),
+            grads_middle[tree] + norm_back(grad_inner * gain_a, normed_a, scale_a[tree]),
             tree,
         )
 

time: 1220 us -> 1200 us (0.984)
    ppermute x32, waiting for transfers between devices: 220 us -> 237 us  [go_right(): return lax.ppermute(value, 'zy', self.right)]
    unnamed x187 -> x205, local copies, waits for them, and re-layouts: 27.7 us -> 20.2 us
  transfers between devices with their start and end apart: 102 -> 102, of which waited for: 39 -> 45; matrix products, arithmetic and copies ran while one was open for 26% -> 25% of each run, Pallas kernels for 34% -> 35%
where the time goes in v5:
time: 1200 us; the launch traced here: 1190 us
  Pallas kernels  469 us (39%)
  waiting for transfers between devices  274 us (23%)
  other arithmetic  177 us (15%)
  local copies, waits for them, and re-layouts  132 us (11%)
  starting transfers between devices  97.1 us (8%)
  matrix products  37.8 us (3%)
    ppermute x32, waiting for transfers between devices, go_right(): return lax.ppermute(value, 'zy', self.right)  237 us
    pallas_call x2, Pallas kernels, ring_sum(): pl.pallas_call(functools.partial(ring_sum_kernel, count, arrays, swaps),...  116 us
    pallas_call x3, Pallas kernels, unit_grads(): pl.pallas_call(functools.partial(unit_grads_kernel, tiles), grid=(width /...  87.9 us
    pallas_call x4, Pallas kernels, back_units(): pl.pallas_call(functools.partial(back_units_kernel, len(units)), grid=(wi...  73.7 us
    pallas_call x2, Pallas kernels, over_units(): pl.pallas_call(kernel, grid=(tiles, tokens // rows), in_specs=[pl.BlockSp...  71.9 us
    pallas_call x4, Pallas kernels, attend_back(): pl.pallas_call(functools.partial(attend_back_kernel, block, rep, rows //...  69.7 us
    dynamic_update_slice x43, local copies, waits for them, and re-layouts, put(): return lax.dynamic_update_slice(whole, part[None], at)  67.1 us
    ppermute x32, starting transfers between devices, go_right(): return lax.ppermute(value, 'zy', self.right)  50.4 us
  transfers between devices with their start and end apart: 102, of which 45 were waited for; matrix products, arithmetic and copies ran while one was open for 25% of the time, Pallas kernels for 35%

profile of v5, /device:TPU:0, one launch (start us, length us, event | category | flops | bytes accessed | tf_op | source)
XLA Modules:
  0.0 1190.4 jit_solution(1641493332127346363)
XLA Ops:
  17.4 14.5 %collective-permute-done.6 = bf16[256,1408]{1,0:T(8,128)(2,1)} collective-permute-done((bf16[256,1408]{1,0:T(8,128)(2,1)S(1)}, bf16[256,1408]{1,0:T(8,128)(2,1)}, u32[]{:S(2)}, u32[]{:S(2)}) %collective-permute-start.6) | collective-permute-done | bytes 720928 | tf_op jit(solution)/shard_map/ppermute | solution.py:106
  93.5 16.3 %project.1 = (bf16[2048,2048]{1,0:T(8,128)(2,1)}, bf16[512,2048]{1,0:T(8,128)(2,1)S(1)}, bf16[2048,256]{1,0:T(8,128)(2,1)S(1)}) custom-call(bf16[2,512,2048]{2,1,0:T(8,128)(2,1)} %own_ref, bf16[2,512,2048]{2,1,0:T(8,128)(2,1)} %collective-permute-done.5.other_ref, f32[1,2048]{1,0:T(1,128)S(1)} %copy.75.gain_ref, bf16[2048,1408]{1,0:T(8,128)(2,1)} %bitcast.421, ...), custom_call_target="tpu_custom_call" | custom-call | flops 1048576 | bytes 1024 | tf_op jit(solution)/shard_map/project/pallas_call | solution.py:540
  170.1 16.3 %tree_attention.2 = (bf16[512,1024]{1,0:T(8,128)(2,1)S(1)}, f32[2,4,1024]{2,1,0:T(4,128)S(1)}) custom-call(s32[4]{0:T(128)S(1)} %get-tuple-element.503.count_ref, s32[4,34]{1,0:T(4,128)S(1)} %broadcast_add_fusion.1.list_ref, s32[4]{0:T(128)S(1)} %iota_add_fusion.4.diag_ref, bf16[512,2048]{1,0:T(8,128)(2,1)S(1)} %get-tuple-element.195.query_ref, ...), custom_call_target="tpu_custom_call" | custom-call | flops 1048576 | bytes 1024 | tf_op jit(solution)/shard_map/tree_attention/pallas_call | solution.py:331
  186.5 26.3 %collective-permute-done.29 = bf16[1024,256]{1,0:T(8,128)(2,1)S(1)} collective-permute-done((bf16[1024,256]{1,0:T(8,128)(2,1)S(1)}, bf16[1024,256]{1,0:T(8,128)(2,1)S(1)}, u32[]{:S(2)}, u32[]{:S(2)}) %collective-permute-start.29) | collective-permute-done | bytes 524320 | tf_op jit(solution)/shard_map/ppermute | solution.py:106
  276.5 16.7 %tree_attention.3 = (bf16[512,1024]{1,0:T(8,128)(2,1)S(1)}, f32[2,4,1024]{2,1,0:T(4,128)S(1)}) custom-call(s32[4]{0:T(128)S(1)} %get-tuple-element.504.count_ref, s32[4,34]{1,0:T(4,128)S(1)} %broadcast_add_fusion.list_ref, s32[4]{0:T(128)S(1)} %iota_add_fusion.4.diag_ref, bf16[512,2048]{1,0:T(8,128)(2,1)S(1)} %get-tuple-element.195.query_ref, ...), custom_call_target="tpu_custom_call" | custom-call | flops 1048576 | bytes 1024 | tf_op jit(solution)/shard_map/tree_attention/pallas_call | solution.py:331
  293.2 16.3 %collective-permute-done.38 = bf16[256,4096]{1,0:T(8,128)(2,1)} collective-permute-done((bf16[256,4096]{1,0:T(8,128)(2,1)}, bf16[256,4096]{1,0:T(8,128)(2,1)}, u32[]{:S(2)}, u32[]{:S(2)}) %collective-permute-start.38) | collective-permute-done | bytes 2097184 | tf_op jit(solution)/shard_map/ppermute | solution.py:106
  314.9 13.4 %collective-permute-done.41 = bf16[256,2048]{1,0:T(8,128)(2,1)S(1)} collective-permute-done((bf16[256,2048]{1,0:T(8,128)(2,1)}, bf16[256,2048]{1,0:T(8,128)(2,1)S(1)}, u32[]{:S(2)}, u32[]{:S(2)}) %collective-permute-start.41) | collective-permute-done | bytes 1048608 | tf_op jit(solution)/shard_map/ppermute | solution.py:106
  356.4 29.9 %collective-permute-done.48 = bf16[256,4096]{1,0:T(8,128)(2,1)} collective-permute-done((bf16[256,4096]{1,0:T(8,128)(2,1)}, bf16[256,4096]{1,0:T(8,128)(2,1)}, u32[]{:S(2)}, u32[]{:S(2)}) %collective-permute-start.48) | collective-permute-done | bytes 2097184 | tf_op jit(solution)/shard_map/ppermute | solution.py:106
  405.3 17.0 %collective-permute-done.50 = bf16[128,4096]{1,0:T(8,128)(2,1)S(1)} collective-permute-done((bf16[128,4096]{1,0:T(8,128)(2,1)S(1)}, bf16[128,4096]{1,0:T(8,128)(2,1)S(1)}, u32[]{:S(2)}, u32[]{:S(2)}) %collective-permute-start.50) | collective-permute-done | bytes 1048608 | tf_op jit(solution)/shard_map/ppermute | solution.py:106
  431.2 43.6 %hidden_units.1 = (bf16[2048,2048]{1,0:T(8,128)(2,1)}, bf16[2048,2048]{1,0:T(8,128)(2,1)}, bf16[2048,2048]{1,0:T(8,128)(2,1)}) custom-call(bf16[2048,2048]{1,0:T(8,128)(2,1)} %pad_maximum_fusion.1.inner_ref.rows_ref, bf16[2048,4096]{1,0:T(8,128)(2,1)} %bitcast.59.gate_ref.up_ref.refs_2_.refs_3_, bf16[2048,4096]{1,0:T(8,128)(2,1)} %bitcast.59.gate_ref.up_ref.refs_2_.refs_3_), custom_call_target="tpu_custom_call" | custom-call | flops 1048576 | bytes 1024 | tf_op jit(solution)/shard_map/hidden_units/pallas_call | solution.py:594
  479.2 25.3 %unit_grads.3 = bf16[2048,2048]{1,0:T(8,128)(2,1)} custom-call(bf16[2048,2048]{1,0:T(8,128)(2,1)} %bitcast.406, bf16[2048,2048]{1,0:T(8,128)(2,1)} %get-tuple-element.259.refs_0_), custom_call_target="tpu_custom_call" | custom-call | flops 1048576 | bytes 1024 | tf_op jit(solution)/shard_map/unit_grads/pallas_call | solution.py:677
  511.4 28.3 %back_hidden.1 = (bf16[2048,2048]{1,0:T(8,128)(2,1)}, bf16[2048,2048]{1,0:T(8,128)(2,1)}) custom-call(bf16[2048,2048]{1,0:T(8,128)(2,1)} %bitcast.407, bf16[2048,2048]{1,0:T(8,128)(2,1)} %bitcast.403, bf16[2048,2048]{1,0:T(8,128)(2,1)} %get-tuple-element.227.slope_ref, bf16[2048,2048]{1,0:T(8,128)(2,1)} %get-tuple-element.228.activated_ref), custom_call_target="tpu_custom_call" | custom-call | flops 1048576 | bytes 1024 | tf_op jit(solution)/shard_map/back_hidden/pallas_call | solution.py:594
  539.7 23.7 %back_units.4 = (bf16[512,2048]{1,0:T(8,128)(2,1)}, bf16[512,2048]{1,0:T(8,128)(2,1)}) custom-call(bf16[2048,2048]{1,0:T(8,128)(2,1)} %get-tuple-element.244.refs_0_, bf16[2048,2048]{1,0:T(8,128)(2,1)} %get-tuple-element.231.refs_1_, bf16[2048,4096]{1,0:T(8,128)(2,1)} %bitcast.59.gate_ref.up_ref.refs_2_.refs_3_, ...), custom_call_target="tpu_custom_call" | custom-call | flops 1048576 | bytes 1024 | tf_op jit(solution)/shard_map/back_units/pallas_call | solution.py:638
  567.8 23.7 %back_units.5 = (bf16[512,2048]{1,0:T(8,128)(2,1)}, bf16[512,2048]{1,0:T(8,128)(2,1)}) custom-call(bf16[2048,2048]{1,0:T(8,128)(2,1)} %get-tuple-element.244.refs_0_, bf16[2048,2048]{1,0:T(8,128)(2,1)} %get-tuple-element.231.refs_1_, bf16[2048,4096]{1,0:T(8,128)(2,1)} %bitcast.59.gate_ref.up_ref.refs_2_.refs_3_, ...), custom_call_target="tpu_custom_call" | custom-call | flops 1048576 | bytes 1024 | tf_op jit(solution)/shard_map/back_units/pallas_call | solution.py:638
  605.6 47.1 %unit_grads.4 = bf16[2048,4096]{1,0:T(8,128)(2,1)} custom-call(bf16[2048,2048]{1,0:T(8,128)(2,1)} %pad_maximum_fusion.1.inner_ref.rows_ref, bf16[2048,2048]{1,0:T(8,128)(2,1)} %get-tuple-element.244.refs_0_, bf16[2048,2048]{1,0:T(8,128)(2,1)} %get-tuple-element.231.refs_1_), custom_call_target="tpu_custom_call" | custom-call | flops 1048576 | bytes 1024 | tf_op jit(solution)/shard_map/unit_grads/pallas_call | solution.py:677
  676.5 17.3 %tree_attention_back.4 = (bf16[1024,256]{1,0:T(8,128)(2,1)}, bf16[8,1024,256]{2,1,0:T(8,128)(2,1)}) custom-call(s32[4,32]{1,0:T(4,128)} %get-tuple-element.502.seen_ref, bf16[512,2048]{1,0:T(8,128)(2,1)} %copy-done, bf16[16,1024]{1,0:T(8,128)(2,1)} %copy-done.16, bf16[512,1024]{1,0:T(8,128)(2,1)} %copy-done.11, bf16[512,1024]{1,0:T(8,128)(2,1)} %fusion.69.grad_ref, ...), custom_call_target="tpu_custom_call" | custom-call | flops 1048576 | bytes 1024 | tf_op jit(solution)/shard_map/tree_attention_back/pallas_call | solution.py:470
  694.4 20.7 %collective-permute-done.69 = bf16[256,2048]{1,0:T(8,128)(2,1)S(1)} collective-permute-done((bf16[256,2048]{1,0:T(8,128)(2,1)}, bf16[256,2048]{1,0:T(8,128)(2,1)S(1)}, u32[]{:S(2)}, u32[]{:S(2)}) %collective-permute-start.69) | collective-permute-done | bytes 1048608 | tf_op jit(solution)/shard_map/ppermute | solution.py:106
  770.6 17.7 %tree_attention_back.5 = (bf16[1024,256]{1,0:T(8,128)(2,1)}, bf16[8,1024,256]{2,1,0:T(8,128)(2,1)}) custom-call(s32[4,32]{1,0:T(4,128)} %get-tuple-element.502.seen_ref, bf16[512,2048]{1,0:T(8,128)(2,1)} %copy-done, bf16[16,1024]{1,0:T(8,128)(2,1)} %copy-done.16, bf16[512,1024]{1,0:T(8,128)(2,1)} %copy-done.11, ...), custom_call_target="tpu_custom_call", output_to_operand_aliasing={{1}: (10, {})} | custom-call | flops 1048576 | bytes 1024 | tf_op jit(solution)/shard_map/tree_attention_back/pallas_call | solution.py:470
  865.3 17.3 %tree_attention_back.6 = (bf16[1024,256]{1,0:T(8,128)(2,1)}, bf16[8,1024,256]{2,1,0:T(8,128)(2,1)}) custom-call(s32[4,32]{1,0:T(4,128)} %get-tuple-element.501.seen_ref, bf16[512,2048]{1,0:T(8,128)(2,1)} %copy-done, bf16[16,1024]{1,0:T(8,128)(2,1)} %copy-done.15, bf16[512,1024]{1,0:T(8,128)(2,1)} %copy-done.9, ...), custom_call_target="tpu_custom_call" | custom-call | flops 1048576 | bytes 1024 | tf_op jit(solution)/shard_map/tree_attention_back/pallas_call | solution.py:470
  882.5 19.8 %collective-permute-done.84 = bf16[1024,256]{1,0:T(8,128)(2,1)} collective-permute-done((bf16[1024,256]{1,0:T(8,128)(2,1)}, bf16[1024,256]{1,0:T(8,128)(2,1)}, u32[]{:S(2)}, u32[]{:S(2)}) %collective-permute-start.84) | collective-permute-done | bytes 524320 | tf_op jit(solution)/shard_map/ppermute | solution.py:106
  949.2 17.5 %tree_attention_back.7 = (bf16[1024,256]{1,0:T(8,128)(2,1)}, bf16[8,1024,256]{2,1,0:T(8,128)(2,1)}) custom-call(s32[4,32]{1,0:T(4,128)} %get-tuple-element.501.seen_ref, bf16[512,2048]{1,0:T(8,128)(2,1)} %copy-done, bf16[16,1024]{1,0:T(8,128)(2,1)} %copy-done.15, bf16[512,1024]{1,0:T(8,128)(2,1)} %copy-done.9, ...), custom_call_target="tpu_custom_call", output_to_operand_aliasing={{1}: (10, {})} | custom-call | flops 1048576 | bytes 1024 | tf_op jit(solution)/shard_map/tree_attention_back/pallas_call | solution.py:470
  992.0 64.9 %ring_sum.2 = f32[1024,256]{1,0:T(8,128)S(1)} custom-call(bf16[8,1024,256]{2,1,0:T(8,128)(2,1)S(1)} %copy-done.4), custom_call_target="tpu_custom_call" | custom-call | flops 1048576 | bytes 1024 | tf_op jit(solution)/shard_map/ring_sum/pallas_call | solution.py:798
  1080.1 15.5 %unit_grads.5 = bf16[2048,768]{1,0:T(8,128)(2,1)} custom-call(bf16[2048,2048]{1,0:T(8,128)(2,1)} %get-tuple-element.304.rows_ref, bf16[2048,768]{1,0:T(8,128)(2,1)} %pad_maximum_fusion.3.refs_0_), custom_call_target="tpu_custom_call" | custom-call | flops 1048576 | bytes 1024 | tf_op jit(solution)/shard_map/unit_grads/pallas_call | solution.py:677
  1101.5 51.5 %ring_sum.3 = (f32[256,768]{1,0:T(8,128)S(1)}, f32[256,512]{1,0:T(8,128)S(1)}, f32[32,256]{1,0:T(8,128)S(1)}, bf16[512,2048]{1,0:T(8,128)(2,1)S(1)}) custom-call(bf16[8,256,768]{2,1,0:T(8,128)(2,1)} %bitcast.428, bf16[8,256,512]{2,1,0:T(8,128)(2,1)S(1)} %bitcast.402, bf16[8,32,256]{2,1,0:T(8,128)(2,1)S(1)} %pad.37.refs_2_, ...), custom_call_target="tpu_custom_call" | custom-call | flops 1048576 | bytes 1024 | tf_op jit(solution)/shard_map/ring_sum/pallas_call | solution.py:798
  (671 shorter events, 587.0 us)
Async XLA Ops:
  15.0 78.5 %collective-permute-start.5 = (bf16[2,512,2048]{2,1,0:T(8,128)(2,1)}, bf16[2,512,2048]{2,1,0:T(8,128)(2,1)}, u32[]{:S(2)}, u32[]{:S(2)}) collective-permute-start(bf16[2,512,2048]{2,1,0:T(8,128)(2,1)} %own_ref), channel_id=1, source_target_pairs={{0,2},{2,0},{1,3},{3,1},{4,6},{6,4},{5,7},{7,5},{8,10},{10,8},{9,1... | collective-permute-start | bytes 12582920 | tf_op jit(solution)/shard_map/ppermute | solution.py:197
  161.2 51.9 %collective-permute-start.27 = (bf16[256,4096]{1,0:T(8,128)(2,1)}, bf16[256,4096]{1,0:T(8,128)(2,1)}, u32[]{:S(2)}, u32[]{:S(2)}) collective-permute-start(bf16[256,4096]{1,0:T(8,128)(2,1)} %copy-done.41), channel_id=1, source_target_pairs={{0,8},{8,16},{16,24},{24,28},{28,20},{20,12},{12,4},{4,0},{1,9},{9... | collective-permute-start | bytes 6291464 | tf_op jit(solution)/shard_map/ppermute | solution.py:106
  161.7 51.4 %collective-permute-start.28 = (bf16[256,4096]{1,0:T(8,128)(2,1)}, bf16[256,4096]{1,0:T(8,128)(2,1)S(1)}, u32[]{:S(2)}, u32[]{:S(2)}) collective-permute-start(bf16[256,4096]{1,0:T(8,128)(2,1)} %copy-done.41), channel_id=1, source_target_pairs={{8,0},{16,8},{24,16},{28,24},{20,28},{12,20},{4,12},{0,4},{9,1},{1... | collective-permute-start | bytes 6291464 | tf_op jit(solution)/shard_map/ppermute | solution.py:109
  163.9 48.8 %collective-permute-start.29 = (bf16[1024,256]{1,0:T(8,128)(2,1)S(1)}, bf16[1024,256]{1,0:T(8,128)(2,1)S(1)}, u32[]{:S(2)}, u32[]{:S(2)}) collective-permute-start(bf16[1024,256]{1,0:T(8,128)(2,1)S(1)} %copy-done.74), channel_id=1, source_target_pairs={{0,8},{8,16},{16,24},{24,28},{28,20},{20,12},{12,4},{4,0},{1,9},{9... | collective-permute-start | bytes 1572872 | tf_op jit(solution)/shard_map/ppermute | solution.py:106
  164.4 48.7 %collective-permute-start.30 = (bf16[1024,256]{1,0:T(8,128)(2,1)S(1)}, bf16[1024,256]{1,0:T(8,128)(2,1)S(1)}, u32[]{:S(2)}, u32[]{:S(2)}) collective-permute-start(bf16[1024,256]{1,0:T(8,128)(2,1)S(1)} %copy-done.74), channel_id=1, source_target_pairs={{8,0},{16,8},{24,16},{28,24},{20,28},{12,20},{4,12},{0,4},{9,1},{1... | collective-permute-start | bytes 1572872 | tf_op jit(solution)/shard_map/ppermute | solution.py:109
  260.7 48.9 %collective-permute-start.38 = (bf16[256,4096]{1,0:T(8,128)(2,1)}, bf16[256,4096]{1,0:T(8,128)(2,1)}, u32[]{:S(2)}, u32[]{:S(2)}) collective-permute-start(bf16[256,4096]{1,0:T(8,128)(2,1)} %collective-permute-done.27), channel_id=1, source_target_pairs={{0,8},{8,16},{16,24},{24,28},{28,20},{20,12},{12,4},{4,0},{1,9},{9... | collective-permute-start | bytes 6291464 | tf_op jit(solution)/shard_map/ppermute | solution.py:106
  270.9 57.5 %collective-permute-start.41 = (bf16[256,2048]{1,0:T(8,128)(2,1)}, bf16[256,2048]{1,0:T(8,128)(2,1)S(1)}, u32[]{:S(2)}, u32[]{:S(2)}) collective-permute-start(bf16[256,2048]{1,0:T(8,128)(2,1)} %collective-permute-done.15), channel_id=1, source_target_pairs={{0,8},{8,16},{16,24},{24,28},{28,20},{20,12},{12,4},{4,0},{1,9},{9... | collective-permute-start | bytes 3145736 | tf_op jit(solution)/shard_map/ppermute | solution.py:106
  272.3 57.0 %collective-permute-start.42 = (bf16[256,2048]{1,0:T(8,128)(2,1)}, bf16[256,2048]{1,0:T(8,128)(2,1)}, u32[]{:S(2)}, u32[]{:S(2)}) collective-permute-start(bf16[256,2048]{1,0:T(8,128)(2,1)} %collective-permute-done.16), channel_id=1, source_target_pairs={{8,0},{16,8},{24,16},{28,24},{20,28},{12,20},{4,12},{0,4},{9,1},{1... | collective-permute-start | bytes 3145736 | tf_op jit(solution)/shard_map/ppermute | solution.py:109
  404.1 70.7 %collective-permute-start.52 = (bf16[256,2048]{1,0:T(8,128)(2,1)S(1)}, bf16[256,2048]{1,0:T(8,128)(2,1)S(1)}, u32[]{:S(2)}, u32[]{:S(2)}) collective-permute-start(bf16[256,2048]{1,0:T(8,128)(2,1)S(1)} %collective-permute-done.41), channel_id=1, source_target_pairs={{0,8},{8,16},{16,24},{24,28},{28,20},{20,12},{12,4},{4,0},{1,9},{9... | collective-permute-start | bytes 3145736 | tf_op jit(solution)/shard_map/ppermute | solution.py:106
  422.3 52.5 %collective-permute-start.53 = (bf16[256,2048]{1,0:T(8,128)(2,1)}, bf16[256,2048]{1,0:T(8,128)(2,1)S(1)}, u32[]{:S(2)}, u32[]{:S(2)}) collective-permute-start(bf16[256,2048]{1,0:T(8,128)(2,1)} %collective-permute-done.42), channel_id=1, source_target_pairs={{8,0},{16,8},{24,16},{28,24},{20,28},{12,20},{4,12},{0,4},{9,1},{1... | collective-permute-start | bytes 3145736 | tf_op jit(solution)/shard_map/ppermute | solution.py:109
  506.4 57.1 %collective-permute-start.56 = (bf16[128,2048]{1,0:T(8,128)(2,1)S(1)}, bf16[128,2048]{1,0:T(8,128)(2,1)S(1)}, u32[]{:S(2)}, u32[]{:S(2)}) collective-permute-start(bf16[128,2048]{1,0:T(8,128)(2,1)S(1)} %get-tuple-element.397), channel_id=1, source_target_pairs={{0,8},{8,16},{16,24},{24,28},{28,20},{20,12},{12,4},{4,0},{1,9},{9... | collective-permute-start | bytes 1572872 | tf_op jit(solution)/shard_map/ppermute | solution.py:106
  507.9 55.5 %collective-permute-start.57 = (bf16[128,2048]{1,0:T(8,128)(2,1)S(1)}, bf16[128,2048]{1,0:T(8,128)(2,1)S(1)}, u32[]{:S(2)}, u32[]{:S(2)}) collective-permute-start(bf16[128,2048]{1,0:T(8,128)(2,1)S(1)} %get-tuple-element.399), channel_id=1, source_target_pairs={{8,0},{16,8},{24,16},{28,24},{20,28},{12,20},{4,12},{0,4},{9,1},{1... | collective-permute-start | bytes 1572872 | tf_op jit(solution)/shard_map/ppermute | solution.py:109
  595.9 56.7 %collective-permute-start.62 = (bf16[512,2048]{1,0:T(8,128)(2,1)S(1)}, bf16[512,2048]{1,0:T(8,128)(2,1)}, u32[]{:S(2)}, u32[]{:S(2)}) collective-permute-start(bf16[512,2048]{1,0:T(8,128)(2,1)S(1)} %add_convert_fusion.5), channel_id=1, source_target_pairs={{0,1},{1,0},{2,3},{3,2},{4,5},{5,4},{6,7},{7,6},{8,9},{9,8},{10,11... | collective-permute-start | bytes 6291464 | tf_op jit(solution)/shard_map/ppermute | solution.py:201
  601.4 51.3 %collective-permute-start.63 = (bf16[256,2048]{1,0:T(8,128)(2,1)}, bf16[256,2048]{1,0:T(8,128)(2,1)S(1)}, u32[]{:S(2)}, u32[]{:S(2)}) collective-permute-start(bf16[256,2048]{1,0:T(8,128)(2,1)} %get-tuple-element.245), channel_id=1, source_target_pairs={{0,8},{8,16},{16,24},{24,28},{28,20},{20,12},{12,4},{4,0},{1,9},{9... | collective-permute-start | bytes 3145736 | tf_op jit(solution)/shard_map/ppermute | solution.py:106
  602.6 50.0 %collective-permute-start.64 = (bf16[256,2048]{1,0:T(8,128)(2,1)}, bf16[256,2048]{1,0:T(8,128)(2,1)}, u32[]{:S(2)}, u32[]{:S(2)}) collective-permute-start(bf16[256,2048]{1,0:T(8,128)(2,1)} %get-tuple-element.246), channel_id=1, source_target_pairs={{8,0},{16,8},{24,16},{28,24},{20,28},{12,20},{4,12},{0,4},{9,1},{1... | collective-permute-start | bytes 3145736 | tf_op jit(solution)/shard_map/ppermute | solution.py:109
  659.3 69.6 %collective-permute-start.66 = (bf16[512,2048]{1,0:T(8,128)(2,1)}, bf16[512,2048]{1,0:T(8,128)(2,1)S(1)}, u32[]{:S(2)}, u32[]{:S(2)}) collective-permute-start(bf16[512,2048]{1,0:T(8,128)(2,1)} %add_convert_fusion.4), channel_id=1, source_target_pairs={{0,1},{1,0},{2,3},{3,2},{4,5},{5,4},{6,7},{7,6},{8,9},{9,8},{10,11... | collective-permute-start | bytes 6291464 | tf_op jit(solution)/shard_map/ppermute | solution.py:201
  839.4 66.1 %collective-permute-start.77 = (bf16[512,2048]{1,0:T(8,128)(2,1)S(1)}, bf16[512,2048]{1,0:T(8,128)(2,1)S(1)}, u32[]{:S(2)}, u32[]{:S(2)}) collective-permute-start(bf16[512,2048]{1,0:T(8,128)(2,1)S(1)} %copy-done.46), channel_id=1, source_target_pairs={{0,1},{1,0},{2,3},{3,2},{4,5},{5,4},{6,7},{7,6},{8,9},{9,8},{10,11... | collective-permute-start | bytes 6291464 | tf_op jit(solution)/shard_map/ppermute | solution.py:201
  844.9 60.7 %collective-permute-start.82 = (bf16[256,4096]{1,0:T(8,128)(2,1)}, bf16[256,4096]{1,0:T(8,128)(2,1)}, u32[]{:S(2)}, u32[]{:S(2)}) collective-permute-start(bf16[256,4096]{1,0:T(8,128)(2,1)} %get-tuple-element.280), channel_id=1, source_target_pairs={{0,8},{8,16},{16,24},{24,28},{28,20},{20,12},{12,4},{4,0},{1,9},{9... | collective-permute-start | bytes 6291464 | tf_op jit(solution)/shard_map/ppermute | solution.py:106
  846.8 58.8 %collective-permute-start.83 = (bf16[256,4096]{1,0:T(8,128)(2,1)S(1)}, bf16[256,4096]{1,0:T(8,128)(2,1)}, u32[]{:S(2)}, u32[]{:S(2)}) collective-permute-start(bf16[256,4096]{1,0:T(8,128)(2,1)S(1)} %get-tuple-element.281), channel_id=1, source_target_pairs={{8,0},{16,8},{24,16},{28,24},{20,28},{12,20},{4,12},{0,4},{9,1},{1... | collective-permute-start | bytes 6291464 | tf_op jit(solution)/shard_map/ppermute | solution.py:109
  914.9 51.7 %collective-permute-start.86 = (bf16[256,4096]{1,0:T(8,128)(2,1)}, bf16[256,4096]{1,0:T(8,128)(2,1)}, u32[]{:S(2)}, u32[]{:S(2)}) collective-permute-start(bf16[256,4096]{1,0:T(8,128)(2,1)} %get-tuple-element.289), channel_id=1, source_target_pairs={{0,8},{8,16},{16,24},{24,28},{28,20},{20,12},{12,4},{4,0},{1,9},{9... | collective-permute-start | bytes 6291464 | tf_op jit(solution)/shard_map/ppermute | solution.py:106
  920.4 50.1 %collective-permute-start.87 = (bf16[256,4096]{1,0:T(8,128)(2,1)}, bf16[256,4096]{1,0:T(8,128)(2,1)}, u32[]{:S(2)}, u32[]{:S(2)}) collective-permute-start(bf16[256,4096]{1,0:T(8,128)(2,1)} %get-tuple-element.290), channel_id=1, source_target_pairs={{8,0},{16,8},{24,16},{28,24},{20,28},{12,20},{4,12},{0,4},{9,1},{1... | collective-permute-start | bytes 6291464 | tf_op jit(solution)/shard_map/ppermute | solution.py:109
  978.0 78.8 %collective-permute-start.91 = (bf16[512,2048]{1,0:T(8,128)(2,1)S(1)}, bf16[512,2048]{1,0:T(8,128)(2,1)S(1)}, u32[]{:S(2)}, u32[]{:S(2)}) collective-permute-start(bf16[512,2048]{1,0:T(8,128)(2,1)S(1)} %fusion.21), channel_id=1, source_target_pairs={{0,1},{1,0},{2,3},{3,2},{4,5},{5,4},{6,7},{7,6},{8,9},{9,8},{10,11... | collective-permute-start | bytes 6291464 | tf_op jit(solution)/shard_map/ppermute | solution.py:201
  980.7 88.4 %collective-permute-start.99 = (f32[128,2048]{1,0:T(8,128)}, f32[128,2048]{1,0:T(8,128)}, u32[]{:S(2)}, u32[]{:S(2)}) collective-permute-start(f32[128,2048]{1,0:T(8,128)} %constant_dynamic-slice_fusion.2), channel_id=1, source_target_pairs={{0,2},{2,0},{1,3},{3,1},{4,6},{6,4},{5,7},{7,5},{8,10},{10,8},{9,1... | collective-permute-start | bytes 3145736 | tf_op jit(solution)/shard_map/ppermute | solution.py:197
  982.7 92.6 %collective-permute-start.100 = (f32[128,2048]{1,0:T(8,128)}, f32[128,2048]{1,0:T(8,128)}, u32[]{:S(2)}, u32[]{:S(2)}) collective-permute-start(f32[128,2048]{1,0:T(8,128)} %constant_dynamic-slice_fusion.1), channel_id=1, source_target_pairs={{0,2},{2,0},{1,3},{3,1},{4,6},{6,4},{5,7},{7,5},{8,10},{10,8},{9,1... | collective-permute-start | bytes 3145736 | tf_op jit(solution)/shard_map/ppermute | solution.py:197
  (176 other events, 5100.8 us)

commit v6 on v5

--- a/solution.py
+++ b/solution.py
@@ -1006,12 +1006,10 @@
             (query,) = after_all((query,), lows)
             kvs.append(kv_rings[1].finish()[0].reshape(chips, 1, chip_rows, 2 * kv_cols))
     arrived = [after_all((arrived,), lows[1:])[0]] + [other_half(low) for low in lows[1:]]
-    layer_in, out_grad, position = after_all((layer_in, out_grad, position), lows)
+    layer_in, out_grad, *turns = after_all((layer_in, out_grad, cosine, sine), lows)
     scale_a = row_scale_of(layer_in.astype(F32))
     grad_low = jnp.concatenate([out_grad, other_grad], axis=1).reshape(trees * chip_rows, width)
-    cosine_rows, sine_rows = (
-        table(rope_angles(position, HEAD_SIZE)).T[:, None, :] for table in (jnp.cos, jnp.sin)
-    )
+    cosine_rows, sine_rows = (table.T[:, None, :] for table in turns)
     for tree in range(trees):
         rows_in = layer_in[tree].astype(F32)
         middle = rows_in + (lows[tree].astype(F32) + arrived[tree].astype(F32))

time: 1200 us -> 1190 us (level)
  transfers between devices with their start and end apart: 102 -> 102, of which waited for: 45 -> 43; matrix products, arithmetic and copies ran while one was open for 25% -> 25% of each run, Pallas kernels for 35% -> 35%
where the time goes in v6:
time: 1190 us; the launch traced here: 1180 us
  Pallas kernels  470 us (39%)
  waiting for transfers between devices  268 us (23%)
  other arithmetic  172 us (14%)
  local copies, waits for them, and re-layouts  143 us (12%)
  starting transfers between devices  86.7 us (7%)
  matrix products  38.3 us (3%)
    ppermute x32, waiting for transfers between devices, go_right(): return lax.ppermute(value, 'zy', self.right)  233 us
    pallas_call x2, Pallas kernels, ring_sum(): pl.pallas_call(functools.partial(ring_sum_kernel, count, arrays, swaps),...  118 us
    pallas_call x3, Pallas kernels, unit_grads(): pl.pallas_call(functools.partial(unit_grads_kernel, tiles), grid=(width /...  87.9 us
    pallas_call x4, Pallas kernels, back_units(): pl.pallas_call(functools.partial(back_units_kernel, len(units)), grid=(wi...  73.7 us
    pallas_call x2, Pallas kernels, over_units(): pl.pallas_call(kernel, grid=(tiles, tokens // rows), in_specs=[pl.BlockSp...  71.9 us
    dynamic_update_slice x43, local copies, waits for them, and re-layouts, put(): return lax.dynamic_update_slice(whole, part[None], at)  70.6 us
    pallas_call x4, Pallas kernels, attend_back(): pl.pallas_call(functools.partial(attend_back_kernel, block, rep, rows //...  69 us
    ppermute x32, starting transfers between devices, go_right(): return lax.ppermute(value, 'zy', self.right)  41.7 us
  transfers between devices with their start and end apart: 102, of which 43 were waited for; matrix products, arithmetic and copies ran while one was open for 25% of the time, Pallas kernels for 35%

profile of v6, /device:TPU:0, one launch (start us, length us, event | category | flops | bytes accessed | tf_op | source)
XLA Modules:
  0.0 1181.7 jit_solution(7068897833054878848)
XLA Ops:
  19.0 14.4 %collective-permute-done.6 = bf16[256,1408]{1,0:T(8,128)(2,1)} collective-permute-done((bf16[256,1408]{1,0:T(8,128)(2,1)S(1)}, bf16[256,1408]{1,0:T(8,128)(2,1)}, u32[]{:S(2)}, u32[]{:S(2)}) %collective-permute-start.6) | collective-permute-done | bytes 720928 | tf_op jit(solution)/shard_map/ppermute | solution.py:106
  101.8 16.3 %project.1 = (bf16[2048,2048]{1,0:T(8,128)(2,1)}, bf16[512,2048]{1,0:T(8,128)(2,1)S(1)}, bf16[2048,256]{1,0:T(8,128)(2,1)S(1)}) custom-call(bf16[2,512,2048]{2,1,0:T(8,128)(2,1)} %own_ref, bf16[2,512,2048]{2,1,0:T(8,128)(2,1)} %collective-permute-done.5.other_ref, f32[1,2048]{1,0:T(1,128)S(1)} %copy.140.gain_ref, bf16[2048,1408]{1,0:T(8,128)(2,1)} %bitcast.423, ...), custom_call_target="tpu_custom_call" | custom-call | flops 1048576 | bytes 1024 | tf_op jit(solution)/shard_map/project/pallas_call | solution.py:540
  178.3 16.3 %tree_attention.2 = (bf16[512,1024]{1,0:T(8,128)(2,1)S(1)}, f32[2,4,1024]{2,1,0:T(4,128)S(1)}) custom-call(s32[4]{0:T(128)S(1)} %get-tuple-element.514.count_ref, s32[4,34]{1,0:T(4,128)S(1)} %broadcast_add_fusion.1.list_ref, s32[4]{0:T(128)S(1)} %iota_add_fusion.4.diag_ref, bf16[512,2048]{1,0:T(8,128)(2,1)S(1)} %get-tuple-element.196.query_ref, ...), custom_call_target="tpu_custom_call" | custom-call | flops 1048576 | bytes 1024 | tf_op jit(solution)/shard_map/tree_attention/pallas_call | solution.py:331
  194.7 26.1 %collective-permute-done.29 = bf16[1024,256]{1,0:T(8,128)(2,1)S(1)} collective-permute-done((bf16[1024,256]{1,0:T(8,128)(2,1)S(1)}, bf16[1024,256]{1,0:T(8,128)(2,1)S(1)}, u32[]{:S(2)}, u32[]{:S(2)}) %collective-permute-start.29) | collective-permute-done | bytes 524320 | tf_op jit(solution)/shard_map/ppermute | solution.py:106
  280.6 16.7 %tree_attention.3 = (bf16[512,1024]{1,0:T(8,128)(2,1)S(1)}, f32[2,4,1024]{2,1,0:T(4,128)S(1)}) custom-call(s32[4]{0:T(128)S(1)} %get-tuple-element.515.count_ref, s32[4,34]{1,0:T(4,128)S(1)} %broadcast_add_fusion.list_ref, s32[4]{0:T(128)S(1)} %iota_add_fusion.4.diag_ref, bf16[512,2048]{1,0:T(8,128)(2,1)S(1)} %get-tuple-element.196.query_ref, ...), custom_call_target="tpu_custom_call" | custom-call | flops 1048576 | bytes 1024 | tf_op jit(solution)/shard_map/tree_attention/pallas_call | solution.py:331
  297.3 16.8 %collective-permute-done.38 = bf16[256,4096]{1,0:T(8,128)(2,1)} collective-permute-done((bf16[256,4096]{1,0:T(8,128)(2,1)}, bf16[256,4096]{1,0:T(8,128)(2,1)}, u32[]{:S(2)}, u32[]{:S(2)}) %collective-permute-start.38) | collective-permute-done | bytes 2097184 | tf_op jit(solution)/shard_map/ppermute | solution.py:106
  359.8 30.1 %collective-permute-done.48 = bf16[256,4096]{1,0:T(8,128)(2,1)} collective-permute-done((bf16[256,4096]{1,0:T(8,128)(2,1)}, bf16[256,4096]{1,0:T(8,128)(2,1)}, u32[]{:S(2)}, u32[]{:S(2)}) %collective-permute-start.48) | collective-permute-done | bytes 2097184 | tf_op jit(solution)/shard_map/ppermute | solution.py:106
  408.9 17.4 %collective-permute-done.50 = bf16[128,4096]{1,0:T(8,128)(2,1)S(1)} collective-permute-done((bf16[128,4096]{1,0:T(8,128)(2,1)S(1)}, bf16[128,4096]{1,0:T(8,128)(2,1)S(1)}, u32[]{:S(2)}, u32[]{:S(2)}) %collective-permute-start.50) | collective-permute-done | bytes 1048608 | tf_op jit(solution)/shard_map/ppermute | solution.py:106
  434.9 43.6 %hidden_units.1 = (bf16[2048,2048]{1,0:T(8,128)(2,1)}, bf16[2048,2048]{1,0:T(8,128)(2,1)}, bf16[2048,2048]{1,0:T(8,128)(2,1)}) custom-call(bf16[2048,2048]{1,0:T(8,128)(2,1)} %pad_maximum_fusion.1.inner_ref.rows_ref, bf16[2048,4096]{1,0:T(8,128)(2,1)} %bitcast.59.gate_ref.up_ref.refs_2_.refs_3_, bf16[2048,4096]{1,0:T(8,128)(2,1)} %bitcast.59.gate_ref.up_ref.refs_2_.refs_3_), custom_call_target="tpu_custom_call" | custom-call | flops 1048576 | bytes 1024 | tf_op jit(solution)/shard_map/hidden_units/pallas_call | solution.py:594
  482.9 25.4 %unit_grads.3 = bf16[2048,2048]{1,0:T(8,128)(2,1)} custom-call(bf16[2048,2048]{1,0:T(8,128)(2,1)} %bitcast.408, bf16[2048,2048]{1,0:T(8,128)(2,1)} %get-tuple-element.260.refs_0_), custom_call_target="tpu_custom_call" | custom-call | flops 1048576 | bytes 1024 | tf_op jit(solution)/shard_map/unit_grads/pallas_call | solution.py:677
  515.0 28.3 %back_hidden.1 = (bf16[2048,2048]{1,0:T(8,128)(2,1)}, bf16[2048,2048]{1,0:T(8,128)(2,1)}) custom-call(bf16[2048,2048]{1,0:T(8,128)(2,1)} %bitcast.409, bf16[2048,2048]{1,0:T(8,128)(2,1)} %bitcast.405, bf16[2048,2048]{1,0:T(8,128)(2,1)} %get-tuple-element.228.slope_ref, bf16[2048,2048]{1,0:T(8,128)(2,1)} %get-tuple-element.229.activated_ref), custom_call_target="tpu_custom_call" | custom-call | flops 1048576 | bytes 1024 | tf_op jit(solution)/shard_map/back_hidden/pallas_call | solution.py:594
  543.3 23.7 %back_units.4 = (bf16[512,2048]{1,0:T(8,128)(2,1)}, bf16[512,2048]{1,0:T(8,128)(2,1)}) custom-call(bf16[2048,2048]{1,0:T(8,128)(2,1)} %get-tuple-element.245.refs_0_, bf16[2048,2048]{1,0:T(8,128)(2,1)} %get-tuple-element.232.refs_1_, bf16[2048,4096]{1,0:T(8,128)(2,1)} %bitcast.59.gate_ref.up_ref.refs_2_.refs_3_, ...), custom_call_target="tpu_custom_call" | custom-call | flops 1048576 | bytes 1024 | tf_op jit(solution)/shard_map/back_units/pallas_call | solution.py:638
  571.3 23.7 %back_units.5 = (bf16[512,2048]{1,0:T(8,128)(2,1)}, bf16[512,2048]{1,0:T(8,128)(2,1)}) custom-call(bf16[2048,2048]{1,0:T(8,128)(2,1)} %get-tuple-element.245.refs_0_, bf16[2048,2048]{1,0:T(8,128)(2,1)} %get-tuple-element.232.refs_1_, bf16[2048,4096]{1,0:T(8,128)(2,1)} %bitcast.59.gate_ref.up_ref.refs_2_.refs_3_, ...), custom_call_target="tpu_custom_call" | custom-call | flops 1048576 | bytes 1024 | tf_op jit(solution)/shard_map/back_units/pallas_call | solution.py:638
  609.1 47.1 %unit_grads.4 = bf16[2048,4096]{1,0:T(8,128)(2,1)} custom-call(bf16[2048,2048]{1,0:T(8,128)(2,1)} %pad_maximum_fusion.1.inner_ref.rows_ref, bf16[2048,2048]{1,0:T(8,128)(2,1)} %get-tuple-element.245.refs_0_, bf16[2048,2048]{1,0:T(8,128)(2,1)} %get-tuple-element.232.refs_1_), custom_call_target="tpu_custom_call" | custom-call | flops 1048576 | bytes 1024 | tf_op jit(solution)/shard_map/unit_grads/pallas_call | solution.py:677
  680.0 17.2 %tree_attention_back.4 = (bf16[1024,256]{1,0:T(8,128)(2,1)}, bf16[8,1024,256]{2,1,0:T(8,128)(2,1)}) custom-call(s32[4,32]{1,0:T(4,128)} %get-tuple-element.513.seen_ref, bf16[512,2048]{1,0:T(8,128)(2,1)} %copy-done, bf16[16,1024]{1,0:T(8,128)(2,1)} %copy-done.16, bf16[512,1024]{1,0:T(8,128)(2,1)} %copy-done.11, bf16[512,1024]{1,0:T(8,128)(2,1)} %fusion.69.grad_ref, ...), custom_call_target="tpu_custom_call" | custom-call | flops 1048576 | bytes 1024 | tf_op jit(solution)/shard_map/tree_attention_back/pallas_call | solution.py:470
  697.6 21.0 %collective-permute-done.69 = bf16[256,2048]{1,0:T(8,128)(2,1)S(1)} collective-permute-done((bf16[256,2048]{1,0:T(8,128)(2,1)}, bf16[256,2048]{1,0:T(8,128)(2,1)S(1)}, u32[]{:S(2)}, u32[]{:S(2)}) %collective-permute-start.69) | collective-permute-done | bytes 1048608 | tf_op jit(solution)/shard_map/ppermute | solution.py:106
  767.9 17.6 %tree_attention_back.5 = (bf16[1024,256]{1,0:T(8,128)(2,1)}, bf16[8,1024,256]{2,1,0:T(8,128)(2,1)}) custom-call(s32[4,32]{1,0:T(4,128)} %get-tuple-element.513.seen_ref, bf16[512,2048]{1,0:T(8,128)(2,1)} %copy-done, bf16[16,1024]{1,0:T(8,128)(2,1)} %copy-done.16, bf16[512,1024]{1,0:T(8,128)(2,1)} %copy-done.11, ...), custom_call_target="tpu_custom_call", output_to_operand_aliasing={{1}: (10, {})} | custom-call | flops 1048576 | bytes 1024 | tf_op jit(solution)/shard_map/tree_attention_back/pallas_call | solution.py:470
  785.4 15.1 %collective-permute-done.73 = bf16[256,4096]{1,0:T(8,128)(2,1)} collective-permute-done((bf16[256,4096]{1,0:T(8,128)(2,1)}, bf16[256,4096]{1,0:T(8,128)(2,1)}, u32[]{:S(2)}, u32[]{:S(2)}) %collective-permute-start.73) | collective-permute-done | bytes 2097184 | tf_op jit(solution)/shard_map/ppermute | solution.py:106
  858.1 17.0 %tree_attention_back.6 = (bf16[1024,256]{1,0:T(8,128)(2,1)}, bf16[8,1024,256]{2,1,0:T(8,128)(2,1)}) custom-call(s32[4,32]{1,0:T(4,128)} %get-tuple-element.512.seen_ref, bf16[512,2048]{1,0:T(8,128)(2,1)} %copy-done, bf16[16,1024]{1,0:T(8,128)(2,1)} %copy-done.15, bf16[512,1024]{1,0:T(8,128)(2,1)} %copy-done.9, ...), custom_call_target="tpu_custom_call" | custom-call | flops 1048576 | bytes 1024 | tf_op jit(solution)/shard_map/tree_attention_back/pallas_call | solution.py:470
  875.1 20.5 %collective-permute-done.84 = bf16[1024,256]{1,0:T(8,128)(2,1)} collective-permute-done((bf16[1024,256]{1,0:T(8,128)(2,1)S(1)}, bf16[1024,256]{1,0:T(8,128)(2,1)}, u32[]{:S(2)}, u32[]{:S(2)}) %collective-permute-start.84) | collective-permute-done | bytes 524320 | tf_op jit(solution)/shard_map/ppermute | solution.py:106
  937.6 17.2 %tree_attention_back.7 = (bf16[1024,256]{1,0:T(8,128)(2,1)}, bf16[8,1024,256]{2,1,0:T(8,128)(2,1)}) custom-call(s32[4,32]{1,0:T(4,128)} %get-tuple-element.512.seen_ref, bf16[512,2048]{1,0:T(8,128)(2,1)} %copy-done, bf16[16,1024]{1,0:T(8,128)(2,1)} %copy-done.15, bf16[512,1024]{1,0:T(8,128)(2,1)} %copy-done.9, ...), custom_call_target="tpu_custom_call", output_to_operand_aliasing={{1}: (10, {})} | custom-call | flops 1048576 | bytes 1024 | tf_op jit(solution)/shard_map/tree_attention_back/pallas_call | solution.py:470
  982.3 66.7 %ring_sum.2 = f32[1024,256]{1,0:T(8,128)S(1)} custom-call(bf16[8,1024,256]{2,1,0:T(8,128)(2,1)S(1)} %copy-done.4), custom_call_target="tpu_custom_call" | custom-call | flops 1048576 | bytes 1024 | tf_op jit(solution)/shard_map/ring_sum/pallas_call | solution.py:798
  1071.3 15.5 %unit_grads.5 = bf16[2048,768]{1,0:T(8,128)(2,1)} custom-call(bf16[2048,2048]{1,0:T(8,128)(2,1)} %get-tuple-element.306.rows_ref, bf16[2048,768]{1,0:T(8,128)(2,1)} %pad_maximum_fusion.3.refs_0_), custom_call_target="tpu_custom_call" | custom-call | flops 1048576 | bytes 1024 | tf_op jit(solution)/shard_map/unit_grads/pallas_call | solution.py:677
  1092.7 51.6 %ring_sum.3 = (f32[256,768]{1,0:T(8,128)S(1)}, f32[256,512]{1,0:T(8,128)S(1)}, f32[32,256]{1,0:T(8,128)S(1)}, bf16[512,2048]{1,0:T(8,128)(2,1)S(1)}) custom-call(bf16[8,256,768]{2,1,0:T(8,128)(2,1)} %bitcast.430, bf16[8,256,512]{2,1,0:T(8,128)(2,1)S(1)} %bitcast.404, bf16[8,32,256]{2,1,0:T(8,128)(2,1)S(1)} %pad.37.refs_2_, ...), custom_call_target="tpu_custom_call" | custom-call | flops 1048576 | bytes 1024 | tf_op jit(solution)/shard_map/ring_sum/pallas_call | solution.py:798
  (731 shorter events, 573.3 us)
Async XLA Ops:
  16.6 85.1 %collective-permute-start.5 = (bf16[2,512,2048]{2,1,0:T(8,128)(2,1)}, bf16[2,512,2048]{2,1,0:T(8,128)(2,1)}, u32[]{:S(2)}, u32[]{:S(2)}) collective-permute-start(bf16[2,512,2048]{2,1,0:T(8,128)(2,1)} %own_ref), channel_id=1, source_target_pairs={{0,2},{2,0},{1,3},{3,1},{4,6},{6,4},{5,7},{7,5},{8,10},{10,8},{9,1... | collective-permute-start | bytes 12582920 | tf_op jit(solution)/shard_map/ppermute | solution.py:197
  169.6 53.2 %collective-permute-start.27 = (bf16[256,4096]{1,0:T(8,128)(2,1)}, bf16[256,4096]{1,0:T(8,128)(2,1)}, u32[]{:S(2)}, u32[]{:S(2)}) collective-permute-start(bf16[256,4096]{1,0:T(8,128)(2,1)} %copy-done.41), channel_id=1, source_target_pairs={{0,8},{8,16},{16,24},{24,28},{28,20},{20,12},{12,4},{4,0},{1,9},{9... | collective-permute-start | bytes 6291464 | tf_op jit(solution)/shard_map/ppermute | solution.py:106
  170.5 52.3 %collective-permute-start.28 = (bf16[256,4096]{1,0:T(8,128)(2,1)}, bf16[256,4096]{1,0:T(8,128)(2,1)S(1)}, u32[]{:S(2)}, u32[]{:S(2)}) collective-permute-start(bf16[256,4096]{1,0:T(8,128)(2,1)} %copy-done.41), channel_id=1, source_target_pairs={{8,0},{16,8},{24,16},{28,24},{20,28},{12,20},{4,12},{0,4},{9,1},{1... | collective-permute-start | bytes 6291464 | tf_op jit(solution)/shard_map/ppermute | solution.py:109
  173.1 49.7 %collective-permute-start.30 = (bf16[1024,256]{1,0:T(8,128)(2,1)S(1)}, bf16[1024,256]{1,0:T(8,128)(2,1)S(1)}, u32[]{:S(2)}, u32[]{:S(2)}) collective-permute-start(bf16[1024,256]{1,0:T(8,128)(2,1)S(1)} %copy-done.77), channel_id=1, source_target_pairs={{8,0},{16,8},{24,16},{28,24},{20,28},{12,20},{4,12},{0,4},{9,1},{1... | collective-permute-start | bytes 1572872 | tf_op jit(solution)/shard_map/ppermute | solution.py:109
  265.2 48.9 %collective-permute-start.38 = (bf16[256,4096]{1,0:T(8,128)(2,1)}, bf16[256,4096]{1,0:T(8,128)(2,1)}, u32[]{:S(2)}, u32[]{:S(2)}) collective-permute-start(bf16[256,4096]{1,0:T(8,128)(2,1)} %collective-permute-done.27), channel_id=1, source_target_pairs={{0,8},{8,16},{16,24},{24,28},{28,20},{20,12},{12,4},{4,0},{1,9},{9... | collective-permute-start | bytes 6291464 | tf_op jit(solution)/shard_map/ppermute | solution.py:106
  265.8 48.9 %collective-permute-start.39 = (bf16[256,4096]{1,0:T(8,128)(2,1)S(1)}, bf16[256,4096]{1,0:T(8,128)(2,1)}, u32[]{:S(2)}, u32[]{:S(2)}) collective-permute-start(bf16[256,4096]{1,0:T(8,128)(2,1)S(1)} %collective-permute-done.28), channel_id=1, source_target_pairs={{8,0},{16,8},{24,16},{28,24},{20,28},{12,20},{4,12},{0,4},{9,1},{1... | collective-permute-start | bytes 6291464 | tf_op jit(solution)/shard_map/ppermute | solution.py:109
  275.4 57.1 %collective-permute-start.41 = (bf16[256,2048]{1,0:T(8,128)(2,1)}, bf16[256,2048]{1,0:T(8,128)(2,1)S(1)}, u32[]{:S(2)}, u32[]{:S(2)}) collective-permute-start(bf16[256,2048]{1,0:T(8,128)(2,1)} %collective-permute-done.15), channel_id=1, source_target_pairs={{0,8},{8,16},{16,24},{24,28},{28,20},{20,12},{12,4},{4,0},{1,9},{9... | collective-permute-start | bytes 3145736 | tf_op jit(solution)/shard_map/ppermute | solution.py:106
  276.0 56.9 %collective-permute-start.42 = (bf16[256,2048]{1,0:T(8,128)(2,1)}, bf16[256,2048]{1,0:T(8,128)(2,1)}, u32[]{:S(2)}, u32[]{:S(2)}) collective-permute-start(bf16[256,2048]{1,0:T(8,128)(2,1)} %collective-permute-done.16), channel_id=1, source_target_pairs={{8,0},{16,8},{24,16},{28,24},{20,28},{12,20},{4,12},{0,4},{9,1},{1... | collective-permute-start | bytes 3145736 | tf_op jit(solution)/shard_map/ppermute | solution.py:109
  408.1 70.4 %collective-permute-start.52 = (bf16[256,2048]{1,0:T(8,128)(2,1)S(1)}, bf16[256,2048]{1,0:T(8,128)(2,1)S(1)}, u32[]{:S(2)}, u32[]{:S(2)}) collective-permute-start(bf16[256,2048]{1,0:T(8,128)(2,1)S(1)} %collective-permute-done.41), channel_id=1, source_target_pairs={{0,8},{8,16},{16,24},{24,28},{28,20},{20,12},{12,4},{4,0},{1,9},{9... | collective-permute-start | bytes 3145736 | tf_op jit(solution)/shard_map/ppermute | solution.py:106
  426.3 52.2 %collective-permute-start.53 = (bf16[256,2048]{1,0:T(8,128)(2,1)}, bf16[256,2048]{1,0:T(8,128)(2,1)S(1)}, u32[]{:S(2)}, u32[]{:S(2)}) collective-permute-start(bf16[256,2048]{1,0:T(8,128)(2,1)} %collective-permute-done.42), channel_id=1, source_target_pairs={{8,0},{16,8},{24,16},{28,24},{20,28},{12,20},{4,12},{0,4},{9,1},{1... | collective-permute-start | bytes 3145736 | tf_op jit(solution)/shard_map/ppermute | solution.py:109
  510.1 56.9 %collective-permute-start.56 = (bf16[128,2048]{1,0:T(8,128)(2,1)S(1)}, bf16[128,2048]{1,0:T(8,128)(2,1)S(1)}, u32[]{:S(2)}, u32[]{:S(2)}) collective-permute-start(bf16[128,2048]{1,0:T(8,128)(2,1)S(1)} %get-tuple-element.410), channel_id=1, source_target_pairs={{0,8},{8,16},{16,24},{24,28},{28,20},{20,12},{12,4},{4,0},{1,9},{9... | collective-permute-start | bytes 1572872 | tf_op jit(solution)/shard_map/ppermute | solution.py:106
  510.6 56.3 %collective-permute-start.57 = (bf16[128,2048]{1,0:T(8,128)(2,1)S(1)}, bf16[128,2048]{1,0:T(8,128)(2,1)S(1)}, u32[]{:S(2)}, u32[]{:S(2)}) collective-permute-start(bf16[128,2048]{1,0:T(8,128)(2,1)S(1)} %get-tuple-element.412), channel_id=1, source_target_pairs={{8,0},{16,8},{24,16},{28,24},{20,28},{12,20},{4,12},{0,4},{9,1},{1... | collective-permute-start | bytes 1572872 | tf_op jit(solution)/shard_map/ppermute | solution.py:109
  599.3 56.9 %collective-permute-start.62 = (bf16[512,2048]{1,0:T(8,128)(2,1)S(1)}, bf16[512,2048]{1,0:T(8,128)(2,1)}, u32[]{:S(2)}, u32[]{:S(2)}) collective-permute-start(bf16[512,2048]{1,0:T(8,128)(2,1)S(1)} %add_convert_fusion.5), channel_id=1, source_target_pairs={{0,1},{1,0},{2,3},{3,2},{4,5},{5,4},{6,7},{7,6},{8,9},{9,8},{10,11... | collective-permute-start | bytes 6291464 | tf_op jit(solution)/shard_map/ppermute | solution.py:201
  604.9 51.3 %collective-permute-start.63 = (bf16[256,2048]{1,0:T(8,128)(2,1)}, bf16[256,2048]{1,0:T(8,128)(2,1)S(1)}, u32[]{:S(2)}, u32[]{:S(2)}) collective-permute-start(bf16[256,2048]{1,0:T(8,128)(2,1)} %get-tuple-element.246), channel_id=1, source_target_pairs={{0,8},{8,16},{16,24},{24,28},{28,20},{20,12},{12,4},{4,0},{1,9},{9... | collective-permute-start | bytes 3145736 | tf_op jit(solution)/shard_map/ppermute | solution.py:106
  606.0 50.1 %collective-permute-start.64 = (bf16[256,2048]{1,0:T(8,128)(2,1)}, bf16[256,2048]{1,0:T(8,128)(2,1)}, u32[]{:S(2)}, u32[]{:S(2)}) collective-permute-start(bf16[256,2048]{1,0:T(8,128)(2,1)} %get-tuple-element.247), channel_id=1, source_target_pairs={{8,0},{16,8},{24,16},{28,24},{20,28},{12,20},{4,12},{0,4},{9,1},{1... | collective-permute-start | bytes 3145736 | tf_op jit(solution)/shard_map/ppermute | solution.py:109
  662.7 69.4 %collective-permute-start.66 = (bf16[512,2048]{1,0:T(8,128)(2,1)}, bf16[512,2048]{1,0:T(8,128)(2,1)S(1)}, u32[]{:S(2)}, u32[]{:S(2)}) collective-permute-start(bf16[512,2048]{1,0:T(8,128)(2,1)} %add_convert_fusion.4), channel_id=1, source_target_pairs={{0,1},{1,0},{2,3},{3,2},{4,5},{5,4},{6,7},{7,6},{8,9},{9,8},{10,11... | collective-permute-start | bytes 6291464 | tf_op jit(solution)/shard_map/ppermute | solution.py:201
  831.8 66.8 %collective-permute-start.77 = (bf16[512,2048]{1,0:T(8,128)(2,1)S(1)}, bf16[512,2048]{1,0:T(8,128)(2,1)S(1)}, u32[]{:S(2)}, u32[]{:S(2)}) collective-permute-start(bf16[512,2048]{1,0:T(8,128)(2,1)S(1)} %copy-done.50), channel_id=1, source_target_pairs={{0,1},{1,0},{2,3},{3,2},{4,5},{5,4},{6,7},{7,6},{8,9},{9,8},{10,11... | collective-permute-start | bytes 6291464 | tf_op jit(solution)/shard_map/ppermute | solution.py:201
  838.3 60.2 %collective-permute-start.82 = (bf16[256,4096]{1,0:T(8,128)(2,1)}, bf16[256,4096]{1,0:T(8,128)(2,1)}, u32[]{:S(2)}, u32[]{:S(2)}) collective-permute-start(bf16[256,4096]{1,0:T(8,128)(2,1)} %get-tuple-element.281), channel_id=1, source_target_pairs={{0,8},{8,16},{16,24},{24,28},{28,20},{20,12},{12,4},{4,0},{1,9},{9... | collective-permute-start | bytes 6291464 | tf_op jit(solution)/shard_map/ppermute | solution.py:106
  840.1 58.5 %collective-permute-start.83 = (bf16[256,4096]{1,0:T(8,128)(2,1)S(1)}, bf16[256,4096]{1,0:T(8,128)(2,1)}, u32[]{:S(2)}, u32[]{:S(2)}) collective-permute-start(bf16[256,4096]{1,0:T(8,128)(2,1)S(1)} %get-tuple-element.282), channel_id=1, source_target_pairs={{8,0},{16,8},{24,16},{28,24},{20,28},{12,20},{4,12},{0,4},{9,1},{1... | collective-permute-start | bytes 6291464 | tf_op jit(solution)/shard_map/ppermute | solution.py:109
  907.8 49.0 %collective-permute-start.86 = (bf16[256,4096]{1,0:T(8,128)(2,1)}, bf16[256,4096]{1,0:T(8,128)(2,1)}, u32[]{:S(2)}, u32[]{:S(2)}) collective-permute-start(bf16[256,4096]{1,0:T(8,128)(2,1)} %get-tuple-element.290), channel_id=1, source_target_pairs={{0,8},{8,16},{16,24},{24,28},{28,20},{20,12},{12,4},{4,0},{1,9},{9... | collective-permute-start | bytes 6291464 | tf_op jit(solution)/shard_map/ppermute | solution.py:106
  910.5 50.5 %collective-permute-start.87 = (bf16[256,4096]{1,0:T(8,128)(2,1)}, bf16[256,4096]{1,0:T(8,128)(2,1)}, u32[]{:S(2)}, u32[]{:S(2)}) collective-permute-start(bf16[256,4096]{1,0:T(8,128)(2,1)} %get-tuple-element.291), channel_id=1, source_target_pairs={{8,0},{16,8},{24,16},{28,24},{20,28},{12,20},{4,12},{0,4},{9,1},{1... | collective-permute-start | bytes 6291464 | tf_op jit(solution)/shard_map/ppermute | solution.py:109
  968.6 80.4 %collective-permute-start.91 = (bf16[512,2048]{1,0:T(8,128)(2,1)S(1)}, bf16[512,2048]{1,0:T(8,128)(2,1)S(1)}, u32[]{:S(2)}, u32[]{:S(2)}) collective-permute-start(bf16[512,2048]{1,0:T(8,128)(2,1)S(1)} %fusion.21), channel_id=1, source_target_pairs={{0,1},{1,0},{2,3},{3,2},{4,5},{5,4},{6,7},{7,6},{8,9},{9,8},{10,11... | collective-permute-start | bytes 6291464 | tf_op jit(solution)/shard_map/ppermute | solution.py:201
  970.9 90.6 %collective-permute-start.99 = (f32[128,2048]{1,0:T(8,128)}, f32[128,2048]{1,0:T(8,128)}, u32[]{:S(2)}, u32[]{:S(2)}) collective-permute-start(f32[128,2048]{1,0:T(8,128)} %constant_dynamic-slice_fusion.2), channel_id=1, source_target_pairs={{0,2},{2,0},{1,3},{3,1},{4,6},{6,4},{5,7},{7,5},{8,10},{10,8},{9,1... | collective-permute-start | bytes 3145736 | tf_op jit(solution)/shard_map/ppermute | solution.py:197
  973.0 94.7 %collective-permute-start.100 = (f32[128,2048]{1,0:T(8,128)}, f32[128,2048]{1,0:T(8,128)S(1)}, u32[]{:S(2)}, u32[]{:S(2)}) collective-permute-start(f32[128,2048]{1,0:T(8,128)} %constant_dynamic-slice_fusion.1), channel_id=1, source_target_pairs={{0,2},{2,0},{1,3},{3,1},{4,6},{6,4},{5,7},{7,5},{8,10},{10,8},{9,1... | collective-permute-start | bytes 3145736 | tf_op jit(solution)/shard_map/ppermute | solution.py:197
  (206 other events, 5524.2 us)
